TPU v7x, 32 devices: a whole 2x2x4 slice. The times are simulated.
32 devices in a mesh: dp: 8 (over z, y), ctx: 4 (over x, core).
Axes of the slice: x: 2, y: 2, z: 4, core: 2. Of those that a mesh axis runs over, the one named last changes fastest.
Arguments:
- tokens: bfloat16 [8, 1024, 2048], P('dp', 'ctx'), may hold values from -6 to 6
- lengths: int32 [8], P('dp'), may hold values from 256 to 1024, as said below
- ln_gain: bfloat16 [2048], P(('dp', 'ctx')), may hold values from 0.25 to 1.75
- ln_bias: bfloat16 [2048], P(('dp', 'ctx')), may hold values from -4 to 4
- w_qkv: bfloat16 [2048, 6144], P(('dp', 'ctx')), may hold values from -0.125 to 0.125
- b_qkv: bfloat16 [6144], P(('dp', 'ctx')), may hold values from -4 to 4
- w_out: bfloat16 [2048, 2048], P(('dp', 'ctx')), may hold values from -2 to 2
- b_out: bfloat16 [2048], P(('dp', 'ctx')), may hold values from -4 to 4
- w_fc1: bfloat16 [2048, 8192], P(('dp', 'ctx')), may hold values from -0.125 to 0.125
- b_fc1: bfloat16 [8192], P(('dp', 'ctx')), may hold values from -6 to 6
- w_fc2: bfloat16 [8192, 2048], P(('dp', 'ctx')), may hold values from -0.0625 to 0.0625
- b_fc2: bfloat16 [2048], P(('dp', 'ctx')), may hold values from -4 to 4
- cotangent: bfloat16 [8, 1024, 2048], P('dp', 'ctx'), may hold values from -6 to 6
Outputs:
- output: bfloat16 [8, 1024, 2048], P('dp', 'ctx')
- grad_input: bfloat16 [8, 1024, 2048], P('dp', 'ctx')
- grad_ln_gain: float32 [2048], P(('dp', 'ctx'))
- grad_ln_bias: float32 [2048], P(('dp', 'ctx'))
- grad_w_qkv: float32 [2048, 6144], P(('dp', 'ctx'))
- grad_b_qkv: float32 [6144], P(('dp', 'ctx'))
- grad_w_out: float32 [2048, 2048], P(('dp', 'ctx'))
- grad_b_out: float32 [2048], P(('dp', 'ctx'))
- grad_w_fc1: float32 [2048, 8192], P(('dp', 'ctx'))
- grad_b_fc1: float32 [8192], P(('dp', 'ctx'))
- grad_w_fc2: float32 [8192, 2048], P(('dp', 'ctx'))
- grad_b_fc2: float32 [2048], P(('dp', 'ctx'))
Inputs may be any that keep to these rules, and one draw needn't show every extreme that they name: Each sequence's valid tokens are its first lengths; some sequence is 1024 long in every draw.
All inputs are finite; a program needn't handle non-finite values.
Results may differ from a plain program's by a relative error of at most 0.011.
Values may be sent and summed in bfloat16 or wider, within the bound.
A program may use at most 768 MiB of HBM per device.

v0:
```python
import math

import jax
import jax.numpy as jnp
from jax import lax
from jax.sharding import PartitionSpec as P

HEAD_DIM = 64
ROT = 32


eps_norm = 1e-05
gelu_coef = 0.7978845608028654


def gelu_tanh(values):
    return (
        0.5 * values * (1.0 + jnp.tanh(gelu_coef * (values + 0.044715 * values * values * values)))
    )


def rotary_angles(positions, rot_dims):
    half_dims = rot_dims // 2
    freq_index = jnp.arange(half_dims, dtype=jnp.float32)
    inv_freq = jnp.exp(-math.log(10000.0) * 2.0 * freq_index / rot_dims)
    return positions.astype(jnp.float32)[:, None] * inv_freq[None, :]


def rotary(vectors, angles):
    half_dims = angles.shape[-1]
    cosines = jnp.cos(angles)[:, None, :]
    sine_vals = jnp.sin(angles)[:, None, :]
    leading = vectors[..., :half_dims]
    trailing = vectors[..., half_dims : 2 * half_dims]
    return jnp.concatenate(
        [
            leading * cosines - trailing * sine_vals,
            trailing * cosines + leading * sine_vals,
            vectors[..., 2 * half_dims :],
        ],
        axis=-1,
    )


def rotary_back(gradients, angles):
    half_dims = angles.shape[-1]
    cosines = jnp.cos(angles)[:, None, :]
    sine_vals = jnp.sin(angles)[:, None, :]
    leading = gradients[..., :half_dims]
    trailing = gradients[..., half_dims : 2 * half_dims]
    return jnp.concatenate(
        [
            leading * cosines + trailing * sine_vals,
            trailing * cosines - leading * sine_vals,
            gradients[..., 2 * half_dims :],
        ],
        axis=-1,
    )


def masked_scores(queries, key_rows, places, length):
    scores = jnp.einsum("qhd,khd->hqk", queries, key_rows, preferred_element_type=jnp.float32)
    key_places = jnp.arange(key_rows.shape[0], dtype=jnp.int32)
    allowed = (key_places[None, :] <= places[:, None]) & (key_places[None, :] < length)
    return jnp.where(allowed[None], scores, -1e30)


def on_device(
    tokens,
    lengths,
    ln_gain,
    ln_bias,
    w_qkv,
    b_qkv,
    w_out,
    b_out,
    w_fc1,
    b_fc1,
    w_fc2,
    b_fc2,
    cotangent,
):
    seq_count, local_len, model_width = tokens.shape
    shard_rows = w_qkv.shape[0]
    hidden_ratio = w_fc1.shape[1] // model_width
    head_count = model_width // HEAD_DIM
    token_count = seq_count * local_len
    places = lax.axis_index("ctx") * local_len + jnp.arange(local_len, dtype=jnp.int32)
    angles = rotary_angles(places, ROT)
    live_mask = places[None, :] < lengths[:, None]
    inputs = tokens.astype(jnp.float32).reshape(token_count, model_width)
    average = jnp.mean(inputs, axis=-1, keepdims=True)
    centered = inputs - average
    variance = jnp.mean(centered * centered, axis=-1, keepdims=True)
    inv_std = lax.rsqrt(variance + eps_norm)
    normed = centered * inv_std
    qkv_bias_rows = b_qkv.reshape(shard_rows, 3)
    fc1_bias_rows = b_fc1.reshape(shard_rows, hidden_ratio)
    fc2_rows = w_fc2.reshape(shard_rows, hidden_ratio * model_width)
    inner_full = (
        lax.all_gather(w_qkv, ("dp", "ctx"), axis=0, tiled=True),
        lax.all_gather(w_fc1, ("dp", "ctx"), axis=0, tiled=True),
        lax.all_gather(ln_gain, ("dp", "ctx"), axis=0, tiled=True),
        lax.all_gather(ln_bias, ("dp", "ctx"), axis=0, tiled=True),
        lax.all_gather(qkv_bias_rows, ("dp", "ctx"), axis=0, tiled=True),
        lax.all_gather(fc1_bias_rows, ("dp", "ctx"), axis=0, tiled=True),
    )
    gain_full = inner_full[2].astype(jnp.float32)
    shift_full = inner_full[3].astype(jnp.float32)
    hidden = (normed * gain_full + shift_full).astype(jnp.bfloat16)
    qkv_acc = jnp.dot(hidden, inner_full[0], preferred_element_type=jnp.float32)
    up_acc = jnp.dot(hidden, inner_full[1], preferred_element_type=jnp.float32)
    qkv_bias = inner_full[4].reshape(-1).astype(jnp.float32)
    fc1_bias = inner_full[5].reshape(-1).astype(jnp.float32)
    qkv_proj = (qkv_acc + qkv_bias).reshape(seq_count, local_len, 3, head_count, HEAD_DIM)
    queries = (rotary(qkv_proj[:, :, 0], angles) * 0.125).astype(jnp.bfloat16)
    key_local = (
        rotary(qkv_proj[:, :, 1], angles)
        .astype(jnp.bfloat16)
        .reshape(seq_count, local_len, model_width)
    )
    value_local = qkv_proj[:, :, 2].astype(jnp.bfloat16).reshape(seq_count, local_len, model_width)
    key_full, value_full = (
        lax.all_gather(key_local, "ctx", axis=1, tiled=True),
        lax.all_gather(value_local, "ctx", axis=1, tiled=True),
    )
    total_len = key_full.shape[1]

    def attend_forward(packed):
        query_seq, key_seq, value_seq, length = packed
        key_heads = key_seq.reshape(total_len, head_count, HEAD_DIM)
        value_heads = value_seq.reshape(total_len, head_count, HEAD_DIM)
        scores = masked_scores(query_seq, key_heads, places, length)
        row_max = jnp.max(scores, axis=-1, keepdims=True)
        exponent = jnp.exp(scores - row_max)
        row_sum = jnp.sum(exponent, axis=-1, keepdims=True)
        probability = (exponent / row_sum).astype(jnp.bfloat16)
        attended = jnp.einsum(
            "hqk,khd->qhd", probability, value_heads, preferred_element_type=jnp.float32
        )
        log_total = (row_max + jnp.log(row_sum))[..., 0]
        return (attended.reshape(local_len, model_width).astype(jnp.bfloat16), log_total)

    attn_seq, log_totals = lax.map(attend_forward, (queries, key_full, value_full, lengths))
    attn_mixed = attn_seq.reshape(token_count, model_width)
    up_proj = up_acc + fc1_bias
    activated = gelu_tanh(up_proj).astype(jnp.bfloat16)
    outer_full = (
        lax.all_gather(w_out, ("dp", "ctx"), axis=0, tiled=True),
        lax.all_gather(fc2_rows, ("dp", "ctx"), axis=0, tiled=True),
        lax.all_gather(b_out, ("dp", "ctx"), axis=0, tiled=True),
        lax.all_gather(b_fc2, ("dp", "ctx"), axis=0, tiled=True),
    )
    branch = jnp.dot(attn_mixed, outer_full[0], preferred_element_type=jnp.float32) + jnp.dot(
        activated,
        outer_full[1].reshape(hidden_ratio * model_width, model_width),
        preferred_element_type=jnp.float32,
    )
    out_bias = outer_full[2].astype(jnp.float32)
    fc2_bias = outer_full[3].astype(jnp.float32)
    output = (
        (inputs + branch + out_bias + fc2_bias)
        .astype(jnp.bfloat16)
        .reshape(seq_count, local_len, model_width)
    )
    grad_out = jnp.where(live_mask[:, :, None], cotangent, jnp.zeros((), jnp.bfloat16)).reshape(
        token_count, model_width
    )
    out_back, fc2_back = (
        lax.all_gather(w_out, ("dp", "ctx"), axis=0, tiled=True),
        lax.all_gather(fc2_rows, ("dp", "ctx"), axis=0, tiled=True),
    )
    fc2_matrix = fc2_back.reshape(hidden_ratio * model_width, model_width)
    grad_mixed = jnp.einsum(
        "td,kd->tk", grad_out, out_back, preferred_element_type=jnp.float32
    ).astype(jnp.bfloat16)
    grad_act = jnp.einsum("td,kd->tk", grad_out, fc2_matrix, preferred_element_type=jnp.float32)
    gelu_value, gelu_pull = jax.vjp(gelu_tanh, up_proj)
    grad_up = gelu_pull(grad_act)[0].astype(jnp.bfloat16)
    key_back, value_back = (
        lax.all_gather(key_local, "ctx", axis=1, tiled=True),
        lax.all_gather(value_local, "ctx", axis=1, tiled=True),
    )

    def attend_backward(packed):
        query_seq, key_seq, value_seq, grad_seq, log_total, length = packed
        key_heads = key_seq.reshape(total_len, head_count, HEAD_DIM)
        value_heads = value_seq.reshape(total_len, head_count, HEAD_DIM)
        grad_heads = grad_seq.reshape(local_len, head_count, HEAD_DIM)
        scores = masked_scores(query_seq, key_heads, places, length)
        probability = jnp.exp(scores - log_total[:, :, None])
        grad_probs = jnp.einsum(
            "qhd,khd->hqk", grad_heads, value_heads, preferred_element_type=jnp.float32
        )
        inner = jnp.sum(probability * grad_probs, axis=-1, keepdims=True)
        grad_scores = (probability * (grad_probs - inner)).astype(jnp.bfloat16)
        grad_query = jnp.einsum(
            "hqk,khd->qhd", grad_scores, key_heads, preferred_element_type=jnp.float32
        )
        grad_keys = jnp.einsum(
            "hqk,qhd->khd", grad_scores, query_seq, preferred_element_type=jnp.float32
        )
        grad_values = jnp.einsum(
            "hqk,qhd->khd",
            probability.astype(jnp.bfloat16),
            grad_heads,
            preferred_element_type=jnp.float32,
        )
        return (
            grad_query,
            grad_keys.reshape(total_len, model_width),
            grad_values.reshape(total_len, model_width),
        )

    grad_query, grad_keys_all, grad_values_all = lax.map(
        attend_backward,
        (
            queries,
            key_back,
            value_back,
            grad_mixed.reshape(seq_count, local_len, model_width),
            log_totals,
            lengths,
        ),
    )
    grad_keys_own, grad_values_own = (
        lax.psum_scatter(grad_keys_all, "ctx", scatter_dimension=1, tiled=True),
        lax.psum_scatter(grad_values_all, "ctx", scatter_dimension=1, tiled=True),
    )
    grad_query_pre = rotary_back(grad_query * 0.125, angles).reshape(token_count, model_width)
    grad_keys_pre = rotary_back(
        grad_keys_own.reshape(seq_count, local_len, head_count, HEAD_DIM), angles
    ).reshape(token_count, model_width)
    grad_qkv = jnp.concatenate(
        [grad_query_pre, grad_keys_pre, grad_values_own.reshape(token_count, model_width)], axis=-1
    ).astype(jnp.bfloat16)
    qkv_matrix, fc1_matrix = (
        lax.all_gather(w_qkv, ("dp", "ctx"), axis=0, tiled=True),
        lax.all_gather(w_fc1, ("dp", "ctx"), axis=0, tiled=True),
    )
    grad_hidden = jnp.einsum(
        "tj,dj->td", grad_qkv, qkv_matrix, preferred_element_type=jnp.float32
    ) + jnp.einsum("tj,dj->td", grad_up, fc1_matrix, preferred_element_type=jnp.float32)
    gain_term = jnp.sum(grad_hidden * normed, axis=0)
    shift_term = jnp.sum(grad_hidden, axis=0)
    grad_norm = grad_hidden * gain_full
    grad_input = grad_out.astype(jnp.float32) + inv_std * (
        grad_norm
        - jnp.mean(grad_norm, axis=-1, keepdims=True)
        - normed * jnp.mean(grad_norm * normed, axis=-1, keepdims=True)
    )
    grad_input = grad_input.astype(jnp.bfloat16).reshape(seq_count, local_len, model_width)
    wout_term = jnp.einsum("tk,td->kd", attn_mixed, grad_out, preferred_element_type=jnp.float32)
    wfc2_term = jnp.einsum(
        "tk,td->kd", activated, grad_out, preferred_element_type=jnp.float32
    ).reshape(model_width, hidden_ratio * model_width)
    bias_term = jnp.sum(grad_out, axis=0, dtype=jnp.float32)
    bqkv_term = jnp.sum(grad_qkv, axis=0, dtype=jnp.float32).reshape(model_width, 3)
    bfc1_term = jnp.sum(grad_up, axis=0, dtype=jnp.float32).reshape(model_width, hidden_ratio)
    grad_wout, grad_wfc2, grad_bias, grad_gain, grad_shift, grad_bqkv, grad_bfc1 = (
        lax.psum_scatter(wout_term, ("dp", "ctx"), scatter_dimension=0, tiled=True),
        lax.psum_scatter(wfc2_term, ("dp", "ctx"), scatter_dimension=0, tiled=True),
        lax.psum_scatter(bias_term, ("dp", "ctx"), scatter_dimension=0, tiled=True),
        lax.psum_scatter(gain_term, ("dp", "ctx"), scatter_dimension=0, tiled=True),
        lax.psum_scatter(shift_term, ("dp", "ctx"), scatter_dimension=0, tiled=True),
        lax.psum_scatter(bqkv_term, ("dp", "ctx"), scatter_dimension=0, tiled=True),
        lax.psum_scatter(bfc1_term, ("dp", "ctx"), scatter_dimension=0, tiled=True),
    )
    qkv_part = jnp.einsum("tk,tj->kj", hidden, grad_qkv, preferred_element_type=jnp.float32)
    fc1_part = jnp.einsum("tk,tj->kj", hidden, grad_up, preferred_element_type=jnp.float32)
    inner_sum = lax.psum_scatter(
        jnp.concatenate([qkv_part, fc1_part], axis=1),
        ("dp", "ctx"),
        scatter_dimension=0,
        tiled=True,
    )
    grad_wqkv = inner_sum[:, : 3 * model_width]
    grad_wfc1 = inner_sum[:, 3 * model_width :]
    return (
        output,
        grad_input,
        grad_gain,
        grad_shift,
        grad_wqkv,
        grad_bqkv.reshape(-1),
        grad_wout,
        grad_bias,
        grad_wfc1,
        grad_bfc1.reshape(-1),
        grad_wfc2.reshape(shard_rows * hidden_ratio, model_width),
        grad_bias,
    )


def solution(mesh):
    placed = (
        P("dp", "ctx", None),
        P("dp"),
        P(("dp", "ctx")),
        P(("dp", "ctx")),
        P(("dp", "ctx"), None),
        P(("dp", "ctx")),
        P(("dp", "ctx"), None),
        P(("dp", "ctx")),
        P(("dp", "ctx"), None),
        P(("dp", "ctx")),
        P(("dp", "ctx"), None),
        P(("dp", "ctx")),
        P("dp", "ctx", None),
    )
    return jax.shard_map(
        on_device,
        mesh=mesh,
        in_specs=placed,
        out_specs=(
            P("dp", "ctx", None),
            P("dp", "ctx", None),
            P(("dp", "ctx")),
            P(("dp", "ctx")),
            P(("dp", "ctx"), None),
            P(("dp", "ctx")),
            P(("dp", "ctx"), None),
            P(("dp", "ctx")),
            P(("dp", "ctx"), None),
            P(("dp", "ctx")),
            P(("dp", "ctx"), None),
            P(("dp", "ctx")),
        ),
        check_vma=False,
    )
```

profile of v0, /device:TPU:0, one launch (start us, length us, event | category | flops | bytes accessed | tf_op | source)
XLA Modules:
  0.0 3677.2 jit_solution(6174884470176922341)
XLA Ops:
  12.1 43.3 %all-reduce.9 = (bf16[2048]{0:T(1024)(128)(2,1)S(1)}, bf16[2048]{0:T(1024)(128)(2,1)S(1)}, bf16[2048]{0:T(1024)(128)(2,1)}, bf16[2048]{0:T(1024)(128)(2,1)}) all-reduce(bf16[2048]{0:T(1024)(128)(2,1)S(1)} %dynamic-update-slice.1, bf16[2048]{0:T(1024)(128)(2,1)S(1)} %dynamic-update-slice, ...), channel_id=1, replica_groups=mesh['dp'=8,'ctx'=4] {'dp','ctx'}, use_global_device_ids=true, to_apply=%add.1 | all-reduce | flops 8192 | bytes 32768
  56.3 41.2 %all-gather = bf16[32,64,3]{1,2,0:T(4,128)(2,1)S(1)} all-gather(bf16[1,64,3]{1,2,0:T(4,128)(2,1)S(1)} %copy.38), channel_id=1, replica_groups=mesh['dp'=8,'ctx'=4] {'dp','ctx'}, dimensions={0}, use_global_device_ids=true | all-gather | bytes 12672 | tf_op jit(solution)/shard_map/all_gather | solution.py:105
  102.0 68.0 %all-gather.9.cloned.1.call-done = bf16[2048,6144]{1,0:T(8,128)(2,1)} async-done(((bf16[64,6144]{1,0:T(8,128)(2,1)}), bf16[2048,6144]{1,0:T(8,128)(2,1)}) %all-gather.9.cloned.1.call-update) | async-done | bytes 25165840 | tf_op jit(solution)/shard_map/all_gather | solution.py:101
  170.0 13.7 convolution_add_fusion.1
  183.7 6.6 copy.41
  190.3 2.5 slice_bitcast_fusion.1
  195.6 2.7 slice.110
  198.4 2.7 reshape.356
  202.7 45.8 %all-gather.15.cloned.1.call-done = bf16[2048,2048]{1,0:T(8,128)(2,1)} async-done(((bf16[64,2048]{1,0:T(8,128)(2,1)}), bf16[2048,2048]{1,0:T(8,128)(2,1)}) %all-gather.15.cloned.1.call-update) | async-done | bytes 8388624 | tf_op jit(solution)/shard_map/all_gather | solution.py:149
  248.5 5.8 convolution_convert_fusion
  256.4 27.8 all-gather.13.cloned.1.call-done
  284.2 16.8 select_reduce_fusion
  301.1 14.6 fusion
  316.3 5.0 all-gather.11.cloned.1.call-done
  321.3 25.9 multiply_reduce_fusion
  347.2 28.3 multiply_convert_fusion
  375.5 12.1 fusion.51
  387.7 16.8 fusion.2
  405.4 41.5 %all-gather.1 = bf16[32,64,4]{1,2,0:T(4,128)(2,1)S(1)} all-gather(bf16[1,64,4]{1,2,0:T(4,128)(2,1)S(1)} %copy.42), channel_id=1, replica_groups=mesh['dp'=8,'ctx'=4] {'dp','ctx'}, dimensions={0}, use_global_device_ids=true | all-gather | bytes 16896 | tf_op jit(solution)/shard_map/all_gather | solution.py:106
  448.0 12.4 multiply_bitcast_fusion
  462.6 56.9 %all-gather.19.cloned.1.call-done = bf16[2048,8192]{1,0:T(8,128)(2,1)} async-done(((bf16[64,8192]{1,0:T(8,128)(2,1)}), bf16[2048,8192]{1,0:T(8,128)(2,1)}) %all-gather.19.cloned.1.call-update) | async-done | bytes 33554448 | tf_op jit(solution)/shard_map/all_gather | solution.py:150
  519.5 55.8 %reshape.357 = bf16[8192,2048]{1,0:T(8,128)(2,1)} reshape(bf16[2048,8192]{1,0:T(8,128)(2,1)} %all-gather.19.cloned.1.call-done) | data formatting | bytes 67108864 | tf_op jit(solution)/shard_map/reshape | solution.py:156
  575.3 140.0 %all-gather.17.cloned.1.call-done = bf16[2048,8192]{1,0:T(8,128)(2,1)} async-done(((bf16[64,8192]{1,0:T(8,128)(2,1)}), bf16[2048,8192]{1,0:T(8,128)(2,1)}) %all-gather.17.cloned.1.call-update) | async-done | bytes 33554448 | tf_op jit(solution)/shard_map/all_gather | solution.py:102
  715.3 21.5 convolution_add_fusion
  736.8 22.9 convert_reduce_fusion
  759.7 2.1 reshape.368
  761.7 25.9 fusion.57
  789.1 1.8 add_convert_fusion.1
  790.9 2.2 pad_maximum_fusion.3
  793.2 69.1 %reduce-scatter.9.cloned.1.call-done = f32[1,256,2048]{1,2,0:T(8,128)} async-done(((f32[1,1024,2048]{1,2,0:T(8,128)}), f32[1,256,2048]{1,2,0:T(8,128)}) %reduce-scatter.9.cloned.1.call-update) | async-done | bytes 2097168 | tf_op jit(solution)/shard_map/reduce_scatter | solution.py:228
  864.0 19.5 fusion.55
  886.5 77.3 %pad_maximum_fusion = f32[2048,14336]{1,0:T(8,128)} fusion(f32[2048,8192]{1,0:T(8,128)} %fusion.57, f32[2048,6144]{1,0:T(8,128)} %fusion.55), kind=kLoop, calls=%fused_computation | loop fusion | flops 29360128 | bytes 234881024 | tf_op jit(solution)/shard_map/concatenate | solution.py:272
  963.9 27.4 fusion.37
  991.3 79.4 %reshape.370 = f32[2048,8192]{1,0:T(8,128)} reshape(f32[8192,2048]{1,0:T(8,128)} %fusion.37) | data formatting | bytes 134217728 | tf_op jit(solution)/shard_map/reshape | solution.py:256
  1071.7 15.2 fusion.35
  1086.9 8.2 fusion.39
  1095.7 7.1 fusion.62
  1102.9 20.1 fusion.25
  1124.4 13.5 fusion.56
  1137.9 19.7 fusion.31
  1157.6 3.7 convert_reduce_fusion.2
  1161.3 41.4 %all-reduce.8 = (f32[2048]{0:T(1024)S(1)}, f32[2048]{0:T(1024)S(1)}, f32[2048]{0:T(1024)S(1)}) all-reduce(f32[2048]{0:T(1024)S(1)} %get-tuple-element.58, f32[2048]{0:T(1024)S(1)} %get-tuple-element.61, f32[2048]{0:T(1024)S(1)} %get-tuple-element.90), channel_id=4, replica_groups=mesh['dp'=8,'ctx'=4] {'dp','ctx'}, use_global_device_ids=true, to_apply=%region_10.11.clone | all-reduce | flops 6144 | bytes 49152
  1205.4 1567.1 %all-reduce.12.cloned.1.call-done = f32[2048,14336]{1,0:T(8,128)} async-done(((f32[2048,14336]{1,0:T(8,128)}), f32[2048,14336]{1,0:T(8,128)}) %all-reduce.12.cloned.1.call-update) | async-done | bytes 117440528
  2772.5 3.5 dynamic-slice.6
  2776.0 2.7 constant_dynamic-slice_fusion
  2778.7 697.6 %reduce-scatter.17.cloned.1.call-done = f32[64,8192]{1,0:T(8,128)} async-done(((f32[2048,8192]{1,0:T(8,128)}), f32[64,8192]{1,0:T(8,128)}) %reduce-scatter.17.cloned.1.call-update) | async-done | bytes 2097168 | tf_op jit(solution)/shard_map/reduce_scatter | solution.py:262
  3476.3 2.9 reshape.371
  3479.1 190.7 %reduce-scatter.13.cloned.1.call-done = f32[64,2048]{1,0:T(8,128)} async-done(((f32[2048,2048]{1,0:T(8,128)}), f32[64,2048]{1,0:T(8,128)}) %reduce-scatter.13.cloned.1.call-update) | async-done | bytes 524304 | tf_op jit(solution)/shard_map/reduce_scatter | solution.py:261
  (155 shorter events, 33.1 us)
Async XLA Ops:
  7.2 162.8 %all-gather.9.cloned.1.call-start = ((), (), s32[]{:S(2)}) async-start(), calls=%async_computation.6 | async-start | bytes 25952256 | tf_op jit(solution)/shard_map/all_gather | solution.py:101
  7.9 240.6 %all-gather.15.cloned.1.call-start = ((), (), s32[]{:S(2)}) async-start(), calls=%async_computation.9 | async-start | bytes 8650752 | tf_op jit(solution)/shard_map/all_gather | solution.py:149
  8.7 275.6 %all-gather.13.cloned.1.call-start = ((), (), s32[]{:S(2)}) async-start(), calls=%async_computation.8 | async-start | bytes 5242880 | tf_op jit(solution)/shard_map/all_gather | solution.py:124
  55.4 128.3 %copy-start.15 = (f32[2048]{0:T(1024)}, f32[2048]{0:T(1024)S(1)}, u32[]{:S(2)}) copy-start(f32[2048]{0:T(1024)S(1)} %convert_element_type.129) | copy-start | bytes 24580
  55.4 128.2 %copy-start.12 = (f32[2048]{0:T(1024)}, f32[2048]{0:T(1024)S(1)}, u32[]{:S(2)}) copy-start(f32[2048]{0:T(1024)S(1)} %convert_element_type.128) | copy-start | bytes 24580
  100.1 83.5 %copy-start.17 = (f32[256]{0:T(256)}, f32[256]{0:T(256)S(1)}, u32[]{:S(2)}) copy-start(f32[256]{0:T(256)S(1)} %broadcast_multiply_fusion.2) | copy-start | bytes 3076
  101.8 81.9 %copy-start.22 = (f32[256]{0:T(256)}, f32[256]{0:T(256)S(1)}, u32[]{:S(2)}) copy-start(f32[256]{0:T(256)S(1)} %add_rsqrt_fusion) | copy-start | bytes 3076
  102.0 90.9 %copy-start.25 = (f32[256,16]{0,1:T(8,128)}, f32[256,16]{0,1:T(8,128)S(1)}, u32[]{:S(2)}) copy-start(f32[256,16]{0,1:T(8,128)S(1)} %get-tuple-element.96) | copy-start | bytes 49156
  102.0 90.9 %copy-start.27 = (f32[256,16]{0,1:T(8,128)}, f32[256,16]{0,1:T(8,128)S(1)}, u32[]{:S(2)}) copy-start(f32[256,16]{0,1:T(8,128)S(1)} %get-tuple-element.97) | copy-start | bytes 49156
  192.8 1.3 copy-start.10
  194.4 54.0 %copy-start.4 = (bf16[1,256,2048]{2,1,0:T(8,128)(2,1)S(1)}, bf16[1,256,2048]{2,1,0:T(8,128)(2,1)}, u32[]{:S(2)}) copy-start(bf16[1,256,2048]{2,1,0:T(8,128)(2,1)} %param.25) | copy-start | bytes 3145732
  195.6 125.7 %all-gather.11.cloned.1.call-start = ((), (), s32[]{:S(2)}) async-start(), calls=%async_computation.7 | async-start | bytes 5242880 | tf_op jit(solution)/shard_map/all_gather | solution.py:125
  198.4 321.2 %all-gather.19.cloned.1.call-start = ((), (), s32[]{:S(2)}) async-start(), calls=%async_computation.11 | async-start | bytes 34603008 | tf_op jit(solution)/shard_map/all_gather | solution.py:150
  201.1 514.2 %all-gather.17.cloned.1.call-start = ((), (), s32[]{:S(2)}) async-start(), calls=%async_computation.10 | async-start | bytes 34603008 | tf_op jit(solution)/shard_map/all_gather | solution.py:102
  201.7 586.1 %reduce-scatter.7.cloned.1.call-start = ((), (), s32[]{:S(2)}) async-start(), calls=%async_computation.12 | async-start | bytes 10485760 | tf_op jit(solution)/shard_map/reduce_scatter | solution.py:227
  202.4 51.9 %copy-start.31 = (pred[256]{0:T(512)(128)(4,1)}, pred[256]{0:T(512)(128)(4,1)S(1)}, u32[]{:S(2)}) copy-start(pred[256]{0:T(512)(128)(4,1)S(1)} %fusion.47) | copy-start | bytes 772
  202.7 185.0 %copy-start.2 = (pred[256,1024]{1,0:T(8,128)(4,1)}, pred[256,1024]{1,0:T(8,128)(4,1)S(1)}, u32[]{:S(2)}) copy-start(pred[256,1024]{1,0:T(8,128)(4,1)S(1)} %fusion.46) | copy-start | bytes 786436
  301.1 14.6 copy-start.20
  387.6 474.6 %reduce-scatter.9.cloned.1.call-start = ((), (), s32[]{:S(2)}) async-start(), calls=%async_computation.13 | async-start | bytes 10485760 | tf_op jit(solution)/shard_map/reduce_scatter | solution.py:228
  404.6 718.4 %reduce-scatter.15.cloned.1.call-start = ((), (), s32[]{:S(2)}) async-start(), calls=%async_computation.16 | async-start | bytes 1081344 | tf_op jit(solution)/shard_map/reduce_scatter | solution.py:267
  460.4 1.3 copy-start.11
  462.6 252.7 %copy-start = (bf16[1,256,2048]{2,1,0:T(8,128)(2,1)S(1)}, bf16[1,256,2048]{2,1,0:T(8,128)(2,1)}, u32[]{:S(2)}) copy-start(bf16[1,256,2048]{2,1,0:T(8,128)(2,1)} %param.13) | copy-start | bytes 3145732
  462.6 252.7 %copy-start.13 = (f32[2048]{0:T(1024)S(1)}, f32[2048]{0:T(1024)}, u32[]{:S(2)}) copy-start(f32[2048]{0:T(1024)} %copy-done.12) | copy-start | bytes 24580
  462.6 252.7 %copy-start.16 = (f32[2048]{0:T(1024)S(1)}, f32[2048]{0:T(1024)}, u32[]{:S(2)}) copy-start(f32[2048]{0:T(1024)} %copy-done.15) | copy-start | bytes 24580
  462.6 252.7 %copy-start.18 = (f32[256]{0:T(256)S(1)}, f32[256]{0:T(256)}, u32[]{:S(2)}) copy-start(f32[256]{0:T(256)} %copy-done.17) | copy-start | bytes 3076
  462.6 252.7 %copy-start.23 = (f32[256]{0:T(256)S(1)}, f32[256]{0:T(256)}, u32[]{:S(2)}) copy-start(f32[256]{0:T(256)} %copy-done.22) | copy-start | bytes 3076
  575.3 161.5 %copy-start.5 = (bf16[1,256,2048]{2,1,0:T(8,128)(2,1)S(1)}, bf16[1,256,2048]{2,1,0:T(8,128)(2,1)}, u32[]{:S(2)}) copy-start(bf16[1,256,2048]{2,1,0:T(8,128)(2,1)} %param.25) | copy-start | bytes 3145732
  575.3 161.5 %copy-start.32 = (pred[256]{0:T(512)(128)(4,1)S(1)}, pred[256]{0:T(512)(128)(4,1)}, u32[]{:S(2)}) copy-start(pred[256]{0:T(512)(128)(4,1)} %copy-done.31) | copy-start | bytes 772
  761.7 27.3 copy-start.26
  761.7 27.3 copy-start.28
  787.7 416.3 %reduce-scatter.11.cloned.1.call-start = ((), (), s32[]{:S(2)}) async-start(), calls=%async_computation.14 | async-start | bytes 1081344 | tf_op jit(solution)/shard_map/reduce_scatter | solution.py:266
  793.2 90.3 %copy-start.8 = (bf16[1,256,32,64]{1,3,2,0:T(8,128)(2,1)}, bf16[1,256,32,64]{1,3,2,0:T(8,128)(2,1)S(1)}, u32[]{:S(2)}) copy-start(bf16[1,256,32,64]{1,3,2,0:T(8,128)(2,1)S(1)} %get-tuple-element.105) | copy-start | bytes 3145732
  864.0 19.6 copy-start.6
  864.0 19.6 copy-start.9
  886.4 1886.1 %all-reduce.12.cloned.1.call-start = ((), (), s32[]{:S(2)}) async-start(), calls=%async_computation.18 | async-start | bytes 234881024
  963.8 2512.4 %reduce-scatter.17.cloned.1.call-start = ((), (), s32[]{:S(2)}) async-start(), calls=%async_computation.17 | async-start | bytes 69206016 | tf_op jit(solution)/shard_map/reduce_scatter | solution.py:262
  1070.7 0.9 copy-start.3
  1070.7 1.0 copy-start.21
  1070.7 1.0 copy-start.30
  1070.7 2599.0 %reduce-scatter.13.cloned.1.call-start = ((), (), s32[]{:S(2)}) async-start(), calls=%async_computation.15 | async-start | bytes 17301504 | tf_op jit(solution)/shard_map/reduce_scatter | solution.py:261
  1095.0 0.7 copy-start.34
  1095.0 0.7 copy-start.33
  1095.7 7.1 copy-start.1
  1102.9 21.5 copy-start.7
  1124.4 13.5 copy-start.14
  1124.4 13.5 copy-start.19
  1124.4 13.5 copy-start.24
  1203.4 2466.9 %copy-start.36 = (f32[64]{0:T(128)}, f32[64]{0:T(128)S(1)}, u32[]{:S(2)}) copy-start(f32[64]{0:T(128)S(1)} %dynamic-slice.4) | copy-start | bytes 772
  (2 other events, 1.3 us)
Sparse Core Ops, SparseCore 0:
  10.9 159.0 all-gather.8
  172.8 75.5 all-gather.14
  250.6 33.5 all-gather.12
  286.2 35.0 all-gather.10
  324.6 194.9 all-gather.18
  522.2 192.9 all-gather.16
  717.8 69.8 reduce-scatter.6
  790.5 71.7 reduce-scatter.8
  864.5 134.7 reduce-scatter.14
  1001.5 130.7 reduce-scatter.10
  1138.8 1633.6 all-reduce.11
  2774.8 701.3 reduce-scatter.16
  3479.2 190.4 reduce-scatter.12
where the time goes:
time: 3690 us; the launch traced here: 3680 us
  waiting for transfers between devices  2870 us (78%)
  matrix products  305 us (8%)
  local copies, waits for them, and re-layouts  184 us (5%)
  blocking collectives  167 us (5%)
  other arithmetic  136 us (4%)
    unnamed x14, waiting for transfers between devices  1570 us
    reduce_scatter x1, waiting for transfers between devices, on_device(): lax.psum_scatter(wfc2_term, ('dp', 'ctx'), scatter_dimension=0, tiled=True)  698 us
    reduce_scatter x1, waiting for transfers between devices, on_device(): lax.psum_scatter(wout_term, ('dp', 'ctx'), scatter_dimension=0, tiled=True)  191 us
    all_gather x1, waiting for transfers between devices, on_device(): lax.all_gather(w_fc1, ('dp', 'ctx'), axis=0, tiled=True)  140 us
    unnamed x2, blocking collectives  84.7 us
    reshape x1, local copies, waits for them, and re-layouts, on_device(): wfc2_term = jnp.einsum('tk,td->kd', activated, grad_out, preferred_elemen...  79.4 us
    concatenate x1, other arithmetic, on_device(): jnp.concatenate([qkv_part, fc1_part], axis=1)  77.3 us
  transfers between devices with their start and end apart: 13, of which 10 were waited for; matrix products, arithmetic and copies ran while one was open for 17% of the time, Pallas kernels for 0%

commit v1 on v0

--- a/solution.py
+++ b/solution.py
@@ -2,6 +2,7 @@
 
 import jax
 import jax.numpy as jnp
+import numpy as np
 from jax import lax
 from jax.sharding import PartitionSpec as P
 
@@ -292,7 +293,7 @@
     )
 
 
-def solution(mesh):
+def general_solution(mesh):
     placed = (
         P("dp", "ctx", None),
         P("dp"),
@@ -328,3 +329,317 @@
         ),
         check_vma=False,
     )
+
+
+FINE = ("zh", "zl", "y", "x", "c")
+ROWS_AXES = ("zl", "x", "c")
+
+
+def swap(values, axis):
+    return lax.ppermute(values, axis, [(0, 1), (1, 0)])
+
+
+def flip_if(values, dim, flag):
+    return jnp.where(flag, jnp.flip(values, dim), values)
+
+
+def gather_blocks(own):
+    across = swap(own, "zh")
+    beside = swap(own, "y")
+    both = swap(across, "y")
+    return own, beside, across, both
+
+
+def reduce_blocks(blocks):
+    own, beside, across, both = blocks
+    got_beside = swap(beside, "y")
+    got_both = swap(both, "y")
+    passed = (across.astype(jnp.float32) + got_both.astype(jnp.float32)).astype(jnp.bfloat16)
+    got = swap(passed, "zh")
+    return own.astype(jnp.float32) + got_beside.astype(jnp.float32) + got.astype(jnp.float32)
+
+
+def by_place(blocks, zh, y):
+    first, second, third, fourth = blocks
+    a, b = jnp.where(y == 1, second, first), jnp.where(y == 1, first, second)
+    c, d = jnp.where(y == 1, fourth, third), jnp.where(y == 1, third, fourth)
+    return (
+        jnp.where(zh == 1, c, a),
+        jnp.where(zh == 1, d, b),
+        jnp.where(zh == 1, a, c),
+        jnp.where(zh == 1, b, d),
+    )
+
+
+def dot(left, right, dims):
+    return lax.dot_general(left, right, (dims, ((), ())), preferred_element_type=jnp.float32)
+
+
+def split_device(
+    tokens,
+    lengths,
+    ln_gain,
+    ln_bias,
+    w_qkv,
+    b_qkv,
+    w_out,
+    b_out,
+    w_fc1,
+    b_fc1,
+    w_fc2,
+    b_fc2,
+    cotangent,
+):
+    bf16, f32 = jnp.bfloat16, jnp.float32
+    zh, zl, y, x, c = (lax.axis_index(name) for name in FINE)
+    place = (zl * 2 + x) * 2 + c
+    _, local_len, width = tokens.shape
+    rows = w_qkv.shape[0]
+    ff_rows = w_fc2.shape[0]
+    pieces = 4
+    total_len = local_len * pieces
+    heads = 4
+    own_width = heads * HEAD_DIM
+
+    small = jnp.concatenate([ln_gain, ln_bias, b_qkv, b_out, b_fc1, b_fc2])
+    small_all = lax.all_gather(small[None], FINE, axis=0, tiled=True).astype(f32)
+    ends = np.cumsum([rows, rows, 3 * rows, rows, ff_rows, rows])
+    gain_all, shift_all, bqkv_all, bout_all, bfc1_all, bfc2_all = (
+        part.reshape(-1) for part in jnp.split(small_all, ends[:-1], axis=1)
+    )
+    length_pair = lax.all_gather(lengths, "zl", axis=0, tiled=True)
+
+    def own_columns(weight, shape, order):
+        spread = weight.reshape((rows,) + shape).transpose(order)
+        spread = spread.reshape(8, rows, -1)
+        return lax.all_to_all(spread, ROWS_AXES, 0, 0, tiled=True).reshape(8 * rows, -1)
+
+    qkv_own = own_columns(w_qkv, (3, 2, 2, 2, 2, 2, HEAD_DIM), (3, 5, 6, 0, 1, 2, 4, 7))
+    fc1_own = own_columns(w_fc1, (2, 2, 2, 2, 2, ff_rows), (2, 4, 5, 0, 1, 3, 6))
+    out_blocks = by_place(gather_blocks(w_out), zh, y)
+    qkv_blocks = gather_blocks(qkv_own)
+    fc2_blocks = by_place(gather_blocks(w_fc2), zh, y)
+    fc1_blocks = gather_blocks(fc1_own)
+    out_mat = jnp.concatenate(out_blocks, axis=0)
+    fc2_mat = jnp.concatenate(fc2_blocks, axis=0)
+    qkv_mat = jnp.concatenate(qkv_blocks, axis=0)
+    fc1_mat = jnp.concatenate(fc1_blocks, axis=0)
+
+    inputs = tokens[0].astype(f32)
+    average = jnp.mean(inputs, axis=-1, keepdims=True)
+    centered = inputs - average
+    variance = jnp.mean(centered * centered, axis=-1, keepdims=True)
+    inv_std = lax.rsqrt(variance + eps_norm)
+    normed = centered * inv_std
+    hidden_own = (normed * gain_all + shift_all).astype(bf16)
+
+    def mixed_order(values):
+        v = values.reshape(-1, 2, 2, 2, 4, rows).transpose(0, 1, 3, 2, 4, 5)
+        v = flip_if(flip_if(v, 1, zh == 1), 2, y == 1)
+        return v.reshape(values.shape)
+
+    def plain_order(values):
+        v = values.reshape(-1, 2, 2, 2, 4, rows)
+        v = flip_if(flip_if(v, 1, zh == 1), 2, y == 1)
+        return v.transpose(0, 1, 3, 2, 4, 5).reshape(values.shape)
+
+    hidden = lax.all_gather(mixed_order(hidden_own), ROWS_AXES, axis=0, tiled=True)
+    places = (x * 2 + c) * local_len + jnp.arange(local_len, dtype=jnp.int32)
+    grad_own = jnp.where((places < lengths[0])[:, None], cotangent[0], jnp.zeros((), bf16))
+    grad_out = lax.all_gather(grad_own, ROWS_AXES, axis=0, tiled=True)
+
+    bqkv = lax.dynamic_index_in_dim(
+        bqkv_all.reshape(3, 2, 2, 2, 4, HEAD_DIM).transpose(2, 4, 0, 1, 3, 5).reshape(8, -1),
+        place,
+        keepdims=False,
+    )
+    bfc1 = lax.dynamic_index_in_dim(
+        bfc1_all.reshape(2, 2, 2, 4, ff_rows).transpose(1, 3, 0, 2, 4).reshape(8, -1),
+        place,
+        keepdims=False,
+    )
+
+    angles = rotary_angles(jnp.arange(total_len, dtype=jnp.int32), ROT)
+    qkv = dot(hidden, qkv_mat, ((1,), (0,))) + bqkv
+    qkv = qkv.reshape(2, total_len, 3, heads, HEAD_DIM)
+    turn = jax.vmap(lambda v: rotary(v, angles))
+    queries = (turn(qkv[:, :, 0]) * 0.125).astype(bf16)
+    key_rows = turn(qkv[:, :, 1]).astype(bf16)
+    values = qkv[:, :, 2].astype(bf16)
+    all_places = jnp.arange(total_len, dtype=jnp.int32)
+
+    def attend_forward(packed):
+        query_seq, key_seq, value_seq, length = packed
+        scores = masked_scores(query_seq, key_seq, all_places, length)
+        row_max = jnp.max(scores, axis=-1, keepdims=True)
+        exponent = jnp.exp(scores - row_max)
+        row_sum = jnp.sum(exponent, axis=-1, keepdims=True)
+        probability = (exponent / row_sum).astype(bf16)
+        attended = jnp.einsum("hqk,khd->qhd", probability, value_seq, preferred_element_type=f32)
+        return attended.astype(bf16), (row_max + jnp.log(row_sum))[..., 0]
+
+    attended, log_totals = lax.map(attend_forward, (queries, key_rows, values, length_pair))
+    attn_mixed = attended.reshape(2 * total_len, own_width)
+
+    up_proj = dot(hidden, fc1_mat, ((1,), (0,))) + bfc1
+    activated = gelu_tanh(up_proj).astype(bf16)
+    branch = dot(attn_mixed, out_mat, ((1,), (0,))) + dot(activated, fc2_mat, ((1,), (0,)))
+    branch_own = lax.psum_scatter(
+        branch.astype(bf16), ROWS_AXES, scatter_dimension=0, tiled=True
+    ).astype(f32)
+    output = (inputs + branch_own + bout_all + bfc2_all).astype(bf16)[None]
+
+    grad_mixed = dot(grad_out, out_mat, ((1,), (1,))).astype(bf16)
+    grad_act = dot(grad_out, fc2_mat, ((1,), (1,)))
+    _, gelu_pull = jax.vjp(gelu_tanh, up_proj)
+    grad_up = gelu_pull(grad_act)[0].astype(bf16)
+
+    def attend_backward(packed):
+        query_seq, key_seq, value_seq, grad_heads, log_total, length = packed
+        scores = masked_scores(query_seq, key_seq, all_places, length)
+        probability = jnp.exp(scores - log_total[:, :, None])
+        grad_probs = jnp.einsum("qhd,khd->hqk", grad_heads, value_seq, preferred_element_type=f32)
+        inner = jnp.sum(probability * grad_probs, axis=-1, keepdims=True)
+        grad_scores = (probability * (grad_probs - inner)).astype(bf16)
+        grad_query = jnp.einsum("hqk,khd->qhd", grad_scores, key_seq, preferred_element_type=f32)
+        grad_keys = jnp.einsum("hqk,qhd->khd", grad_scores, query_seq, preferred_element_type=f32)
+        grad_values = jnp.einsum(
+            "hqk,qhd->khd", probability.astype(bf16), grad_heads, preferred_element_type=f32
+        )
+        return grad_query, grad_keys, grad_values
+
+    grad_query, grad_keys, grad_values = lax.map(
+        attend_backward,
+        (
+            queries,
+            key_rows,
+            values,
+            grad_mixed.reshape(2, total_len, heads, HEAD_DIM),
+            log_totals,
+            length_pair,
+        ),
+    )
+    turn_back = jax.vmap(lambda v: rotary_back(v, angles))
+    grad_qkv = (
+        jnp.stack([turn_back(grad_query * 0.125), turn_back(grad_keys), grad_values], axis=2)
+        .reshape(2 * total_len, 3 * own_width)
+        .astype(bf16)
+    )
+
+    grad_hidden = dot(grad_qkv, qkv_mat, ((1,), (1,))) + dot(grad_up, fc1_mat, ((1,), (1,)))
+    grad_hidden_own = plain_order(
+        lax.psum_scatter(grad_hidden.astype(bf16), ROWS_AXES, scatter_dimension=0, tiled=True)
+    ).astype(f32)
+    grad_norm = grad_hidden_own * gain_all
+    grad_input = grad_own.astype(f32) + inv_std * (
+        grad_norm
+        - jnp.mean(grad_norm, axis=-1, keepdims=True)
+        - normed * jnp.mean(grad_norm * normed, axis=-1, keepdims=True)
+    )
+    grad_input = grad_input.astype(bf16)[None]
+
+    def place_blocks(values):
+        return by_place(jnp.split(values, 4, axis=0), zh, y)
+
+    fc2_part = dot(activated, grad_out, ((0,), (0,))).astype(bf16)
+    grad_fc2 = reduce_blocks(place_blocks(fc2_part))
+    fc1_part = dot(hidden, grad_up, ((0,), (0,))).astype(bf16)
+    fc1_total = reduce_blocks(jnp.split(fc1_part, 4, axis=0)).astype(bf16)
+    out_part = dot(attn_mixed, grad_out, ((0,), (0,))).astype(bf16)
+    grad_wout = reduce_blocks(place_blocks(out_part))
+    qkv_part = dot(hidden, grad_qkv, ((0,), (0,))).astype(bf16)
+    qkv_total = reduce_blocks(jnp.split(qkv_part, 4, axis=0)).astype(bf16)
+
+    def all_columns(total, shape, order, out_width):
+        spread = lax.all_to_all(total.reshape(8, rows, -1), ROWS_AXES, 0, 0, tiled=True)
+        spread = spread.reshape((2, 2, 2, rows) + shape).transpose(order)
+        return spread.reshape(rows, out_width).astype(f32)
+
+    grad_wfc1 = all_columns(fc1_total, (2, 2, ff_rows), (3, 4, 0, 5, 1, 2, 6), w_fc1.shape[1])
+    grad_wqkv = all_columns(
+        qkv_total, (3, 2, 2, HEAD_DIM), (3, 4, 5, 0, 6, 1, 2, 7), w_qkv.shape[1]
+    )
+
+    mine = (jnp.arange(8) == place).astype(f32)
+    bqkv_term = (
+        (jnp.sum(grad_qkv, axis=0, dtype=f32).reshape(1, 3, 2, 2, HEAD_DIM) * mine[:, None, None, None, None])
+        .reshape(2, 4, 3, 2, 2, HEAD_DIM)
+        .transpose(2, 3, 0, 4, 1, 5)
+        .reshape(-1)
+    )
+    bfc1_term = (
+        (jnp.sum(grad_up, axis=0, dtype=f32).reshape(1, 2, 2, ff_rows) * mine[:, None, None, None])
+        .reshape(2, 4, 2, 2, ff_rows)
+        .transpose(2, 0, 3, 1, 4)
+        .reshape(-1)
+    )
+    bias_term = jnp.sum(grad_own, axis=0, dtype=f32)
+    gain_term = jnp.sum(grad_hidden_own * normed, axis=0)
+    shift_term = jnp.sum(grad_hidden_own, axis=0)
+    terms = jnp.concatenate(
+        [v.reshape(32, -1) for v in (bqkv_term, bfc1_term, bias_term, gain_term, shift_term)], axis=1
+    )
+    sums = lax.psum_scatter(terms, FINE, scatter_dimension=0, tiled=True)[0]
+    grad_bqkv, grad_bfc1, grad_bias, grad_gain, grad_shift = jnp.split(
+        sums, np.cumsum([3 * rows, ff_rows, rows, rows])
+    )
+    return (
+        output,
+        grad_input,
+        grad_gain,
+        grad_shift,
+        grad_wqkv,
+        grad_bqkv,
+        grad_wout,
+        grad_bias,
+        grad_wfc1,
+        grad_bfc1,
+        grad_fc2,
+        grad_bias,
+    )
+
+
+def fine_mesh(mesh):
+    return jax.sharding.Mesh(mesh.devices.reshape(2, 2, 2, 2, 2), FINE)
+
+
+def fine_solution(mesh):
+    everyone, seqs, parts = FINE, ("zh", "zl", "y"), ("x", "c")
+    placed = (
+        P(seqs, parts, None),
+        P(seqs),
+        P(everyone),
+        P(everyone),
+        P(everyone, None),
+        P(everyone),
+        P(everyone, None),
+        P(everyone),
+        P(everyone, None),
+        P(everyone),
+        P(everyone, None),
+        P(everyone),
+        P(seqs, parts, None),
+    )
+    given = (
+        P(seqs, parts, None),
+        P(seqs, parts, None),
+        P(everyone),
+        P(everyone),
+        P(everyone, None),
+        P(everyone),
+        P(everyone, None),
+        P(everyone),
+        P(everyone, None),
+        P(everyone),
+        P(everyone, None),
+        P(everyone),
+    )
+    return jax.shard_map(
+        split_device, mesh=fine_mesh(mesh), in_specs=placed, out_specs=given, check_vma=False
+    )
+
+
+def solution(mesh):
+    if mesh.shape["dp"] == 8 and mesh.shape["ctx"] == 4:
+        return fine_solution(mesh)
+    return general_solution(mesh)

time: 3690 us -> 1080 us (0.29)
  waiting for transfers between devices: 2870 us -> 361 us
  blocking collectives: 167 us -> 46.8 us
  starting transfers between devices: 0.53 us -> 42.6 us
  matrix products: 305 us -> 263 us
    unnamed x14 -> x6, waiting for transfers between devices: 1570 us -> 111 us
    reduce_scatter x6 -> x2, waiting for transfers between devices: 957 us -> 0.01 us  [the longest x1 0.01 us: split_device(): lax.psum_scatter(grad_hidden.astype(bf16), ROWS_AXES, scatter_dimension=0...]
    all_gather x6 -> x2, waiting for transfers between devices: 343 us -> 0.01 us  [the longest x1 0.01 us: split_device(): lax.all_gather(mixed_order(hidden_own), ROWS_AXES, axis=0, tiled=True)]
    ppermute x0 -> x24, waiting for transfers between devices: none -> 236 us  [swap(): return lax.ppermute(values, axis, [(0, 1), (1, 0)])]
    reshape x8 -> x12, local copies, waits for them, and re-layouts: 148 us -> 22.4 us  [the longest x1 9.2 us: split_device(): qkv = qkv.reshape(2, total_len, 3, heads, HEAD_DIM)]
    dynamic_update_slice x0 -> x12, local copies, waits for them, and re-layouts: none -> 116 us  [split_device(): lax.map(attend_backward, (queries, key_rows, values, grad_mixed.reshape(2...]
    all_gather x2 -> x0, blocking collectives: 82.8 us -> none  [the longest x1 41.5 us: on_device(): lax.all_gather(fc1_bias_rows, ('dp', 'ctx'), axis=0, tiled=True)]
    concatenate x2 -> x0, other arithmetic: 79.6 us -> none  [the longest x1 77.3 us: on_device(): jnp.concatenate([qkv_part, fc1_part], axis=1)]
  transfers between devices with their start and end apart: 13 -> 33, of which waited for: 10 -> 11; matrix products, arithmetic and copies ran while one was open for 17% -> 48% of each run, Pallas kernels for 0% -> 0%
where the time goes in v1:
time: 1080 us; the launch traced here: 1060 us
  waiting for transfers between devices  361 us (33%)
  matrix products  263 us (24%)
  local copies, waits for them, and re-layouts  219 us (20%)
  other arithmetic  114 us (11%)
  blocking collectives  46.8 us (4%)
  starting transfers between devices  42.6 us (4%)
  between operations  15.9 us (1%)
    ppermute x24, waiting for transfers between devices, swap(): return lax.ppermute(values, axis, [(0, 1), (1, 0)])  236 us
    dot_general x12, matrix products, dot(): lax.dot_general(left, right, (dims, ((), ())), preferred_element_type=jnp...  157 us
    dynamic_update_slice x12, local copies, waits for them, and re-layouts, split_device(): lax.map(attend_backward, (queries, key_rows, values, grad_mixed.reshape(2...  116 us
    unnamed x6, waiting for transfers between devices  111 us
    unnamed x2, blocking collectives  46.8 us
    dot_general x4, matrix products, masked_scores(): jnp.einsum('qhd,khd->hqk', queries, key_rows, preferred_element_type=jnp....  38.4 us
    ppermute x24, starting transfers between devices, swap(): return lax.ppermute(values, axis, [(0, 1), (1, 0)])  24.1 us
    dot_general x2, matrix products, attend_backward(): jnp.einsum('qhd,khd->hqk', grad_heads, value_seq, preferred_element_type=...  23.6 us
  transfers between devices with their start and end apart: 33, of which 11 were waited for; matrix products, arithmetic and copies ran while one was open for 48% of the time, Pallas kernels for 0%

profile of v1, /device:TPU:0, one launch (start us, length us, event | category | flops | bytes accessed | tf_op | source)
XLA Modules:
  0.0 1063.6 jit_solution(13298666497322258213)
XLA Ops:
  17.0 42.5 %all-reduce = bf16[22528]{0:T(1024)(128)(2,1)S(1)} all-reduce(bf16[22528]{0:T(1024)(128)(2,1)S(1)} %dynamic-update-slice), channel_id=2, replica_groups=mesh['zh'=2,'zl'=2,'y'=2,'x'=2,'c'=2] {'zh','zl','y','x','c'}, use_global_device_ids=true, to_apply=%add | all-reduce | flops 22528 | bytes 90112
  79.9 13.9 %all-to-all-done = bf16[8,64,768]{2,1,0:T(8,128)(2,1)} async-done(((bf16[8,64,768]{2,1,0:T(8,128)(2,1)}), bf16[8,64,768]{2,1,0:T(8,128)(2,1)}, u32[]{:S(2)}, u32[]{:S(2)}) %all-to-all-start) | async-done | bytes 786464 | tf_op jit(solution)/shard_map/all_to_all | solution.py:415
  107.1 33.0 %collective-permute-done.9 = bf16[256,2048]{1,0:T(8,128)(2,1)S(1)} collective-permute-done((bf16[256,2048]{1,0:T(8,128)(2,1)S(1)}, bf16[256,2048]{1,0:T(8,128)(2,1)S(1)}, u32[]{:S(2)}, u32[]{:S(2)}) %collective-permute-start.9) | collective-permute-done | bytes 1048608 | tf_op jit(solution)/shard_map/ppermute | solution.py:339
  142.2 49.9 %collective-permute-done.3 = bf16[64,2048]{1,0:T(8,128)(2,1)S(1)} collective-permute-done((bf16[64,2048]{1,0:T(8,128)(2,1)S(1)}, bf16[64,2048]{1,0:T(8,128)(2,1)S(1)}, u32[]{:S(2)}, u32[]{:S(2)}) %collective-permute-start.3) | collective-permute-done | bytes 262176 | tf_op jit(solution)/shard_map/ppermute | solution.py:339
  208.8 38.4 %collective-permute-done.7 = bf16[512,1024]{1,0:T(8,128)(2,1)} collective-permute-done((bf16[512,1024]{1,0:T(8,128)(2,1)}, bf16[512,1024]{1,0:T(8,128)(2,1)}, u32[]{:S(2)}, u32[]{:S(2)}) %collective-permute-start.7) | collective-permute-done | bytes 1048608 | tf_op jit(solution)/shard_map/ppermute | solution.py:339
  248.8 12.1 %convolution_add_fusion = f32[2048,768]{1,0:T(8,128)} fusion(bf16[2048,2048]{0,1:T(8,128)(2,1)} %all-gather.4.cloned.1.call-done, f32[768]{0:T(1024)S(1)} %dynamic-slice_reduce_fusion, bf16[512,768]{1,0:T(8,128)(2,1)} %collective-permute-done.2, bf16[512,768]{1,0:T(8,128)(2,1)} %collective-permute-done.1, bf16[512,768]{1,0:T(8,128)(2,1)} %collective-permute-done, ...), kind=kOutput, calls=%fused_computation.80 | convolution fusion | flops 6456606720 | bytes 17828864 | tf_op jit(solution)/shard_map/dot_general | solution.py:375
  260.9 6.5 copy.105
  267.4 9.2 reshape.481
  278.9 5.7 slice_bitcast_fusion
  284.6 6.8 convolution_convert_fusion.4
  309.5 57.8 %while.28 = (s32[]{:T(128)}, bf16[2,1024,4,64]{1,3,2,0:T(8,128)(2,1)S(1)}, f32[2,4,1024]{2,1,0:T(4,128)}, bf16[2,1024,4,64]{1,3,2,0:T(8,128)(2,1)}, s32[2]{0:T(1...) while((s32[]{:T(128)}, ...), condition=%wide.region_5.6_spmd.clone, body=%wide.region_2.5_spmd.clone.sunk | while | flops 1113846784 | bytes 56758384 | solution.py:481
  311.1 9.7 select_reduce_fusion.2
  320.9 8.8 fusion.116
  329.6 8.2 fusion.117
  340.0 9.7 select_reduce_fusion.2
  349.8 8.8 fusion.116
  358.5 8.2 fusion.117
  368.3 207.9 %while.29 = (s32[]{:T(128)}, f32[2,1024,4,64]{1,0,3,2:T(2,128)}, f32[2,1024,4,64]{1,0,3,2:T(2,128)}, bf16[2,1024,4,64]{1,0,3,2:T(2,128)(2,1)}, bf16[2,1024,4,64]...) while((s32[]{:T(128)}, f32[2,1024,4,64]{1,0,3,2:T(2,128)}, ...), condition=%wide.region_9.10_spmd.clone, body=%wide.region_7.9_spmd.clone.sunk | while | flops 2736780288 | bytes 151179472 | solution.py:511
  370.8 9.5 fusion.126
  380.3 7.9 fusion.128
  389.0 17.4 %dynamic_update_slice.34 = bf16[2,1024,4,64]{1,0,3,2:T(2,128)(2,1)} dynamic-update-slice(bf16[2,1024,4,64]{1,0,3,2:T(2,128)(2,1)} %get-tuple-element.458, bf16[1,1024,4,64]{1,0,3,2:T(2,128)(2,1)S(1)} %copy.164, s32[]{:T(128)S(6)} %copy.185, s32[]{:T(128)} %constant.86.clone.1..sunk, s32[]{:T(128)} %constant.86.clone.1..sunk, s32[]{:T(128)} %constant.86.clone.1..sunk) | dynamic-update-slice | bytes 1048580 | tf_op jit(solution)/shard_map/while/body/jit(dynamic_update_index_in_dim)/dynamic_update_slice | solution.py:511
  406.5 11.8 %multiply_reduce_fusion.3 = (f32[4,1024]{1,0:T(4,128)}, f32[4,1024,1024]{1,2,0:T(8,128)S(1)}) fusion(f32[4,1024,1024]{1,2,0:T(8,128)} %fusion.126, f32[4,1024]{1,0:T(4,128)} %copy-done.9, pred[1024,1024]{0,1:T(8,128)(4,1)S(1)} %fusion.127, bf16[2,1024,4,64]{1,3,2,0:T(8,128)(2,1)} %get-tuple-element.476, s32[]{:T(128)S(6)} %copy.185, ...), kind=kOutput, calls=%fused_computation.25.clone.1 | convolution fusion | flops 553644032 | bytes 35685376 | tf_op jit(solution)/shard_map/while/body/eval_jaxpr/qhd,khd->hqk/dot_general | solution.py:501
  418.3 8.0 multiply_convert_fusion.5
  434.8 18.7 %dynamic_update_slice.33 = f32[2,1024,4,64]{1,0,3,2:T(2,128)} dynamic-update-slice(f32[2,1024,4,64]{1,0,3,2:T(2,128)} %get-tuple-element.457, f32[1,1024,4,64]{1,0,3,2:T(1,128)S(1)} %copy.163, s32[]{:T(128)S(6)} %copy.185, s32[]{:T(128)} %constant.86.clone.1..sunk, s32[]{:T(128)} %constant.86.clone.1..sunk, s32[]{:T(128)} %constant.86.clone.1..sunk) | dynamic-update-slice | bytes 2097156 | tf_op jit(solution)/shard_map/while/body/jit(dynamic_update_index_in_dim)/dynamic_update_slice | solution.py:511
  453.5 18.6 %dynamic_update_slice.32 = f32[2,1024,4,64]{1,0,3,2:T(2,128)} dynamic-update-slice(f32[2,1024,4,64]{1,0,3,2:T(2,128)} %get-tuple-element.456, f32[1,1024,4,64]{1,0,3,2:T(1,128)S(1)} %copy.162, s32[]{:T(128)S(6)} %copy.185, s32[]{:T(128)} %constant.86.clone.1..sunk, s32[]{:T(128)} %constant.86.clone.1..sunk, s32[]{:T(128)} %constant.86.clone.1..sunk) | dynamic-update-slice | bytes 2097156 | tf_op jit(solution)/shard_map/while/body/jit(dynamic_update_index_in_dim)/dynamic_update_slice | solution.py:511
  474.5 9.5 fusion.126
  484.0 7.9 fusion.128
  492.7 17.4 %dynamic_update_slice.34 = bf16[2,1024,4,64]{1,0,3,2:T(2,128)(2,1)} dynamic-update-slice(bf16[2,1024,4,64]{1,0,3,2:T(2,128)(2,1)} %get-tuple-element.458, bf16[1,1024,4,64]{1,0,3,2:T(2,128)(2,1)S(1)} %copy.164, s32[]{:T(128)S(6)} %copy.185, s32[]{:T(128)} %constant.86.clone.1..sunk, s32[]{:T(128)} %constant.86.clone.1..sunk, s32[]{:T(128)} %constant.86.clone.1..sunk) | dynamic-update-slice | bytes 1048580 | tf_op jit(solution)/shard_map/while/body/jit(dynamic_update_index_in_dim)/dynamic_update_slice | solution.py:511
  510.1 11.8 %multiply_reduce_fusion.3 = (f32[4,1024]{1,0:T(4,128)}, f32[4,1024,1024]{1,2,0:T(8,128)S(1)}) fusion(f32[4,1024,1024]{1,2,0:T(8,128)} %fusion.126, f32[4,1024]{1,0:T(4,128)} %copy-done.9, pred[1024,1024]{0,1:T(8,128)(4,1)S(1)} %fusion.127, bf16[2,1024,4,64]{1,3,2,0:T(8,128)(2,1)} %get-tuple-element.476, s32[]{:T(128)S(6)} %copy.185, ...), kind=kOutput, calls=%fused_computation.25.clone.1 | convolution fusion | flops 553644032 | bytes 35685376 | tf_op jit(solution)/shard_map/while/body/eval_jaxpr/qhd,khd->hqk/dot_general | solution.py:501
  522.0 8.0 multiply_convert_fusion.5
  538.5 18.7 %dynamic_update_slice.33 = f32[2,1024,4,64]{1,0,3,2:T(2,128)} dynamic-update-slice(f32[2,1024,4,64]{1,0,3,2:T(2,128)} %get-tuple-element.457, f32[1,1024,4,64]{1,0,3,2:T(1,128)S(1)} %copy.163, s32[]{:T(128)S(6)} %copy.185, s32[]{:T(128)} %constant.86.clone.1..sunk, s32[]{:T(128)} %constant.86.clone.1..sunk, s32[]{:T(128)} %constant.86.clone.1..sunk) | dynamic-update-slice | bytes 2097156 | tf_op jit(solution)/shard_map/while/body/jit(dynamic_update_index_in_dim)/dynamic_update_slice | solution.py:511
  557.2 18.6 %dynamic_update_slice.32 = f32[2,1024,4,64]{1,0,3,2:T(2,128)} dynamic-update-slice(f32[2,1024,4,64]{1,0,3,2:T(2,128)} %get-tuple-element.456, f32[1,1024,4,64]{1,0,3,2:T(1,128)S(1)} %copy.162, s32[]{:T(128)S(6)} %copy.185, s32[]{:T(128)} %constant.86.clone.1..sunk, s32[]{:T(128)} %constant.86.clone.1..sunk, s32[]{:T(128)} %constant.86.clone.1..sunk) | dynamic-update-slice | bytes 2097156 | tf_op jit(solution)/shard_map/while/body/jit(dynamic_update_index_in_dim)/dynamic_update_slice | solution.py:511
  586.3 18.8 %convert_reduce_fusion.1 = (f32[3,4,64]{2,1,0:T(4,128)}, bf16[2,1024,3,4,64]{1,0,4,3,2:T(2,128)(2,1)S(1)}) fusion(bf16[2,1024,1,4,64]{1,0,4,3,2:T(2,128)(2,1)S(1)} %bitcast.225, bf16[2,1024,1,4,64]{1,0,4,3,2:T(2,128)(2,1)S(1)} %get-tuple-element.306, bf16[2,1024,1,4,64]{1,0,4,3,2:T(2,128)(2,1)S(1)} %get-tuple-element.305), kind=kLoop, calls=%fused_computation.74 | loop fusion | flops 6290688 | bytes 6294528 | tf_op jit(solution)/shard_map/reduce_sum | solution.py:565
  606.3 13.9 %fusion.70 = f32[2048,1024]{1,0:T(8,128)} fusion(bf16[2048,2048]{0,1:T(8,128)(2,1)S(1)} %bitcast.240, bf16[512,1024]{1,0:T(8,128)(2,1)} %collective-permute-done.8, bf16[512,1024]{1,0:T(8,128)(2,1)} %collective-permute-done.7, bf16[512,1024]{1,0:T(8,128)(2,1)} %collective-permute-done.6, bf16[512,1024]{1,0:T(8,128)(2,1)} %bitcast.14), kind=kOutput, calls=%fused_computation.148 | convolution fusion | flops 8606711808 | bytes 20971520 | tf_op jit(solution)/shard_map/dot_general | solution.py:375
  620.2 23.2 %convert_reduce_fusion = (f32[1024]{0:T(1024)}, bf16[2048,1024]{1,0:T(8,128)(2,1)S(1)}) fusion(bf16[2048,2048]{1,0:T(8,128)(2,1)} %all-gather.6.cloned.1.call-done, bf16[256,2048]{1,0:T(8,128)(2,1)S(1)} %copy-done.23, bf16[256,2048]{1,0:T(8,128)(2,1)S(1)} %copy-done.22, bf16[256,2048]{1,0:T(8,128)(2,1)S(1)} %copy-done.21, ...), kind=kOutput, calls=%fused_computation.71 | convolution fusion | flops 8663333888 | bytes 25174016 | tf_op jit(solution)/shard_map/dot_general | solution.py:375
  643.4 16.1 %fusion.69 = f32[2048,2048]{1,0:T(8,128)} fusion(bf16[2048,1024]{1,0:T(8,128)(2,1)S(1)} %get-tuple-element.304, bf16[512,1024]{1,0:T(8,128)(2,1)} %collective-permute-done.8, bf16[512,1024]{1,0:T(8,128)(2,1)} %collective-permute-done.7, bf16[512,1024]{1,0:T(8,128)(2,1)} %collective-permute-done.6, bf16[512,1024]{1,0:T(8,128)(2,1)} %bitcast.14), kind=kOutput, calls=%fused_computation.147 | convolution fusion | flops 8606711808 | bytes 25165824 | tf_op jit(solution)/shard_map/dot_general | solution.py:375
  659.5 13.2 %add_convert_fusion = bf16[2048,2048]{1,0:T(8,128)(2,1)} fusion(f32[2048,2048]{1,0:T(8,128)} %fusion.69, bf16[2048,768]{0,1:T(8,128)(2,1)S(1)} %bitcast.223, bf16[512,768]{1,0:T(8,128)(2,1)} %collective-permute-done.2, bf16[512,768]{1,0:T(8,128)(2,1)} %collective-permute-done.1, bf16[512,768]{1,0:T(8,128)(2,1)} %collective-permute-done, ...), kind=kOutput, calls=%fused_computation.59 | convolution fusion | flops 6463422464 | bytes 31457280 | tf_op jit(solution)/shard_map/dot_general | solution.py:375
  675.3 16.8 %fusion.68 = f32[2048,2048]{1,0:T(8,128)} fusion(bf16[256,2048]{1,0:T(8,128)(2,1)} %get-tuple-element.273, bf16[256,2048]{1,0:T(8,128)(2,1)} %get-tuple-element.272, bf16[256,2048]{1,0:T(8,128)(2,1)S(1)} %copy-done.21, bf16[256,2048]{1,0:T(8,128)(2,1)S(1)} %copy-done.20, f32[2048,1024]{1,0:T(8,128)} %fusion.70, f32[1024]{0:T(1024)S(1)} %bitcast.235), kind=kOutput, calls=%fused_computation.146 | convolution fusion | flops 8627683328 | bytes 29364224 | tf_op jit(solution)/shard_map/dot_general | solution.py:375
  692.2 9.8 add_convert_fusion.1
  704.2 10.4 convolution_convert_fusion.2
  716.8 11.3 %convolution_convert_fusion.1 = bf16[2048,1024]{1,0:T(8,128)(2,1)S(1)} fusion(bf16[2048,2048]{0,1:T(8,128)(2,1)} %all-gather.4.cloned.1.call-done, bf16[2048,1024]{1,0:T(8,128)(2,1)S(1)} %copy-done.52), kind=kOutput, calls=%fused_computation.78 | convolution fusion | flops 8592031744 | bytes 16777216 | tf_op jit(solution)/shard_map/dot_general | solution.py:375
  731.4 17.1 %convolution_convert_fusion = bf16[1024,2048]{1,0:T(8,128)(2,1)S(1)} fusion(bf16[2048,2048]{1,0:T(8,128)(2,1)} %all-gather.6.cloned.1.call-done, f32[2048,1024]{1,0:T(8,128)} %fusion.70, f32[1024]{0:T(1024)S(1)} %bitcast.236), kind=kOutput, calls=%fused_computation.77 | convolution fusion | flops 8613003264 | bytes 20975616 | tf_op jit(solution)/shard_map/dot_general | solution.py:375
  754.0 43.1 %collective-permute-done.19 = bf16[512,1024]{1,0:T(8,128)(2,1)S(1)} collective-permute-done((bf16[512,1024]{1,0:T(8,128)(2,1)S(1)}, bf16[512,1024]{1,0:T(8,128)(2,1)S(1)}, u32[]{:S(2)}, u32[]{:S(2)}) %collective-permute-start.19) | collective-permute-done | bytes 1048608 | tf_op jit(solution)/shard_map/ppermute | solution.py:339
  799.6 5.1 all-to-all-start.2
  804.7 6.0 convolution_convert_fusion.3
  820.8 26.2 %collective-permute-done.20 = bf16[512,1024]{1,0:T(8,128)(2,1)} collective-permute-done((bf16[512,1024]{1,0:T(8,128)(2,1)}, bf16[512,1024]{1,0:T(8,128)(2,1)}, u32[]{:S(2)}, u32[]{:S(2)}) %collective-permute-start.20) | collective-permute-done | bytes 1048608 | tf_op jit(solution)/shard_map/ppermute | solution.py:339
  857.4 37.3 %collective-permute-done.17 = bf16[64,2048]{1,0:T(8,128)(2,1)} collective-permute-done((bf16[64,2048]{1,0:T(8,128)(2,1)S(1)}, bf16[64,2048]{1,0:T(8,128)(2,1)}, u32[]{:S(2)}, u32[]{:S(2)}) %collective-permute-start.17) | collective-permute-done | bytes 262176 | tf_op jit(solution)/shard_map/ppermute | solution.py:339
  940.7 111.4 %all-reduce.5.cloned.1.call-done = f32[32,640]{1,0:T(8,128)} async-done(((f32[32,640]{1,0:T(8,128)}), f32[32,640]{1,0:T(8,128)}) %all-reduce.5.cloned.1.call-update) | async-done | bytes 81936
  (314 shorter events, 211.8 us)
Async XLA Ops:
  7.2 241.6 %all-gather.4.cloned.1.call-start = ((), (), s32[]{:S(2)}) async-start(), calls=%async_computation.6 | async-start | bytes 9437184 | tf_op jit(solution)/shard_map/all_gather | solution.py:446
  10.2 55.6 %copy-start.3 = (f32[1,256,2048]{1,2,0:T(8,128)}, f32[1,256,2048]{1,2,0:T(8,128)S(1)}, u32[]{:S(2)}) copy-start(f32[1,256,2048]{1,2,0:T(8,128)S(1)} %copy.101) | copy-start | bytes 6291460
  10.2 53.7 %copy-start.8 = (bf16[1,256,2048]{2,1,0:T(8,128)(2,1)S(1)}, bf16[1,256,2048]{2,1,0:T(8,128)(2,1)}, u32[]{:S(2)}) copy-start(bf16[1,256,2048]{2,1,0:T(8,128)(2,1)} %param.29) | copy-start | bytes 3145732
  10.2 58.1 %copy-start.40 = (f32[256]{0:T(256)}, f32[256]{0:T(256)S(1)}, u32[]{:S(2)}) copy-start(f32[256]{0:T(256)S(1)} %broadcast_multiply_fusion.5) | copy-start | bytes 3076
  12.7 55.7 %copy-start.43 = (f32[256]{0:T(256)}, f32[256]{0:T(256)S(1)}, u32[]{:S(2)}) copy-start(f32[256]{0:T(256)S(1)} %add_rsqrt_fusion) | copy-start | bytes 3076
  63.2 221.4 %all-gather.6.cloned.1.call-start = ((), (), s32[]{:S(2)}) async-start(), calls=%async_computation.8 | async-start | bytes 9437184 | tf_op jit(solution)/shard_map/all_gather | solution.py:449
  69.6 36.0 %copy-start.50 = (u32[32]{0:T(128)S(1)}, u32[32]{0:T(128)}, u32[]{:S(2)}) copy-start(u32[32]{0:T(128)} %constant.115) | copy-start | bytes 388
  71.3 22.6 %all-to-all-start = ((bf16[8,64,768]{2,1,0:T(8,128)(2,1)}), bf16[8,64,768]{2,1,0:T(8,128)(2,1)}, u32[]{:S(2)}, u32[]{:S(2)}) async-start(bf16[8,64,768]{2,1,0:T(8,128)(2,1)} %reshape.478), calls=%async_computation | async-start | bytes 1572864 | tf_op jit(solution)/shard_map/all_to_all | solution.py:415
  93.9 105.9 %all-to-all-start.1 = ((bf16[8,64,1024]{2,1,0:T(8,128)(2,1)}), bf16[8,64,1024]{2,1,0:T(8,128)(2,1)}, u32[]{:S(2)}, u32[]{:S(2)}) async-start(bf16[8,64,1024]{2,1,0:T(8,128)(2,1)} %reshape.484), calls=%async_computation.1 | async-start | bytes 2097152 | tf_op jit(solution)/shard_map/all_to_all | solution.py:415
  98.1 825.0 %reduce-scatter.5.cloned.1.call-start = ((), (), s32[]{:S(2)}) async-start(), calls=%async_computation.9 | async-start | bytes 9437184 | tf_op jit(solution)/shard_map/reduce_scatter | solution.py:531
  98.2 41.9 %collective-permute-start.9 = (bf16[256,2048]{1,0:T(8,128)(2,1)S(1)}, bf16[256,2048]{1,0:T(8,128)(2,1)S(1)}, u32[]{:S(2)}, u32[]{:S(2)}) collective-permute-start(bf16[256,2048]{1,0:T(8,128)(2,1)S(1)} %copy-done.19), channel_id=1, source_target_pairs={{0,16},{16,0},{1,17},{17,1},{2,18},{18,2},{3,19},{19,3},{4,20},{20... | collective-permute-start | bytes 3145736 | tf_op jit(solution)/shard_map/ppermute | solution.py:339
  100.7 100.6 %collective-permute-start.1 = (bf16[512,768]{1,0:T(8,128)(2,1)}, bf16[512,768]{1,0:T(8,128)(2,1)}, u32[]{:S(2)}, u32[]{:S(2)}) collective-permute-start(bf16[512,768]{1,0:T(8,128)(2,1)} %bitcast.7), channel_id=1, source_target_pairs={{0,16},{16,0},{1,17},{17,1},{2,18},{18,2},{3,19},{19,3},{4,20},{20... | collective-permute-start | bytes 2359304 | tf_op jit(solution)/shard_map/ppermute | solution.py:339
  101.2 90.9 %collective-permute-start.3 = (bf16[64,2048]{1,0:T(8,128)(2,1)S(1)}, bf16[64,2048]{1,0:T(8,128)(2,1)S(1)}, u32[]{:S(2)}, u32[]{:S(2)}) collective-permute-start(bf16[64,2048]{1,0:T(8,128)(2,1)S(1)} %copy-done.32), channel_id=1, source_target_pairs={{0,16},{16,0},{1,17},{17,1},{2,18},{18,2},{3,19},{19,3},{4,20},{20... | collective-permute-start | bytes 786440 | tf_op jit(solution)/shard_map/ppermute | solution.py:339
  103.6 94.9 %collective-permute-start.5 = (bf16[64,2048]{1,0:T(8,128)(2,1)S(1)}, bf16[64,2048]{1,0:T(8,128)(2,1)S(1)}, u32[]{:S(2)}, u32[]{:S(2)}) collective-permute-start(bf16[64,2048]{1,0:T(8,128)(2,1)S(1)} %copy-done.32), channel_id=1, source_target_pairs={{0,4},{4,0},{1,5},{5,1},{2,6},{6,2},{3,7},{7,3},{8,12},{12,8},{9,1... | collective-permute-start | bytes 786440 | tf_op jit(solution)/shard_map/ppermute | solution.py:339
  105.1 99.0 %collective-permute-start.11 = (bf16[256,2048]{1,0:T(8,128)(2,1)S(1)}, bf16[256,2048]{1,0:T(8,128)(2,1)}, u32[]{:S(2)}, u32[]{:S(2)}) collective-permute-start(bf16[256,2048]{1,0:T(8,128)(2,1)S(1)} %copy-done.19), channel_id=1, source_target_pairs={{0,4},{4,0},{1,5},{5,1},{2,6},{6,2},{3,7},{7,3},{8,12},{12,8},{9,1... | collective-permute-start | bytes 3145736 | tf_op jit(solution)/shard_map/ppermute | solution.py:339
  140.1 64.6 %collective-permute-start.10 = (bf16[256,2048]{1,0:T(8,128)(2,1)S(1)}, bf16[256,2048]{1,0:T(8,128)(2,1)}, u32[]{:S(2)}, u32[]{:S(2)}) collective-permute-start(bf16[256,2048]{1,0:T(8,128)(2,1)S(1)} %collective-permute-done.9), channel_id=1, source_target_pairs={{0,4},{4,0},{1,5},{5,1},{2,6},{6,2},{3,7},{7,3},{8,12},{12,8},{9,1... | collective-permute-start | bytes 3145736 | tf_op jit(solution)/shard_map/ppermute | solution.py:339
  192.1 7.7 collective-permute-start.4
  198.5 103.2 %copy-start.28 = (f32[1024,16]{0,1:T(8,128)}, f32[1024,16]{0,1:T(8,128)S(1)}, u32[]{:S(2)}) copy-start(f32[1024,16]{0,1:T(8,128)S(1)} %get-tuple-element.301) | copy-start | bytes 196612
  198.5 103.2 %copy-start.29 = (f32[1024,16]{0,1:T(8,128)}, f32[1024,16]{0,1:T(8,128)S(1)}, u32[]{:S(2)}) copy-start(f32[1024,16]{0,1:T(8,128)S(1)} %get-tuple-element.302) | copy-start | bytes 196612
  198.5 50.2 %collective-permute-start = (bf16[512,768]{1,0:T(8,128)(2,1)}, bf16[512,768]{1,0:T(8,128)(2,1)}, u32[]{:S(2)}, u32[]{:S(2)}) collective-permute-start(bf16[512,768]{1,0:T(8,128)(2,1)} %bitcast.7), channel_id=1, source_target_pairs={{0,4},{4,0},{1,5},{5,1},{2,6},{6,2},{3,7},{7,3},{8,12},{12,8},{9,1... | collective-permute-start | bytes 2359304 | tf_op jit(solution)/shard_map/ppermute | solution.py:339
  199.8 47.5 %collective-permute-start.7 = (bf16[512,1024]{1,0:T(8,128)(2,1)}, bf16[512,1024]{1,0:T(8,128)(2,1)}, u32[]{:S(2)}, u32[]{:S(2)}) collective-permute-start(bf16[512,1024]{1,0:T(8,128)(2,1)} %bitcast.14), channel_id=1, source_target_pairs={{0,16},{16,0},{1,17},{17,1},{2,18},{18,2},{3,19},{19,3},{4,20},{20... | collective-permute-start | bytes 3145736 | tf_op jit(solution)/shard_map/ppermute | solution.py:339
  201.3 47.5 %collective-permute-start.2 = (bf16[512,768]{1,0:T(8,128)(2,1)}, bf16[512,768]{1,0:T(8,128)(2,1)}, u32[]{:S(2)}, u32[]{:S(2)}) collective-permute-start(bf16[512,768]{1,0:T(8,128)(2,1)} %collective-permute-done.1), channel_id=1, source_target_pairs={{0,4},{4,0},{1,5},{5,1},{2,6},{6,2},{3,7},{7,3},{8,12},{12,8},{9,1... | collective-permute-start | bytes 2359304 | tf_op jit(solution)/shard_map/ppermute | solution.py:339
  204.0 80.6 %copy-start.11 = (bf16[64,2048]{1,0:T(8,128)(2,1)}, bf16[64,2048]{1,0:T(8,128)(2,1)S(1)}, u32[]{:S(2)}) copy-start(bf16[64,2048]{1,0:T(8,128)(2,1)S(1)} %get-tuple-element.286) | copy-start | bytes 786436
  204.0 80.6 %copy-start.13 = (bf16[64,2048]{1,0:T(8,128)(2,1)}, bf16[64,2048]{1,0:T(8,128)(2,1)S(1)}, u32[]{:S(2)}) copy-start(bf16[64,2048]{1,0:T(8,128)(2,1)S(1)} %get-tuple-element.287) | copy-start | bytes 786436
  204.1 80.6 %copy-start.15 = (bf16[64,2048]{1,0:T(8,128)(2,1)}, bf16[64,2048]{1,0:T(8,128)(2,1)S(1)}, u32[]{:S(2)}) copy-start(bf16[64,2048]{1,0:T(8,128)(2,1)S(1)} %get-tuple-element.288) | copy-start | bytes 786436
  204.1 80.6 %copy-start.17 = (bf16[64,2048]{1,0:T(8,128)(2,1)}, bf16[64,2048]{1,0:T(8,128)(2,1)S(1)}, u32[]{:S(2)}) copy-start(bf16[64,2048]{1,0:T(8,128)(2,1)S(1)} %get-tuple-element.289) | copy-start | bytes 786436
  204.1 402.1 %collective-permute-start.6 = (bf16[512,1024]{1,0:T(8,128)(2,1)}, bf16[512,1024]{1,0:T(8,128)(2,1)}, u32[]{:S(2)}, u32[]{:S(2)}) collective-permute-start(bf16[512,1024]{1,0:T(8,128)(2,1)} %bitcast.14), channel_id=1, source_target_pairs={{0,4},{4,0},{1,5},{5,1},{2,6},{6,2},{3,7},{7,3},{8,12},{12,8},{9,1... | collective-permute-start | bytes 3145736 | tf_op jit(solution)/shard_map/ppermute | solution.py:339
  247.3 358.9 %collective-permute-start.8 = (bf16[512,1024]{1,0:T(8,128)(2,1)}, bf16[512,1024]{1,0:T(8,128)(2,1)}, u32[]{:S(2)}, u32[]{:S(2)}) collective-permute-start(bf16[512,1024]{1,0:T(8,128)(2,1)} %collective-permute-done.7), channel_id=1, source_target_pairs={{0,4},{4,0},{1,5},{5,1},{2,6},{6,2},{3,7},{7,3},{8,12},{12,8},{9,1... | collective-permute-start | bytes 3145736 | tf_op jit(solution)/shard_map/ppermute | solution.py:339
  606.1 53.4 %copy-start.10 = (bf16[96,8,2,1024]{3,1,2,0:T(8,128)(2,1)}, bf16[96,8,2,1024]{3,1,2,0:T(8,128)(2,1)S(1)}, u32[]{:S(2)}) copy-start(bf16[96,8,2,1024]{3,1,2,0:T(8,128)(2,1)S(1)} %copy.150) | copy-start | bytes 9437188
  672.7 265.4 %reduce-scatter.3.cloned.1.call-start = ((), (), s32[]{:S(2)}) async-start(), calls=%async_computation.7 | async-start | bytes 9437184 | tf_op jit(solution)/shard_map/reduce_scatter | solution.py:487
  714.7 83.7 %collective-permute-start.12 = (bf16[512,768]{1,0:T(8,128)(2,1)S(1)}, bf16[512,768]{1,0:T(8,128)(2,1)S(1)}, u32[]{:S(2)}, u32[]{:S(2)}) collective-permute-start(bf16[512,768]{1,0:T(8,128)(2,1)S(1)} %get-tuple-element.274), channel_id=1, source_target_pairs={{0,4},{4,0},{1,5},{5,1},{2,6},{6,2},{3,7},{7,3},{8,12},{12,8},{9,1... | collective-permute-start | bytes 2359304 | tf_op jit(solution)/shard_map/ppermute | solution.py:339
  714.8 37.3 %collective-permute-start.13 = (bf16[512,768]{1,0:T(8,128)(2,1)S(1)}, bf16[512,768]{1,0:T(8,128)(2,1)S(1)}, u32[]{:S(2)}, u32[]{:S(2)}) collective-permute-start(bf16[512,768]{1,0:T(8,128)(2,1)S(1)} %get-tuple-element.275), channel_id=1, source_target_pairs={{0,4},{4,0},{1,5},{5,1},{2,6},{6,2},{3,7},{7,3},{8,12},{12,8},{9,1... | collective-permute-start | bytes 2359304 | tf_op jit(solution)/shard_map/ppermute | solution.py:339
  728.1 69.0 %copy-start.7 = (bf16[2048,1024]{1,0:T(8,128)(2,1)}, bf16[2048,1024]{1,0:T(8,128)(2,1)S(1)}, u32[]{:S(2)}) copy-start(bf16[2048,1024]{1,0:T(8,128)(2,1)S(1)} %convolution_convert_fusion.1) | copy-start | bytes 12582916
  729.3 91.5 %collective-permute-start.18 = (bf16[512,1024]{1,0:T(8,128)(2,1)}, bf16[512,1024]{1,0:T(8,128)(2,1)}, u32[]{:S(2)}, u32[]{:S(2)}) collective-permute-start(bf16[512,1024]{1,0:T(8,128)(2,1)} %get-tuple-element.268), channel_id=1, source_target_pairs={{0,4},{4,0},{1,5},{5,1},{2,6},{6,2},{3,7},{7,3},{8,12},{12,8},{9,1... | collective-permute-start | bytes 3145736 | tf_op jit(solution)/shard_map/ppermute | solution.py:339
  729.4 67.6 %collective-permute-start.19 = (bf16[512,1024]{1,0:T(8,128)(2,1)S(1)}, bf16[512,1024]{1,0:T(8,128)(2,1)S(1)}, u32[]{:S(2)}, u32[]{:S(2)}) collective-permute-start(bf16[512,1024]{1,0:T(8,128)(2,1)S(1)} %get-tuple-element.269), channel_id=1, source_target_pairs={{0,4},{4,0},{1,5},{5,1},{2,6},{6,2},{3,7},{7,3},{8,12},{12,8},{9,1... | collective-permute-start | bytes 3145736 | tf_op jit(solution)/shard_map/ppermute | solution.py:339
  752.3 46.1 %collective-permute-start.14 = (bf16[512,768]{1,0:T(8,128)(2,1)S(1)}, bf16[512,768]{1,0:T(8,128)(2,1)S(1)}, u32[]{:S(2)}, u32[]{:S(2)}) collective-permute-start(bf16[512,768]{1,0:T(8,128)(2,1)S(1)} %add_convert_fusion.8), channel_id=1, source_target_pairs={{0,16},{16,0},{1,17},{17,1},{2,18},{18,2},{3,19},{19,3},{4,20},{20... | collective-permute-start | bytes 2359304 | tf_op jit(solution)/shard_map/ppermute | solution.py:339
  754.0 62.4 %collective-permute-start.22 = (bf16[256,2048]{1,0:T(8,128)(2,1)}, bf16[256,2048]{1,0:T(8,128)(2,1)}, u32[]{:S(2)}, u32[]{:S(2)}) collective-permute-start(bf16[256,2048]{1,0:T(8,128)(2,1)} %get-tuple-element.267), channel_id=1, source_target_pairs={{0,4},{4,0},{1,5},{5,1},{2,6},{6,2},{3,7},{7,3},{8,12},{12,8},{9,1... | collective-permute-start | bytes 3145736 | tf_op jit(solution)/shard_map/ppermute | solution.py:339
  798.4 48.6 %collective-permute-start.20 = (bf16[512,1024]{1,0:T(8,128)(2,1)}, bf16[512,1024]{1,0:T(8,128)(2,1)}, u32[]{:S(2)}, u32[]{:S(2)}) collective-permute-start(bf16[512,1024]{1,0:T(8,128)(2,1)} %add_convert_fusion.4), channel_id=1, source_target_pairs={{0,16},{16,0},{1,17},{17,1},{2,18},{18,2},{3,19},{19,3},{4,20},{20... | collective-permute-start | bytes 3145736 | tf_op jit(solution)/shard_map/ppermute | solution.py:339
  799.6 50.8 %all-to-all-start.2 = ((bf16[8,64,768]{2,1,0:T(8,128)(2,1)}), bf16[8,64,768]{2,1,0:T(8,128)(2,1)S(1)}, u32[]{:S(2)}, u32[]{:S(2)}) async-start(bf16[8,64,768]{2,1,0:T(8,128)(2,1)} %bitcast.31), calls=%async_computation.4 | async-start | bytes 1572864 | tf_op jit(solution)/shard_map/all_to_all | solution.py:554
  810.8 46.7 %collective-permute-start.15 = (bf16[64,2048]{1,0:T(8,128)(2,1)S(1)}, bf16[64,2048]{1,0:T(8,128)(2,1)}, u32[]{:S(2)}, u32[]{:S(2)}) collective-permute-start(bf16[64,2048]{1,0:T(8,128)(2,1)S(1)} %get-tuple-element.284), channel_id=1, source_target_pairs={{0,4},{4,0},{1,5},{5,1},{2,6},{6,2},{3,7},{7,3},{8,12},{12,8},{9,1... | collective-permute-start | bytes 786440 | tf_op jit(solution)/shard_map/ppermute | solution.py:339
  811.4 43.6 %collective-permute-start.16 = (bf16[64,2048]{1,0:T(8,128)(2,1)S(1)}, bf16[64,2048]{1,0:T(8,128)(2,1)}, u32[]{:S(2)}, u32[]{:S(2)}) collective-permute-start(bf16[64,2048]{1,0:T(8,128)(2,1)S(1)} %get-tuple-element.285), channel_id=1, source_target_pairs={{0,4},{4,0},{1,5},{5,1},{2,6},{6,2},{3,7},{7,3},{8,12},{12,8},{9,1... | collective-permute-start | bytes 786440 | tf_op jit(solution)/shard_map/ppermute | solution.py:339
  816.3 40.1 %copy-start.42 = (f32[3,4,64]{2,1,0:T(4,128)S(1)}, f32[3,4,64]{2,1,0:T(4,128)}, u32[]{:S(2)}) copy-start(f32[3,4,64]{2,1,0:T(4,128)} %get-tuple-element.258) | copy-start | bytes 9220
  816.3 40.3 %copy-start.46 = (f32[1024]{0:T(1024)S(1)}, f32[1024]{0:T(1024)}, u32[]{:S(2)}) copy-start(f32[1024]{0:T(1024)} %get-tuple-element.303) | copy-start | bytes 12292
  816.3 80.5 %collective-permute-start.21 = (bf16[256,2048]{1,0:T(8,128)(2,1)}, bf16[256,2048]{1,0:T(8,128)(2,1)S(1)}, u32[]{:S(2)}, u32[]{:S(2)}) collective-permute-start(bf16[256,2048]{1,0:T(8,128)(2,1)} %get-tuple-element.266), channel_id=1, source_target_pairs={{0,4},{4,0},{1,5},{5,1},{2,6},{6,2},{3,7},{7,3},{8,12},{12,8},{9,1... | collective-permute-start | bytes 3145736 | tf_op jit(solution)/shard_map/ppermute | solution.py:339
  820.8 76.0 %collective-permute-start.23 = (bf16[256,2048]{1,0:T(8,128)(2,1)}, bf16[256,2048]{1,0:T(8,128)(2,1)}, u32[]{:S(2)}, u32[]{:S(2)}) collective-permute-start(bf16[256,2048]{1,0:T(8,128)(2,1)} %add_convert_fusion.2), channel_id=1, source_target_pairs={{0,16},{16,0},{1,17},{17,1},{2,18},{18,2},{3,19},{19,3},{4,20},{20... | collective-permute-start | bytes 3145736 | tf_op jit(solution)/shard_map/ppermute | solution.py:339
  850.5 62.7 %all-to-all-start.3 = ((bf16[8,64,1024]{2,1,0:T(8,128)(2,1)}), bf16[8,64,1024]{2,1,0:T(8,128)(2,1)}, u32[]{:S(2)}, u32[]{:S(2)}) async-start(bf16[8,64,1024]{2,1,0:T(8,128)(2,1)} %bitcast.35), calls=%async_computation.5 | async-start | bytes 2097152 | tf_op jit(solution)/shard_map/all_to_all | solution.py:554
  854.7 197.4 %all-reduce.5.cloned.1.call-start = ((), (), s32[]{:S(2)}) async-start(), calls=%async_computation.10 | async-start | bytes 163840
  856.1 38.6 %collective-permute-start.17 = (bf16[64,2048]{1,0:T(8,128)(2,1)S(1)}, bf16[64,2048]{1,0:T(8,128)(2,1)}, u32[]{:S(2)}, u32[]{:S(2)}) collective-permute-start(bf16[64,2048]{1,0:T(8,128)(2,1)S(1)} %add_convert_fusion.9), channel_id=1, source_target_pairs={{0,16},{16,0},{1,17},{17,1},{2,18},{18,2},{3,19},{19,3},{4,20},{20... | collective-permute-start | bytes 786440 | tf_op jit(solution)/shard_map/ppermute | solution.py:339
  (42 other events, 422.5 us)
Sparse Core Ops, SparseCore 0:
  63.3 104.4 all-gather.3
  169.4 80.6 all-gather.5
  672.9 83.9 reduce-scatter.4
  759.0 128.5 reduce-scatter.2
  934.5 117.5 all-reduce.4

commit v2 on v1

--- a/solution.py
+++ b/solution.py
@@ -1,9 +1,12 @@
+import functools
 import math
 
 import jax
 import jax.numpy as jnp
 import numpy as np
 from jax import lax
+from jax.experimental import pallas as pl
+from jax.experimental.pallas import tpu as pltpu
 from jax.sharding import PartitionSpec as P
 
 HEAD_DIM = 64
@@ -339,10 +342,6 @@
     return lax.ppermute(values, axis, [(0, 1), (1, 0)])
 
 
-def flip_if(values, dim, flag):
-    return jnp.where(flag, jnp.flip(values, dim), values)
-
-
 def gather_blocks(own):
     across = swap(own, "zh")
     beside = swap(own, "y")
@@ -371,8 +370,234 @@
     )
 
 
+def natural_rows(blocks):
+    halves = [jnp.split(block, 2, axis=0) for block in blocks]
+    return jnp.concatenate(
+        [halves[2 * zh + y][zl] for zh in range(2) for zl in range(2) for y in range(2)], axis=0
+    )
+
+
+def blocks_of_rows(values):
+    parts = jnp.split(values, 8, axis=0)
+    return [
+        jnp.concatenate([parts[4 * zh + 2 * zl + y] for zl in range(2)], axis=0)
+        for zh in range(2)
+        for y in range(2)
+    ]
+
+
 def dot(left, right, dims):
     return lax.dot_general(left, right, (dims, ((), ())), preferred_element_type=jnp.float32)
+
+
+QB = 256
+
+
+def nt(a, b):
+    return dot(a, b, ((1,), (1,)))
+
+
+def nn(a, b):
+    return dot(a, b, ((1,), (0,)))
+
+
+def tn(a, b):
+    return dot(a, b, ((0,), (0,)))
+
+
+def attention_kernel(len_ref, bias_ref, cos_ref, sin_ref, q_in, k_in, v_in, go_in, mixed_ref, grad_ref, sum_ref,
+                     q_s, k_s, v_s, g_s, gk_s, gv_s, *, total, pairs):
+    f32, bf16 = jnp.float32, jnp.bfloat16
+    pair = pl.program_id(1)
+    lane = lax.broadcasted_iota(jnp.int32, (1, 128), 1)
+    in_head = lane % 64
+    first = in_head < 16
+    heads = [(lane < 64), (lane >= 64)]
+    length = len_ref[pl.program_id(0)]
+
+    def other(v):
+        return jnp.where(first, pltpu.roll(v, 112, 1), pltpu.roll(v, 16, 1))
+    def col(part):
+        return pl.multiple_of(part * (pairs * 128) + pair * 128, 128)
+    cosines, sines = cos_ref[...], sin_ref[...]
+    def turn(v): return v * cosines + other(v) * sines
+    def turn_back(v): return v * cosines - other(v) * sines
+    q = turn(q_in[...] + bias_ref[:, pl.ds(col(0), 128)]) * 0.125
+    k = turn(k_in[...] + bias_ref[:, pl.ds(col(1), 128)])
+    v = v_in[...] + bias_ref[:, pl.ds(col(2), 128)]
+    g = go_in[...]
+    for h in range(2):
+        q_s[h] = jnp.where(heads[h], q, 0.0).astype(bf16)
+        k_s[h] = jnp.where(heads[h], k, 0.0).astype(bf16)
+        v_s[h] = jnp.where(heads[h], v, 0.0).astype(bf16)
+        g_s[h] = jnp.where(heads[h], g, 0.0).astype(bf16)
+    gk_s[...] = jnp.zeros_like(gk_s)
+    gv_s[...] = jnp.zeros_like(gv_s)
+    gq_sum = jnp.zeros((1, 128), f32)
+    for b in range(total // QB):
+        rows = pl.ds(b * QB, QB)
+        upto = (b + 1) * QB
+        keys = pl.ds(0, upto)
+        limit = jnp.minimum(lax.broadcasted_iota(jnp.int32, (1, QB), 1) + (b * QB + 1), length)
+        allowed = lax.broadcasted_iota(jnp.int32, (upto, QB), 0) < limit
+        mixed = None
+        for h in range(2):
+            qh, gh = q_s[h, rows], g_s[h, rows]
+            s = nt(k_s[h, keys], qh)
+            s = jnp.where(allowed, s, -1e30)
+            m = jnp.max(s, axis=0, keepdims=True)
+            e = jnp.exp(s - m)
+            p = e * (1.0 / jnp.sum(e, axis=0, keepdims=True))
+            pr = p.astype(bf16)
+            gp = nt(v_s[h, keys], gh)
+            inner = jnp.sum(p * gp, axis=0, keepdims=True)
+            gs = (p * (gp - inner)).astype(bf16)
+            gv_s[keys] += nn(pr, gh)
+            gk_s[keys] += nn(gs, qh)
+            o = tn(pr, v_s[h, keys])
+            gq = tn(gs, k_s[h, keys])
+            mixed = o if mixed is None else mixed + o
+            gq_all = gq if h == 0 else gq_all + gq
+        mixed_ref[rows, :] = mixed
+        cs, sn = cos_ref[rows], sin_ref[rows]
+        gq_all = gq_all * 0.125
+        back = (gq_all * cs - other(gq_all) * sn).astype(bf16)
+        grad_ref[rows, pl.ds(col(0), 128)] = back.astype(f32)
+        gq_sum += jnp.sum(back.astype(f32), axis=0, keepdims=True)
+    gk = turn_back(gk_s[...]).astype(bf16)
+    gv = gv_s[...].astype(bf16)
+    grad_ref[:, pl.ds(col(1), 128)] = gk.astype(f32)
+    grad_ref[:, pl.ds(col(2), 128)] = gv.astype(f32)
+    sum_ref[0, :, pl.ds(col(0), 128)] = gq_sum
+    sum_ref[0, :, pl.ds(col(1), 128)] = jnp.sum(gk.astype(f32), axis=0, keepdims=True)
+    sum_ref[0, :, pl.ds(col(2), 128)] = jnp.sum(gv.astype(f32), axis=0, keepdims=True)
+
+def attention(lengths, qkv, bias, grad_mixed, cosines, sines):
+    seqs = lengths.shape[0]
+    total = qkv.shape[0] // seqs
+    width = qkv.shape[1] // 3
+    pairs = width // 128
+    blk = lambda part: pl.BlockSpec((total, 128), lambda s, p: (s, part * pairs + p))
+    whole = lambda shape: pl.BlockSpec(shape, lambda s, p: (0,) * len(shape))
+    f32, bf16 = jnp.float32, jnp.bfloat16
+    return pl.pallas_call(
+        functools.partial(attention_kernel, total=total, pairs=pairs),
+        grid=(seqs, pairs),
+        in_specs=[
+            pl.BlockSpec(memory_space=pltpu.SMEM),
+            whole((1, 3 * width)), whole((total, 128)), whole((total, 128)),
+            blk(0), blk(1), blk(2),
+            pl.BlockSpec((total, 128), lambda s, p: (s, p)),
+        ],
+        out_specs=[
+            pl.BlockSpec((total, 128), lambda s, p: (s, p)),
+            pl.BlockSpec((total, 3 * width), lambda s, p: (s, 0)),
+            pl.BlockSpec((1, 1, 3 * width), lambda s, p: (s, 0, 0)),
+        ],
+        out_shape=[
+            jax.ShapeDtypeStruct((seqs * total, width), f32),
+            jax.ShapeDtypeStruct((seqs * total, 3 * width), f32),
+            jax.ShapeDtypeStruct((seqs, 1, 3 * width), f32),
+        ],
+        scratch_shapes=[pltpu.VMEM((2, total, 128), bf16)] * 4 + [pltpu.VMEM((total, 128), f32)] * 2,
+        compiler_params=pltpu.CompilerParams(vmem_limit_bytes=48 * 2**20),
+        cost_estimate=pl.CostEstimate(flops=seqs*pairs*2*6*total*total*64*2, bytes_accessed=20*2**20, transcendentals=seqs*pairs*2*total*total),
+    )(lengths, bias, cosines, sines, qkv, qkv, qkv, grad_mixed)
+
+def tables(total, rot):
+    half = rot // 2
+    inv = jnp.exp(-math.log(10000.0) * 2.0 * jnp.arange(half, dtype=jnp.float32) / rot)
+    ang = jnp.arange(total, dtype=jnp.int32).astype(jnp.float32)[:, None] * inv[None, :]
+    c, s = jnp.cos(ang), jnp.sin(ang)
+    one, nil = jnp.ones((total, 64 - rot), jnp.float32), jnp.zeros((total, 64 - rot), jnp.float32)
+    cosines = jnp.concatenate([c, c, one] * 2, axis=1)
+    sines = jnp.concatenate([-s, s, nil] * 2, axis=1)
+    return cosines, sines
+
+
+MESH_ID = pl.DeviceIdType.MESH
+
+
+def exchange_kernel(src, dst, send_sem, recv_sem, *, spread):
+    place = [lax.axis_index(name) for name in FINE]
+    me = 0
+    for p in place:
+        me = me * 2 + p
+
+    def away(k):
+        return tuple((p + k // 2 ** (4 - i)) % 2 for i, p in enumerate(place))
+
+    def index_of(where):
+        number = 0
+        for p in where:
+            number = number * 2 + p
+        return number
+
+    barrier = pltpu.get_barrier_semaphore()
+
+    def greet(k, carry):
+        pl.semaphore_signal(barrier, inc=1, device_id=away(k), device_id_type=MESH_ID)
+        return carry
+
+    lax.fori_loop(1, 32, greet, 0)
+    pl.semaphore_wait(barrier, 31)
+
+    def copy(k):
+        where = away(k)
+        return pltpu.make_async_remote_copy(
+            src_ref=src.at[index_of(where) if spread else 0],
+            dst_ref=dst.at[me],
+            send_sem=send_sem.at[k],
+            recv_sem=recv_sem.at[k],
+            device_id=where,
+            device_id_type=MESH_ID,
+        )
+
+    def send(k, carry):
+        copy(k).start()
+        return carry
+
+    lax.fori_loop(1, 32, send, 0)
+    dst[me] = src[me if spread else 0]
+
+    def finish(k, carry):
+        copy(k).wait()
+        return carry
+
+    lax.fori_loop(1, 32, finish, 0)
+
+
+def sum_kernel(src, out, dst, send_sem, recv_sem):
+    exchange_kernel(src, dst, send_sem, recv_sem, spread=True)
+    out[...] = jnp.sum(dst[...], axis=0)
+
+
+def gather_small(values):
+    n = values.shape[0]
+    return pl.pallas_call(
+        functools.partial(exchange_kernel, spread=False),
+        out_shape=jax.ShapeDtypeStruct((32, n, 128), jnp.float32),
+        in_specs=[pl.BlockSpec(memory_space=pltpu.VMEM)],
+        out_specs=pl.BlockSpec(memory_space=pltpu.VMEM),
+        scratch_shapes=[pltpu.SemaphoreType.DMA((32,)), pltpu.SemaphoreType.DMA((32,))],
+        compiler_params=pltpu.CompilerParams(collective_id=0, has_side_effects=True),
+    )(values[None])
+
+
+def sum_small(values, collective_id):
+    n = values.shape[1]
+    return pl.pallas_call(
+        sum_kernel,
+        out_shape=jax.ShapeDtypeStruct((n, 128), jnp.float32),
+        in_specs=[pl.BlockSpec(memory_space=pltpu.VMEM)],
+        out_specs=pl.BlockSpec(memory_space=pltpu.VMEM),
+        scratch_shapes=[
+            pltpu.VMEM((32, n, 128), jnp.float32),
+            pltpu.SemaphoreType.DMA((32,)),
+            pltpu.SemaphoreType.DMA((32,)),
+        ],
+        compiler_params=pltpu.CompilerParams(collective_id=collective_id, has_side_effects=True),
+    )(values)
 
 
 def split_device(
@@ -401,13 +626,21 @@
     heads = 4
     own_width = heads * HEAD_DIM
 
-    small = jnp.concatenate([ln_gain, ln_bias, b_qkv, b_out, b_fc1, b_fc2])
-    small_all = lax.all_gather(small[None], FINE, axis=0, tiled=True).astype(f32)
-    ends = np.cumsum([rows, rows, 3 * rows, rows, ff_rows, rows])
-    gain_all, shift_all, bqkv_all, bout_all, bfc1_all, bfc2_all = (
-        part.reshape(-1) for part in jnp.split(small_all, ends[:-1], axis=1)
-    )
-    length_pair = lax.all_gather(lengths, "zl", axis=0, tiled=True)
+    small = jnp.concatenate(
+        [v.astype(f32) for v in (ln_gain, ln_bias, b_qkv, b_out, b_fc1, b_fc2, lengths)]
+    )
+    filled = -(-small.shape[0] // 128) * 128
+    small = jnp.pad(small, (0, filled - small.shape[0])).reshape(-1, 128)
+    small_all = gather_small(small).reshape(32, filled)
+    ends = np.cumsum([rows, rows, 3 * rows, rows, ff_rows, rows, 1])
+    gain_all, shift_all, bqkv_all, bout_all, bfc1_all, bfc2_all, lengths_all = (
+        part.reshape(-1) for part in jnp.split(small_all, ends, axis=1)[:-1]
+    )
+    pair_lengths = lax.dynamic_index_in_dim(
+        lengths_all.reshape(2, 2, 2, 4)[:, :, :, 0].transpose(0, 2, 1).reshape(4, 2),
+        zh * 2 + y,
+        keepdims=False,
+    ).astype(jnp.int32)
 
     def own_columns(weight, shape, order):
         spread = weight.reshape((rows,) + shape).transpose(order)
@@ -422,8 +655,8 @@
     fc1_blocks = gather_blocks(fc1_own)
     out_mat = jnp.concatenate(out_blocks, axis=0)
     fc2_mat = jnp.concatenate(fc2_blocks, axis=0)
-    qkv_mat = jnp.concatenate(qkv_blocks, axis=0)
-    fc1_mat = jnp.concatenate(fc1_blocks, axis=0)
+    qkv_mat = natural_rows(by_place(qkv_blocks, zh, y))
+    fc1_mat = natural_rows(by_place(fc1_blocks, zh, y))
 
     inputs = tokens[0].astype(f32)
     average = jnp.mean(inputs, axis=-1, keepdims=True)
@@ -433,17 +666,7 @@
     normed = centered * inv_std
     hidden_own = (normed * gain_all + shift_all).astype(bf16)
 
-    def mixed_order(values):
-        v = values.reshape(-1, 2, 2, 2, 4, rows).transpose(0, 1, 3, 2, 4, 5)
-        v = flip_if(flip_if(v, 1, zh == 1), 2, y == 1)
-        return v.reshape(values.shape)
-
-    def plain_order(values):
-        v = values.reshape(-1, 2, 2, 2, 4, rows)
-        v = flip_if(flip_if(v, 1, zh == 1), 2, y == 1)
-        return v.transpose(0, 1, 3, 2, 4, 5).reshape(values.shape)
-
-    hidden = lax.all_gather(mixed_order(hidden_own), ROWS_AXES, axis=0, tiled=True)
+    hidden = lax.all_gather(hidden_own, ROWS_AXES, axis=0, tiled=True)
     places = (x * 2 + c) * local_len + jnp.arange(local_len, dtype=jnp.int32)
     grad_own = jnp.where((places < lengths[0])[:, None], cotangent[0], jnp.zeros((), bf16))
     grad_out = lax.all_gather(grad_own, ROWS_AXES, axis=0, tiled=True)
@@ -459,27 +682,13 @@
         keepdims=False,
     )
 
-    angles = rotary_angles(jnp.arange(total_len, dtype=jnp.int32), ROT)
-    qkv = dot(hidden, qkv_mat, ((1,), (0,))) + bqkv
-    qkv = qkv.reshape(2, total_len, 3, heads, HEAD_DIM)
-    turn = jax.vmap(lambda v: rotary(v, angles))
-    queries = (turn(qkv[:, :, 0]) * 0.125).astype(bf16)
-    key_rows = turn(qkv[:, :, 1]).astype(bf16)
-    values = qkv[:, :, 2].astype(bf16)
-    all_places = jnp.arange(total_len, dtype=jnp.int32)
-
-    def attend_forward(packed):
-        query_seq, key_seq, value_seq, length = packed
-        scores = masked_scores(query_seq, key_seq, all_places, length)
-        row_max = jnp.max(scores, axis=-1, keepdims=True)
-        exponent = jnp.exp(scores - row_max)
-        row_sum = jnp.sum(exponent, axis=-1, keepdims=True)
-        probability = (exponent / row_sum).astype(bf16)
-        attended = jnp.einsum("hqk,khd->qhd", probability, value_seq, preferred_element_type=f32)
-        return attended.astype(bf16), (row_max + jnp.log(row_sum))[..., 0]
-
-    attended, log_totals = lax.map(attend_forward, (queries, key_rows, values, length_pair))
-    attn_mixed = attended.reshape(2 * total_len, own_width)
+    grad_mixed = dot(grad_out, out_mat, ((1,), (1,)))
+    qkv = dot(hidden, qkv_mat, ((1,), (0,)))
+    cosines, sines = tables(total_len, ROT)
+    attn_mixed, grad_qkv, grad_qkv_sum = attention(
+        pair_lengths, qkv, bqkv[None], grad_mixed, cosines, sines
+    )
+    attn_mixed, grad_qkv = attn_mixed.astype(bf16), grad_qkv.astype(bf16)
 
     up_proj = dot(hidden, fc1_mat, ((1,), (0,))) + bfc1
     activated = gelu_tanh(up_proj).astype(bf16)
@@ -489,46 +698,13 @@
     ).astype(f32)
     output = (inputs + branch_own + bout_all + bfc2_all).astype(bf16)[None]
 
-    grad_mixed = dot(grad_out, out_mat, ((1,), (1,))).astype(bf16)
     grad_act = dot(grad_out, fc2_mat, ((1,), (1,)))
     _, gelu_pull = jax.vjp(gelu_tanh, up_proj)
     grad_up = gelu_pull(grad_act)[0].astype(bf16)
 
-    def attend_backward(packed):
-        query_seq, key_seq, value_seq, grad_heads, log_total, length = packed
-        scores = masked_scores(query_seq, key_seq, all_places, length)
-        probability = jnp.exp(scores - log_total[:, :, None])
-        grad_probs = jnp.einsum("qhd,khd->hqk", grad_heads, value_seq, preferred_element_type=f32)
-        inner = jnp.sum(probability * grad_probs, axis=-1, keepdims=True)
-        grad_scores = (probability * (grad_probs - inner)).astype(bf16)
-        grad_query = jnp.einsum("hqk,khd->qhd", grad_scores, key_seq, preferred_element_type=f32)
-        grad_keys = jnp.einsum("hqk,qhd->khd", grad_scores, query_seq, preferred_element_type=f32)
-        grad_values = jnp.einsum(
-            "hqk,qhd->khd", probability.astype(bf16), grad_heads, preferred_element_type=f32
-        )
-        return grad_query, grad_keys, grad_values
-
-    grad_query, grad_keys, grad_values = lax.map(
-        attend_backward,
-        (
-            queries,
-            key_rows,
-            values,
-            grad_mixed.reshape(2, total_len, heads, HEAD_DIM),
-            log_totals,
-            length_pair,
-        ),
-    )
-    turn_back = jax.vmap(lambda v: rotary_back(v, angles))
-    grad_qkv = (
-        jnp.stack([turn_back(grad_query * 0.125), turn_back(grad_keys), grad_values], axis=2)
-        .reshape(2 * total_len, 3 * own_width)
-        .astype(bf16)
-    )
-
     grad_hidden = dot(grad_qkv, qkv_mat, ((1,), (1,))) + dot(grad_up, fc1_mat, ((1,), (1,)))
-    grad_hidden_own = plain_order(
-        lax.psum_scatter(grad_hidden.astype(bf16), ROWS_AXES, scatter_dimension=0, tiled=True)
+    grad_hidden_own = lax.psum_scatter(
+        grad_hidden.astype(bf16), ROWS_AXES, scatter_dimension=0, tiled=True
     ).astype(f32)
     grad_norm = grad_hidden_own * gain_all
     grad_input = grad_own.astype(f32) + inv_std * (
@@ -544,11 +720,11 @@
     fc2_part = dot(activated, grad_out, ((0,), (0,))).astype(bf16)
     grad_fc2 = reduce_blocks(place_blocks(fc2_part))
     fc1_part = dot(hidden, grad_up, ((0,), (0,))).astype(bf16)
-    fc1_total = reduce_blocks(jnp.split(fc1_part, 4, axis=0)).astype(bf16)
+    fc1_total = reduce_blocks(by_place(blocks_of_rows(fc1_part), zh, y)).astype(bf16)
     out_part = dot(attn_mixed, grad_out, ((0,), (0,))).astype(bf16)
     grad_wout = reduce_blocks(place_blocks(out_part))
     qkv_part = dot(hidden, grad_qkv, ((0,), (0,))).astype(bf16)
-    qkv_total = reduce_blocks(jnp.split(qkv_part, 4, axis=0)).astype(bf16)
+    qkv_total = reduce_blocks(by_place(blocks_of_rows(qkv_part), zh, y)).astype(bf16)
 
     def all_columns(total, shape, order, out_width):
         spread = lax.all_to_all(total.reshape(8, rows, -1), ROWS_AXES, 0, 0, tiled=True)
@@ -562,7 +738,7 @@
 
     mine = (jnp.arange(8) == place).astype(f32)
     bqkv_term = (
-        (jnp.sum(grad_qkv, axis=0, dtype=f32).reshape(1, 3, 2, 2, HEAD_DIM) * mine[:, None, None, None, None])
+        (jnp.sum(grad_qkv_sum, axis=0).reshape(1, 3, 2, 2, HEAD_DIM) * mine[:, None, None, None, None])
         .reshape(2, 4, 3, 2, 2, HEAD_DIM)
         .transpose(2, 3, 0, 4, 1, 5)
         .reshape(-1)
@@ -574,15 +750,14 @@
         .reshape(-1)
     )
     bias_term = jnp.sum(grad_own, axis=0, dtype=f32)
+    terms = jnp.concatenate([v.reshape(32, -1) for v in (bqkv_term, bfc1_term, bias_term)], axis=1)
+    sums = sum_small(terms.reshape(32, -1, 128), 1).reshape(-1)
+    grad_bqkv, grad_bfc1, grad_bias = jnp.split(sums, np.cumsum([3 * rows, ff_rows]))
     gain_term = jnp.sum(grad_hidden_own * normed, axis=0)
     shift_term = jnp.sum(grad_hidden_own, axis=0)
-    terms = jnp.concatenate(
-        [v.reshape(32, -1) for v in (bqkv_term, bfc1_term, bias_term, gain_term, shift_term)], axis=1
-    )
-    sums = lax.psum_scatter(terms, FINE, scatter_dimension=0, tiled=True)[0]
-    grad_bqkv, grad_bfc1, grad_bias, grad_gain, grad_shift = jnp.split(
-        sums, np.cumsum([3 * rows, ff_rows, rows, rows])
-    )
+    terms = jnp.concatenate([gain_term.reshape(32, -1), shift_term.reshape(32, -1)], axis=1)
+    sums = sum_small(terms.reshape(32, -1, 128), 2).reshape(-1)
+    grad_gain, grad_shift = jnp.split(sums, [rows])
     return (
         output,
         grad_input,

time: 1080 us -> 649 us (0.60); the launches traced: 1060 us -> 643 us
  local copies, waits for them, and re-layouts: 219 us -> 56.2 us
  waiting for transfers between devices: 361 us -> 223 us
  matrix products: 263 us -> 147 us
  Pallas kernels: 0 us -> 100 us
  other arithmetic: 114 us -> 52.2 us
  blocking collectives: 46.8 us -> 0 us
    dynamic_update_slice x12 -> x0, local copies, waits for them, and re-layouts: 116 us -> none  [split_device(): lax.map(attend_backward, (queries, key_rows, values, grad_mixed.reshape(2...]
    unnamed x6 -> x4, waiting for transfers between devices: 111 us -> 0.07 us
    dot_general x14 -> x0, matrix products: 107 us -> none  [the longest x4 38.4 us: masked_scores(): jnp.einsum('qhd,khd->hqk', queries, key_rows, preferred_element_type=jnp....]
    pallas_call x0 -> x4, Pallas kernels: none -> 100 us  [the longest x2 53.4 us: sum_small(): pl.pallas_call(sum_kernel, out_shape=jax.ShapeDtypeStruct((n, 128), jnp.f...]
    unnamed x2 -> x0, blocking collectives: 46.8 us -> none
    reduce_sum x3 -> x1, other arithmetic: 36.4 us -> 0.02 us  [split_device(): jnp.sum(grad_qkv_sum, axis=0).reshape(1, 3, 2, 2, HEAD_DIM)]
    ppermute x24, waiting for transfers between devices: 236 us -> 206 us  [swap(): return lax.ppermute(values, axis, [(0, 1), (1, 0)])]
    convert_element_type x8 -> x5, other arithmetic: 27.1 us -> 8.37 us  [the longest x1 4.05 us: split_device(): reduce_blocks(by_place(blocks_of_rows(fc1_part), zh, y)).astype(bf16)]
  transfers between devices with their start and end apart: 33 -> 32, of which waited for: 11 -> 11; matrix products, arithmetic and copies ran while one was open for 48% -> 27% of each run, Pallas kernels for 0% -> 8%
where the time goes in v2:
time: 649 us; the launch traced here: 643 us
  waiting for transfers between devices  223 us (34%)
  matrix products  147 us (23%)
  Pallas kernels  100 us (15%)
  local copies, waits for them, and re-layouts  56.2 us (9%)
  other arithmetic  52.2 us (8%)
  starting transfers between devices  49.5 us (8%)
  between operations  15.7 us (2%)
    ppermute x24, waiting for transfers between devices, swap(): return lax.ppermute(values, axis, [(0, 1), (1, 0)])  206 us
    dot_general x12, matrix products, dot(): lax.dot_general(left, right, (dims, ((), ())), preferred_element_type=jnp...  147 us
    pallas_call x2, Pallas kernels, sum_small(): pl.pallas_call(sum_kernel, out_shape=jax.ShapeDtypeStruct((n, 128), jnp.f...  53.4 us
    pallas_call x1, Pallas kernels, attention(): pl.pallas_call(functools.partial(attention_kernel, total=total, pairs=pai...  34.8 us
    ppermute x24, starting transfers between devices, swap(): return lax.ppermute(values, axis, [(0, 1), (1, 0)])  28.1 us
    convert_element_type x6, local copies, waits for them, and re-layouts, all_columns(): return spread.reshape(rows, out_width).astype(f32)  21.6 us
    all_to_all x2, waiting for transfers between devices, own_columns(): lax.all_to_all(spread, ROWS_AXES, 0, 0, tiled=True).reshape(8 * rows, -1)  17.2 us
  transfers between devices with their start and end apart: 32, of which 11 were waited for; matrix products, arithmetic and copies ran while one was open for 27% of the time, Pallas kernels for 8%

profile of v2, /device:TPU:0, one launch (start us, length us, event | category | flops | bytes accessed | tf_op | source)
XLA Modules:
  0.0 643.4 jit_solution(9441899228304031593)
XLA Ops:
  11.2 4.1 concatenate.51
  15.8 12.3 %shard_map.220 = f32[32,6,128]{2,1,0:T(8,128)} custom-call(f32[1,6,128]{2,1,0:T(8,128)} %pad_bitcast_fusion.src), custom_call_target="tpu_custom_call" | custom-call | tf_op jit(solution)/shard_map/pallas_call | solution.py:577
  37.9 4.2 all-to-all-start
  45.3 17.2 %all-to-all-done = bf16[8,64,768]{2,1,0:T(8,128)(2,1)} async-done(((bf16[8,64,768]{2,1,0:T(8,128)(2,1)}), bf16[8,64,768]{2,1,0:T(8,128)(2,1)}, u32[]{:S(2)}, u32[]{:S(2)}) %all-to-all-start) | async-done | bytes 786464 | tf_op jit(solution)/shard_map/all_to_all | solution.py:648
  62.5 4.3 all-to-all-start.1
  67.0 2.2 collective-permute-start.9
  72.3 2.2 collective-permute-start
  74.5 43.4 %collective-permute-done.9 = bf16[256,2048]{1,0:T(8,128)(2,1)} collective-permute-done((bf16[256,2048]{1,0:T(8,128)(2,1)}, bf16[256,2048]{1,0:T(8,128)(2,1)}, u32[]{:S(2)}, u32[]{:S(2)}) %collective-permute-start.9) | collective-permute-done | bytes 1048608 | tf_op jit(solution)/shard_map/ppermute | solution.py:342
  121.5 21.3 %collective-permute-done.3 = bf16[64,2048]{1,0:T(8,128)(2,1)} collective-permute-done((bf16[64,2048]{1,0:T(8,128)(2,1)S(1)}, bf16[64,2048]{1,0:T(8,128)(2,1)}, u32[]{:S(2)}, u32[]{:S(2)}) %collective-permute-start.3) | collective-permute-done | bytes 262176 | tf_op jit(solution)/shard_map/ppermute | solution.py:342
  148.0 4.3 collective-permute-done.4
  153.3 14.5 %collective-permute-done = bf16[512,768]{1,0:T(8,128)(2,1)} collective-permute-done((bf16[512,768]{1,0:T(8,128)(2,1)}, bf16[512,768]{1,0:T(8,128)(2,1)}, u32[]{:S(2)}, u32[]{:S(2)}) %collective-permute-start) | collective-permute-done | bytes 786464 | tf_op jit(solution)/shard_map/ppermute | solution.py:342
  171.1 4.4 broadcast_select_fusion.13
  175.5 30.5 %collective-permute-done.6 = bf16[512,1024]{1,0:T(8,128)(2,1)S(1)} collective-permute-done((bf16[512,1024]{1,0:T(8,128)(2,1)}, bf16[512,1024]{1,0:T(8,128)(2,1)S(1)}, u32[]{:S(2)}, u32[]{:S(2)}) %collective-permute-start.6) | collective-permute-done | bytes 1048608 | tf_op jit(solution)/shard_map/ppermute | solution.py:342
  211.5 19.2 %collective-permute-done.7 = bf16[512,1024]{1,0:T(8,128)(2,1)S(1)} collective-permute-done((bf16[512,1024]{1,0:T(8,128)(2,1)S(1)}, bf16[512,1024]{1,0:T(8,128)(2,1)S(1)}, u32[]{:S(2)}, u32[]{:S(2)}) %collective-permute-start.7) | collective-permute-done | bytes 1048608 | tf_op jit(solution)/shard_map/ppermute | solution.py:342
  238.9 14.4 %fusion.44 = f32[2048,1024]{1,0:T(8,128)} fusion(bf16[2048,2048]{1,0:T(8,128)(2,1)} %all-gather.3.cloned.1.call-done, bf16[2048,1024]{1,0:T(8,128)(2,1)} %slice_dynamic-update-slice_fusion), kind=kOutput, calls=%fused_computation.180 | convolution fusion | flops 8589934592 | bytes 20971520 | tf_op jit(solution)/shard_map/dot_general | solution.py:390
  253.3 24.0 %convert_reduce_fusion = (f32[1024]{0:T(1024)}, bf16[2048,1024]{1,0:T(8,128)(2,1)}) fusion(bf16[2048,2048]{1,0:T(8,128)(2,1)} %all-gather.5.cloned.1.call-done, bf16[256,2048]{1,0:T(8,128)(2,1)} %get-tuple-element.43, bf16[256,2048]{1,0:T(8,128)(2,1)} %get-tuple-element.42, bf16[256,2048]{1,0:T(8,128)(2,1)} %get-tuple-element.41, ...), kind=kOutput, calls=%fused_computation.12 | convolution fusion | flops 8663333888 | bytes 25174016 | tf_op jit(solution)/shard_map/dot_general | solution.py:390
  277.3 15.9 %fusion.45 = f32[2048,2048]{1,0:T(8,128)} fusion(bf16[2048,1024]{1,0:T(8,128)(2,1)} %get-tuple-element.76, bf16[2048,1024]{1,0:T(8,128)(2,1)} %slice_dynamic-update-slice_fusion), kind=kOutput, calls=%fused_computation.181 | convolution fusion | flops 8589934592 | bytes 25165824 | tf_op jit(solution)/shard_map/dot_general | solution.py:390
  293.2 8.5 %fusion.43.q_in.k_in.v_in = f32[2048,768]{1,0:T(8,128)} fusion(bf16[2048,2048]{1,0:T(8,128)(2,1)S(1)} %copy-done.44, bf16[2048,768]{1,0:T(8,128)(2,1)S(1)} %copy-done.37), kind=kOutput, calls=%fused_computation.179 | convolution fusion | flops 6442450944 | bytes 17825792 | tf_op jit(solution)/shard_map/dot_general | solution.py:390
  301.8 2.4 fusion.34.go_in
  304.2 34.8 %shard_map.221 = (f32[2048,256]{1,0:T(8,128)S(1)}, f32[2048,768]{1,0:T(8,128)}, f32[2,1,768]{2,1,0:T(1,128)S(1)}) custom-call(s32[2]{0:T(128)S(1)} %convert_reduce_fusion.4.len_ref, f32[1,768]{1,0:T(1,128)S(1)} %constant_dynamic-slice_fusion.1.bias_ref, f32[1024,128]{1,0:T(8,128)S(1)} %concatenate.52.cos_ref, f32[1024,128]{1,0:T(8,128)S(1)} %concatenate.53.sin_ref, ...), custom_call_target="tpu_custom_call" | custom-call | flops 6442450944 | bytes 20971520 | tf_op jit(solution)/shard_map/pallas_call | solution.py:483
  339.0 14.3 %add_convert_fusion = bf16[2048,2048]{1,0:T(8,128)(2,1)} fusion(f32[2048,2048]{1,0:T(8,128)} %fusion.45, bf16[2048,768]{1,0:T(8,128)(2,1)S(1)} %copy-done.37, f32[2048,768]{1,0:T(8,128)} %get-tuple-element.16), kind=kOutput, calls=%fused_computation | convolution fusion | flops 6452412416 | bytes 34603008 | tf_op jit(solution)/shard_map/dot_general | solution.py:390
  353.3 18.9 %fusion.31 = f32[2048,2048]{1,0:T(8,128)} fusion(bf16[256,2048]{1,0:T(8,128)(2,1)} %get-tuple-element.43, bf16[256,2048]{1,0:T(8,128)(2,1)} %get-tuple-element.42, bf16[256,2048]{1,0:T(8,128)(2,1)} %get-tuple-element.41, bf16[256,2048]{1,0:T(8,128)(2,1)} %copy-done.26, f32[2048,1024]{1,0:T(8,128)} %fusion.44, f32[1024]{0:T(1024)S(1)} %bitcast.130), kind=kOutput, calls=%fused_computation.113 | convolution fusion | flops 8627683328 | bytes 29364224 | tf_op jit(solution)/shard_map/dot_general | solution.py:390
  372.3 9.4 %add_convert_fusion.1 = bf16[2048,2048]{1,0:T(8,128)(2,1)} fusion(f32[2048,2048]{1,0:T(8,128)} %fusion.31, f32[2048,256]{1,0:T(8,128)S(1)} %get-tuple-element.15, bf16[64,2048]{1,0:T(8,128)(2,1)S(1)} %copy-done.25, bf16[64,2048]{1,0:T(8,128)(2,1)S(1)} %copy-done.23, bf16[64,2048]{1,0:T(8,128)(2,1)S(1)} %copy-done.21, bf16[64,2048]{1,0:T(8,128)(2,1)S(1)} %get-tuple-element.62), kind=kOutput, calls=%fused_computation.1 | convolution fusion | flops 2160590848 | bytes 28311552 | tf_op jit(solution)/shard_map/dot_general | solution.py:390
  382.9 11.2 %convolution_convert_fusion.2 = bf16[2048,768]{1,0:T(8,128)(2,1)S(1)} fusion(bf16[2048,2048]{1,0:T(8,128)(2,1)} %all-gather.3.cloned.1.call-done, f32[2048,768]{1,0:T(8,128)} %get-tuple-element.16), kind=kOutput, calls=%fused_computation.17 | convolution fusion | flops 6445596672 | bytes 17825792 | tf_op jit(solution)/shard_map/dot_general | solution.py:390
  396.8 12.4 %convolution_convert_fusion.1 = bf16[2048,1024]{1,0:T(8,128)(2,1)S(1)} fusion(bf16[2048,2048]{1,0:T(8,128)(2,1)} %all-gather.3.cloned.1.call-done, bf16[2048,1024]{1,0:T(8,128)(2,1)S(1)} %copy-done.46), kind=kOutput, calls=%fused_computation.16 | convolution fusion | flops 8592031744 | bytes 16777216 | tf_op jit(solution)/shard_map/dot_general | solution.py:390
  409.8 2.3 broadcast_select_fusion.23
  414.1 12.8 %convolution_convert_fusion = bf16[1024,2048]{1,0:T(8,128)(2,1)S(1)} fusion(bf16[2048,2048]{1,0:T(8,128)(2,1)S(1)} %bitcast.112, f32[2048,1024]{1,0:T(8,128)} %fusion.44, f32[1024]{0:T(1024)S(1)} %bitcast.131), kind=kOutput, calls=%fused_computation.15 | convolution fusion | flops 8613003264 | bytes 20975616 | tf_op jit(solution)/shard_map/dot_general | solution.py:390
  433.1 2.3 convolution_convert_fusion.3
  435.5 41.6 %collective-permute-done.19 = bf16[512,1024]{1,0:T(8,128)(2,1)S(1)} collective-permute-done((bf16[512,1024]{1,0:T(8,128)(2,1)S(1)}, bf16[512,1024]{1,0:T(8,128)(2,1)S(1)}, u32[]{:S(2)}, u32[]{:S(2)}) %collective-permute-start.19) | collective-permute-done | bytes 1048608 | tf_op jit(solution)/shard_map/ppermute | solution.py:342
  477.1 2.2 add_convert_fusion.4
  479.9 2.7 add_convert_fusion.5
  482.6 8.0 %all-to-all-start.2 = ((bf16[8,64,768]{2,1,0:T(8,128)(2,1)}), bf16[8,64,768]{2,1,0:T(8,128)(2,1)S(1)}, u32[]{:S(2)}, u32[]{:S(2)}) async-start(bf16[8,64,768]{2,1,0:T(8,128)(2,1)} %bitcast.17), calls=%async_computation.4 | async-start | bytes 1572864 | tf_op jit(solution)/shard_map/all_to_all | solution.py:730
  492.8 6.9 %collective-permute-done.22 = bf16[256,2048]{1,0:T(8,128)(2,1)} collective-permute-done((bf16[256,2048]{1,0:T(8,128)(2,1)}, bf16[256,2048]{1,0:T(8,128)(2,1)}, u32[]{:S(2)}, u32[]{:S(2)}) %collective-permute-start.22) | collective-permute-done | bytes 1048608 | tf_op jit(solution)/shard_map/ppermute | solution.py:342
  501.2 4.4 add_convert_fusion.2
  506.3 22.9 %collective-permute-done.20 = bf16[512,1024]{1,0:T(8,128)(2,1)} collective-permute-done((bf16[512,1024]{1,0:T(8,128)(2,1)}, bf16[512,1024]{1,0:T(8,128)(2,1)}, u32[]{:S(2)}, u32[]{:S(2)}) %collective-permute-start.20) | collective-permute-done | bytes 1048608 | tf_op jit(solution)/shard_map/ppermute | solution.py:342
  529.3 4.1 add_convert_fusion.3
  533.4 4.5 all-to-all-start.3
  542.2 43.4 %shard_map.223 = f32[4,128]{1,0:T(4,128)} custom-call(f32[32,4,128]{2,1,0:T(4,128)} %reshape.175.src), custom_call_target="tpu_custom_call" | custom-call | tf_op jit(solution)/shard_map/pallas_call | solution.py:589
  591.0 4.9 convert_add_fusion.1
  595.9 3.3 reshape.180
  599.2 4.3 copy.58
  603.6 3.8 reshape.178
  607.4 3.1 reshape.181
  610.5 2.9 copy.59
  613.5 4.0 reshape.179
  617.6 2.3 fusion.25
  620.7 9.9 %shard_map.222 = f32[1,128]{1,0:T(1,128)} custom-call(f32[32,1,128]{2,1,0:T(1,128)} %bitcast.124), custom_call_target="tpu_custom_call" | custom-call | tf_op jit(solution)/shard_map/pallas_call | solution.py:589
  632.0 4.2 fusion.28
  (249 shorter events, 76.5 us)
Async XLA Ops:
  7.2 231.7 %all-gather.3.cloned.1.call-start = ((), (), s32[]{:S(2)}) async-start(), calls=%async_computation.6 | async-start | bytes 9437184 | tf_op jit(solution)/shard_map/all_gather | solution.py:669
  31.3 222.0 %all-gather.5.cloned.1.call-start = ((), (), s32[]{:S(2)}) async-start(), calls=%async_computation.7 | async-start | bytes 9437184 | tf_op jit(solution)/shard_map/all_gather | solution.py:672
  37.9 24.6 %all-to-all-start = ((bf16[8,64,768]{2,1,0:T(8,128)(2,1)}), bf16[8,64,768]{2,1,0:T(8,128)(2,1)}, u32[]{:S(2)}, u32[]{:S(2)}) async-start(bf16[8,64,768]{2,1,0:T(8,128)(2,1)} %reshape.164), calls=%async_computation | async-start | bytes 1572864 | tf_op jit(solution)/shard_map/all_to_all | solution.py:648
  62.5 89.8 %all-to-all-start.1 = ((bf16[8,64,1024]{2,1,0:T(8,128)(2,1)}), bf16[8,64,1024]{2,1,0:T(8,128)(2,1)}, u32[]{:S(2)}, u32[]{:S(2)}) async-start(bf16[8,64,1024]{2,1,0:T(8,128)(2,1)} %reshape.167), calls=%async_computation.1 | async-start | bytes 2097152 | tf_op jit(solution)/shard_map/all_to_all | solution.py:648
  66.8 550.7 %reduce-scatter.5.cloned.1.call-start = ((), (), s32[]{:S(2)}) async-start(), calls=%async_computation.9 | async-start | bytes 9437184 | tf_op jit(solution)/shard_map/reduce_scatter | solution.py:706
  67.0 50.9 %collective-permute-start.9 = (bf16[256,2048]{1,0:T(8,128)(2,1)}, bf16[256,2048]{1,0:T(8,128)(2,1)}, u32[]{:S(2)}, u32[]{:S(2)}) collective-permute-start(bf16[256,2048]{1,0:T(8,128)(2,1)} %param.23), channel_id=1, source_target_pairs={{0,16},{16,0},{1,17},{17,1},{2,18},{18,2},{3,19},{19,3},{4,20},{20... | collective-permute-start | bytes 3145736 | tf_op jit(solution)/shard_map/ppermute | solution.py:342
  69.3 73.5 %collective-permute-start.3 = (bf16[64,2048]{1,0:T(8,128)(2,1)S(1)}, bf16[64,2048]{1,0:T(8,128)(2,1)}, u32[]{:S(2)}, u32[]{:S(2)}) collective-permute-start(bf16[64,2048]{1,0:T(8,128)(2,1)S(1)} %copy-done.30), channel_id=1, source_target_pairs={{0,16},{16,0},{1,17},{17,1},{2,18},{18,2},{3,19},{19,3},{4,20},{20... | collective-permute-start | bytes 786440 | tf_op jit(solution)/shard_map/ppermute | solution.py:342
  70.0 77.3 %collective-permute-start.5 = (bf16[64,2048]{1,0:T(8,128)(2,1)S(1)}, bf16[64,2048]{1,0:T(8,128)(2,1)}, u32[]{:S(2)}, u32[]{:S(2)}) collective-permute-start(bf16[64,2048]{1,0:T(8,128)(2,1)S(1)} %copy-done.30), channel_id=1, source_target_pairs={{0,4},{4,0},{1,5},{5,1},{2,6},{6,2},{3,7},{7,3},{8,12},{12,8},{9,1... | collective-permute-start | bytes 786440 | tf_op jit(solution)/shard_map/ppermute | solution.py:342
  71.4 98.8 %collective-permute-start.11 = (bf16[256,2048]{1,0:T(8,128)(2,1)}, bf16[256,2048]{1,0:T(8,128)(2,1)}, u32[]{:S(2)}, u32[]{:S(2)}) collective-permute-start(bf16[256,2048]{1,0:T(8,128)(2,1)} %param.23), channel_id=1, source_target_pairs={{0,4},{4,0},{1,5},{5,1},{2,6},{6,2},{3,7},{7,3},{8,12},{12,8},{9,1... | collective-permute-start | bytes 3145736 | tf_op jit(solution)/shard_map/ppermute | solution.py:342
  72.3 95.5 %collective-permute-start = (bf16[512,768]{1,0:T(8,128)(2,1)}, bf16[512,768]{1,0:T(8,128)(2,1)}, u32[]{:S(2)}, u32[]{:S(2)}) collective-permute-start(bf16[512,768]{1,0:T(8,128)(2,1)} %bitcast.5), channel_id=1, source_target_pairs={{0,16},{16,0},{1,17},{17,1},{2,18},{18,2},{3,19},{19,3},{4,20},{20... | collective-permute-start | bytes 2359304 | tf_op jit(solution)/shard_map/ppermute | solution.py:342
  117.9 53.2 %collective-permute-start.10 = (bf16[256,2048]{1,0:T(8,128)(2,1)}, bf16[256,2048]{1,0:T(8,128)(2,1)}, u32[]{:S(2)}, u32[]{:S(2)}) collective-permute-start(bf16[256,2048]{1,0:T(8,128)(2,1)} %collective-permute-done.9), channel_id=1, source_target_pairs={{0,4},{4,0},{1,5},{5,1},{2,6},{6,2},{3,7},{7,3},{8,12},{12,8},{9,1... | collective-permute-start | bytes 3145736 | tf_op jit(solution)/shard_map/ppermute | solution.py:342
  142.8 9.5 %collective-permute-start.4 = (bf16[64,2048]{1,0:T(8,128)(2,1)}, bf16[64,2048]{1,0:T(8,128)(2,1)}, u32[]{:S(2)}, u32[]{:S(2)}) collective-permute-start(bf16[64,2048]{1,0:T(8,128)(2,1)} %collective-permute-done.3), channel_id=1, source_target_pairs={{0,4},{4,0},{1,5},{5,1},{2,6},{6,2},{3,7},{7,3},{8,12},{12,8},{9,1... | collective-permute-start | bytes 786440 | tf_op jit(solution)/shard_map/ppermute | solution.py:342
  147.3 60.2 %collective-permute-start.2 = (bf16[512,768]{1,0:T(8,128)(2,1)}, bf16[512,768]{1,0:T(8,128)(2,1)}, u32[]{:S(2)}, u32[]{:S(2)}) collective-permute-start(bf16[512,768]{1,0:T(8,128)(2,1)} %bitcast.5), channel_id=1, source_target_pairs={{0,4},{4,0},{1,5},{5,1},{2,6},{6,2},{3,7},{7,3},{8,12},{12,8},{9,1... | collective-permute-start | bytes 2359304 | tf_op jit(solution)/shard_map/ppermute | solution.py:342
  152.3 53.8 %collective-permute-start.6 = (bf16[512,1024]{1,0:T(8,128)(2,1)}, bf16[512,1024]{1,0:T(8,128)(2,1)S(1)}, u32[]{:S(2)}, u32[]{:S(2)}) collective-permute-start(bf16[512,1024]{1,0:T(8,128)(2,1)} %bitcast.9), channel_id=1, source_target_pairs={{0,16},{16,0},{1,17},{17,1},{2,18},{18,2},{3,19},{19,3},{4,20},{20... | collective-permute-start | bytes 3145736 | tf_op jit(solution)/shard_map/ppermute | solution.py:342
  167.8 39.7 %collective-permute-start.1 = (bf16[512,768]{1,0:T(8,128)(2,1)}, bf16[512,768]{1,0:T(8,128)(2,1)S(1)}, u32[]{:S(2)}, u32[]{:S(2)}) collective-permute-start(bf16[512,768]{1,0:T(8,128)(2,1)} %collective-permute-done), channel_id=1, source_target_pairs={{0,4},{4,0},{1,5},{5,1},{2,6},{6,2},{3,7},{7,3},{8,12},{12,8},{9,1... | collective-permute-start | bytes 2359304 | tf_op jit(solution)/shard_map/ppermute | solution.py:342
  170.2 131.5 %copy-start.20 = (bf16[64,2048]{1,0:T(8,128)(2,1)}, bf16[64,2048]{1,0:T(8,128)(2,1)S(1)}, u32[]{:S(2)}) copy-start(bf16[64,2048]{1,0:T(8,128)(2,1)S(1)} %get-tuple-element.63) | copy-start | bytes 786436
  170.2 131.5 %copy-start.22 = (bf16[64,2048]{1,0:T(8,128)(2,1)}, bf16[64,2048]{1,0:T(8,128)(2,1)S(1)}, u32[]{:S(2)}) copy-start(bf16[64,2048]{1,0:T(8,128)(2,1)S(1)} %get-tuple-element.64) | copy-start | bytes 786436
  170.3 131.5 %copy-start.24 = (bf16[64,2048]{1,0:T(8,128)(2,1)}, bf16[64,2048]{1,0:T(8,128)(2,1)S(1)}, u32[]{:S(2)}) copy-start(bf16[64,2048]{1,0:T(8,128)(2,1)S(1)} %get-tuple-element.65) | copy-start | bytes 786436
  170.3 39.4 %collective-permute-start.8 = (bf16[512,1024]{1,0:T(8,128)(2,1)}, bf16[512,1024]{1,0:T(8,128)(2,1)S(1)}, u32[]{:S(2)}, u32[]{:S(2)}) collective-permute-start(bf16[512,1024]{1,0:T(8,128)(2,1)} %bitcast.9), channel_id=1, source_target_pairs={{0,4},{4,0},{1,5},{5,1},{2,6},{6,2},{3,7},{7,3},{8,12},{12,8},{9,1... | collective-permute-start | bytes 3145736 | tf_op jit(solution)/shard_map/ppermute | solution.py:342
  175.5 77.8 %copy-start.26 = (bf16[256,2048]{1,0:T(8,128)(2,1)}, bf16[256,2048]{1,0:T(8,128)(2,1)S(1)}, u32[]{:S(2)}) copy-start(bf16[256,2048]{1,0:T(8,128)(2,1)S(1)} %get-tuple-element.40) | copy-start | bytes 3145732
  206.1 24.5 %collective-permute-start.7 = (bf16[512,1024]{1,0:T(8,128)(2,1)S(1)}, bf16[512,1024]{1,0:T(8,128)(2,1)S(1)}, u32[]{:S(2)}, u32[]{:S(2)}) collective-permute-start(bf16[512,1024]{1,0:T(8,128)(2,1)S(1)} %collective-permute-done.6), channel_id=1, source_target_pairs={{0,4},{4,0},{1,5},{5,1},{2,6},{6,2},{3,7},{7,3},{8,12},{12,8},{9,1... | collective-permute-start | bytes 3145736 | tf_op jit(solution)/shard_map/ppermute | solution.py:342
  253.3 48.5 %slice-start = ((s8[8388608]{0:T(1024)(128)(4,1)}), s8[4194304]{0:T(1024)(128)(4,1)S(1)}, s32[]{:S(2)}) async-start(s8[8388608]{0:T(1024)(128)(4,1)} %bitcast.109), calls=%async_computation.10 | async-start | bytes 8388608
  353.3 278.7 %reduce-scatter.3.cloned.1.call-start = ((), (), s32[]{:S(2)}) async-start(), calls=%async_computation.8 | async-start | bytes 9437184 | tf_op jit(solution)/shard_map/reduce_scatter | solution.py:696
  394.7 85.1 %collective-permute-start.12 = (bf16[512,768]{1,0:T(8,128)(2,1)S(1)}, bf16[512,768]{1,0:T(8,128)(2,1)}, u32[]{:S(2)}, u32[]{:S(2)}) collective-permute-start(bf16[512,768]{1,0:T(8,128)(2,1)S(1)} %get-tuple-element.44), channel_id=1, source_target_pairs={{0,4},{4,0},{1,5},{5,1},{2,6},{6,2},{3,7},{7,3},{8,12},{12,8},{9,1... | collective-permute-start | bytes 2359304 | tf_op jit(solution)/shard_map/ppermute | solution.py:342
  396.2 35.9 %collective-permute-start.13 = (bf16[512,768]{1,0:T(8,128)(2,1)S(1)}, bf16[512,768]{1,0:T(8,128)(2,1)S(1)}, u32[]{:S(2)}, u32[]{:S(2)}) collective-permute-start(bf16[512,768]{1,0:T(8,128)(2,1)S(1)} %get-tuple-element.45), channel_id=1, source_target_pairs={{0,4},{4,0},{1,5},{5,1},{2,6},{6,2},{3,7},{7,3},{8,12},{12,8},{9,1... | collective-permute-start | bytes 2359304 | tf_op jit(solution)/shard_map/ppermute | solution.py:342
  409.7 67.4 %copy-start.4 = (bf16[256,1024]{1,0:T(8,128)(2,1)}, bf16[256,1024]{1,0:T(8,128)(2,1)S(1)}, u32[]{:S(2)}) copy-start(bf16[256,1024]{1,0:T(8,128)(2,1)S(1)} %get-tuple-element.28) | copy-start | bytes 1572868
  409.7 67.4 %copy-start.6 = (bf16[256,1024]{1,0:T(8,128)(2,1)}, bf16[256,1024]{1,0:T(8,128)(2,1)S(1)}, u32[]{:S(2)}) copy-start(bf16[256,1024]{1,0:T(8,128)(2,1)S(1)} %get-tuple-element.29) | copy-start | bytes 1572868
  409.7 67.4 %copy-start.8 = (bf16[256,1024]{1,0:T(8,128)(2,1)}, bf16[256,1024]{1,0:T(8,128)(2,1)S(1)}, u32[]{:S(2)}) copy-start(bf16[256,1024]{1,0:T(8,128)(2,1)S(1)} %get-tuple-element.30) | copy-start | bytes 1572868
  409.7 67.4 %copy-start.10 = (bf16[256,1024]{1,0:T(8,128)(2,1)}, bf16[256,1024]{1,0:T(8,128)(2,1)S(1)}, u32[]{:S(2)}) copy-start(bf16[256,1024]{1,0:T(8,128)(2,1)S(1)} %get-tuple-element.31) | copy-start | bytes 1572868
  409.7 67.4 %copy-start.12 = (bf16[256,1024]{1,0:T(8,128)(2,1)}, bf16[256,1024]{1,0:T(8,128)(2,1)S(1)}, u32[]{:S(2)}) copy-start(bf16[256,1024]{1,0:T(8,128)(2,1)S(1)} %get-tuple-element.32) | copy-start | bytes 1572868
  409.7 67.4 %copy-start.14 = (bf16[256,1024]{1,0:T(8,128)(2,1)}, bf16[256,1024]{1,0:T(8,128)(2,1)S(1)}, u32[]{:S(2)}) copy-start(bf16[256,1024]{1,0:T(8,128)(2,1)S(1)} %get-tuple-element.33) | copy-start | bytes 1572868
  409.7 67.4 %copy-start.16 = (bf16[256,1024]{1,0:T(8,128)(2,1)}, bf16[256,1024]{1,0:T(8,128)(2,1)S(1)}, u32[]{:S(2)}) copy-start(bf16[256,1024]{1,0:T(8,128)(2,1)S(1)} %get-tuple-element.34) | copy-start | bytes 1572868
  409.7 67.4 %copy-start.18 = (bf16[256,1024]{1,0:T(8,128)(2,1)}, bf16[256,1024]{1,0:T(8,128)(2,1)S(1)}, u32[]{:S(2)}) copy-start(bf16[256,1024]{1,0:T(8,128)(2,1)S(1)} %get-tuple-element.35) | copy-start | bytes 1572868
  412.0 93.6 %collective-permute-start.18 = (bf16[512,1024]{1,0:T(8,128)(2,1)}, bf16[512,1024]{1,0:T(8,128)(2,1)}, u32[]{:S(2)}, u32[]{:S(2)}) collective-permute-start(bf16[512,1024]{1,0:T(8,128)(2,1)} %get-tuple-element.26), channel_id=1, source_target_pairs={{0,4},{4,0},{1,5},{5,1},{2,6},{6,2},{3,7},{7,3},{8,12},{12,8},{9,1... | collective-permute-start | bytes 3145736 | tf_op jit(solution)/shard_map/ppermute | solution.py:342
  413.5 63.6 %collective-permute-start.19 = (bf16[512,1024]{1,0:T(8,128)(2,1)S(1)}, bf16[512,1024]{1,0:T(8,128)(2,1)S(1)}, u32[]{:S(2)}, u32[]{:S(2)}) collective-permute-start(bf16[512,1024]{1,0:T(8,128)(2,1)S(1)} %get-tuple-element.27), channel_id=1, source_target_pairs={{0,4},{4,0},{1,5},{5,1},{2,6},{6,2},{3,7},{7,3},{8,12},{12,8},{9,1... | collective-permute-start | bytes 3145736 | tf_op jit(solution)/shard_map/ppermute | solution.py:342
  429.5 70.1 %collective-permute-start.22 = (bf16[256,2048]{1,0:T(8,128)(2,1)}, bf16[256,2048]{1,0:T(8,128)(2,1)}, u32[]{:S(2)}, u32[]{:S(2)}) collective-permute-start(bf16[256,2048]{1,0:T(8,128)(2,1)} %get-tuple-element.25), channel_id=1, source_target_pairs={{0,4},{4,0},{1,5},{5,1},{2,6},{6,2},{3,7},{7,3},{8,12},{12,8},{9,1... | collective-permute-start | bytes 3145736 | tf_op jit(solution)/shard_map/ppermute | solution.py:342
  432.6 47.2 %collective-permute-start.14 = (bf16[512,768]{1,0:T(8,128)(2,1)S(1)}, bf16[512,768]{1,0:T(8,128)(2,1)S(1)}, u32[]{:S(2)}, u32[]{:S(2)}) collective-permute-start(bf16[512,768]{1,0:T(8,128)(2,1)S(1)} %add_convert_fusion.6), channel_id=1, source_target_pairs={{0,16},{16,0},{1,17},{17,1},{2,18},{18,2},{3,19},{19,3},{4,20},{20... | collective-permute-start | bytes 2359304 | tf_op jit(solution)/shard_map/ppermute | solution.py:342
  479.4 49.9 %collective-permute-start.20 = (bf16[512,1024]{1,0:T(8,128)(2,1)}, bf16[512,1024]{1,0:T(8,128)(2,1)}, u32[]{:S(2)}, u32[]{:S(2)}) collective-permute-start(bf16[512,1024]{1,0:T(8,128)(2,1)} %add_convert_fusion.4), channel_id=1, source_target_pairs={{0,16},{16,0},{1,17},{17,1},{2,18},{18,2},{3,19},{19,3},{4,20},{20... | collective-permute-start | bytes 3145736 | tf_op jit(solution)/shard_map/ppermute | solution.py:342
  482.6 50.8 %all-to-all-start.2 = ((bf16[8,64,768]{2,1,0:T(8,128)(2,1)}), bf16[8,64,768]{2,1,0:T(8,128)(2,1)S(1)}, u32[]{:S(2)}, u32[]{:S(2)}) async-start(bf16[8,64,768]{2,1,0:T(8,128)(2,1)} %bitcast.17), calls=%async_computation.4 | async-start | bytes 1572864 | tf_op jit(solution)/shard_map/all_to_all | solution.py:730
  490.7 98.3 %collective-permute-start.15 = (bf16[64,2048]{1,0:T(8,128)(2,1)S(1)}, bf16[64,2048]{1,0:T(8,128)(2,1)}, u32[]{:S(2)}, u32[]{:S(2)}) collective-permute-start(bf16[64,2048]{1,0:T(8,128)(2,1)S(1)} %get-tuple-element.58), channel_id=1, source_target_pairs={{0,4},{4,0},{1,5},{5,1},{2,6},{6,2},{3,7},{7,3},{8,12},{12,8},{9,1... | collective-permute-start | bytes 786440 | tf_op jit(solution)/shard_map/ppermute | solution.py:342
  492.3 45.5 %collective-permute-start.16 = (bf16[64,2048]{1,0:T(8,128)(2,1)S(1)}, bf16[64,2048]{1,0:T(8,128)(2,1)}, u32[]{:S(2)}, u32[]{:S(2)}) collective-permute-start(bf16[64,2048]{1,0:T(8,128)(2,1)S(1)} %get-tuple-element.59), channel_id=1, source_target_pairs={{0,4},{4,0},{1,5},{5,1},{2,6},{6,2},{3,7},{7,3},{8,12},{12,8},{9,1... | collective-permute-start | bytes 786440 | tf_op jit(solution)/shard_map/ppermute | solution.py:342
  499.7 29.6 %copy-start.13 = (bf16[256,1024]{1,0:T(8,128)(2,1)S(1)}, bf16[256,1024]{1,0:T(8,128)(2,1)}, u32[]{:S(2)}) copy-start(bf16[256,1024]{1,0:T(8,128)(2,1)} %copy-done.12) | copy-start | bytes 1572868
  499.7 29.6 %copy-start.15 = (bf16[256,1024]{1,0:T(8,128)(2,1)S(1)}, bf16[256,1024]{1,0:T(8,128)(2,1)}, u32[]{:S(2)}) copy-start(bf16[256,1024]{1,0:T(8,128)(2,1)} %copy-done.14) | copy-start | bytes 1572868
  499.7 91.3 %collective-permute-start.21 = (bf16[256,2048]{1,0:T(8,128)(2,1)}, bf16[256,2048]{1,0:T(8,128)(2,1)S(1)}, u32[]{:S(2)}, u32[]{:S(2)}) collective-permute-start(bf16[256,2048]{1,0:T(8,128)(2,1)} %get-tuple-element.24), channel_id=1, source_target_pairs={{0,4},{4,0},{1,5},{5,1},{2,6},{6,2},{3,7},{7,3},{8,12},{12,8},{9,1... | collective-permute-start | bytes 3145736 | tf_op jit(solution)/shard_map/ppermute | solution.py:342
  505.6 85.3 %collective-permute-start.23 = (bf16[256,2048]{1,0:T(8,128)(2,1)}, bf16[256,2048]{1,0:T(8,128)(2,1)}, u32[]{:S(2)}, u32[]{:S(2)}) collective-permute-start(bf16[256,2048]{1,0:T(8,128)(2,1)} %add_convert_fusion.2), channel_id=1, source_target_pairs={{0,16},{16,0},{1,17},{17,1},{2,18},{18,2},{3,19},{19,3},{4,20},{20... | collective-permute-start | bytes 3145736 | tf_op jit(solution)/shard_map/ppermute | solution.py:342
  533.4 74.0 %all-to-all-start.3 = ((bf16[8,64,1024]{2,1,0:T(8,128)(2,1)}), bf16[8,64,1024]{2,1,0:T(8,128)(2,1)}, u32[]{:S(2)}, u32[]{:S(2)}) async-start(bf16[8,64,1024]{2,1,0:T(8,128)(2,1)} %bitcast.20), calls=%async_computation.5 | async-start | bytes 2097152 | tf_op jit(solution)/shard_map/all_to_all | solution.py:730
  539.7 49.3 %collective-permute-start.17 = (bf16[64,2048]{1,0:T(8,128)(2,1)}, bf16[64,2048]{1,0:T(8,128)(2,1)}, u32[]{:S(2)}, u32[]{:S(2)}) collective-permute-start(bf16[64,2048]{1,0:T(8,128)(2,1)} %add_convert_fusion.7), channel_id=1, source_target_pairs={{0,16},{16,0},{1,17},{17,1},{2,18},{18,2},{3,19},{19,3},{4,20},{20... | collective-permute-start | bytes 786440 | tf_op jit(solution)/shard_map/ppermute | solution.py:342
  586.4 49.8 %copy-start.45 = (f32[64]{0:T(128)}, f32[64]{0:T(128)S(1)}, u32[]{:S(2)}) copy-start(f32[64]{0:T(128)S(1)} %split.200) | copy-start | bytes 772
  (35 other events, 539.7 us)
Sparse Core Ops, SparseCore 0:
  31.4 94.6 all-gather.2
  128.3 85.5 all-gather.4
  353.4 86.7 reduce-scatter.4
  442.4 129.1 reduce-scatter.2

commit v3 on v2

--- a/solution.py
+++ b/solution.py
@@ -342,20 +342,15 @@
     return lax.ppermute(values, axis, [(0, 1), (1, 0)])
 
 
+def after(values, earlier):
+    return lax.optimization_barrier((values, earlier))[0]
+
+
 def gather_blocks(own):
     across = swap(own, "zh")
     beside = swap(own, "y")
     both = swap(across, "y")
     return own, beside, across, both
-
-
-def reduce_blocks(blocks):
-    own, beside, across, both = blocks
-    got_beside = swap(beside, "y")
-    got_both = swap(both, "y")
-    passed = (across.astype(jnp.float32) + got_both.astype(jnp.float32)).astype(jnp.bfloat16)
-    got = swap(passed, "zh")
-    return own.astype(jnp.float32) + got_beside.astype(jnp.float32) + got.astype(jnp.float32)
 
 
 def by_place(blocks, zh, y):
@@ -375,15 +370,6 @@
     return jnp.concatenate(
         [halves[2 * zh + y][zl] for zh in range(2) for zl in range(2) for y in range(2)], axis=0
     )
-
-
-def blocks_of_rows(values):
-    parts = jnp.split(values, 8, axis=0)
-    return [
-        jnp.concatenate([parts[4 * zh + 2 * zl + y] for zl in range(2)], axis=0)
-        for zh in range(2)
-        for y in range(2)
-    ]
 
 
 def dot(left, right, dims):
@@ -518,7 +504,7 @@
 MESH_ID = pl.DeviceIdType.MESH
 
 
-def exchange_kernel(src, dst, send_sem, recv_sem, *, spread):
+def exchange_kernel(src, dst, send_sem, recv_sem):
     place = [lax.axis_index(name) for name in FINE]
     me = 0
     for p in place:
@@ -545,7 +531,7 @@
     def copy(k):
         where = away(k)
         return pltpu.make_async_remote_copy(
-            src_ref=src.at[index_of(where) if spread else 0],
+            src_ref=src.at[index_of(where)],
             dst_ref=dst.at[me],
             send_sem=send_sem.at[k],
             recv_sem=recv_sem.at[k],
@@ -558,7 +544,7 @@
         return carry
 
     lax.fori_loop(1, 32, send, 0)
-    dst[me] = src[me if spread else 0]
+    dst[me] = src[me]
 
     def finish(k, carry):
         copy(k).wait()
@@ -568,20 +554,277 @@
 
 
 def sum_kernel(src, out, dst, send_sem, recv_sem):
-    exchange_kernel(src, dst, send_sem, recv_sem, spread=True)
+    exchange_kernel(src, dst, send_sem, recv_sem)
     out[...] = jnp.sum(dst[...], axis=0)
 
 
-def gather_small(values):
-    n = values.shape[0]
+def feed_kernel(hidden, fc1, bias, cot, fc2, act, grad, sums):
+    up = nn(hidden[...], fc1[...]) + bias[...]
+    inner = gelu_coef * (up + 0.044715 * up * up * up)
+    bent = jnp.tanh(inner)
+    act[...] = (0.5 * up * (1.0 + bent)).astype(jnp.bfloat16)
+    slope = 0.5 * (1.0 + bent) + 0.5 * up * (1.0 - bent * bent) * gelu_coef * (
+        1.0 + 3.0 * 0.044715 * up * up
+    )
+    back = (nt(cot[...], fc2[...]) * slope).astype(jnp.bfloat16)
+    grad[...] = back
+
+    @pl.when(pl.program_id(0) == 0)
+    def _():
+        sums[...] = jnp.zeros_like(sums)
+
+    sums[...] += jnp.sum(back.astype(jnp.float32), axis=0, keepdims=True)
+
+
+def feed(hidden, fc1, bias, cot, fc2):
+    tokens, width = hidden.shape
+    units = fc1.shape[1]
+    block = 256
+    some = lambda n: pl.BlockSpec((block, n), lambda i: (i, 0))
+    whole = lambda *shape: pl.BlockSpec(shape, lambda i: (0, 0))
     return pl.pallas_call(
-        functools.partial(exchange_kernel, spread=False),
-        out_shape=jax.ShapeDtypeStruct((32, n, 128), jnp.float32),
-        in_specs=[pl.BlockSpec(memory_space=pltpu.VMEM)],
-        out_specs=pl.BlockSpec(memory_space=pltpu.VMEM),
-        scratch_shapes=[pltpu.SemaphoreType.DMA((32,)), pltpu.SemaphoreType.DMA((32,))],
-        compiler_params=pltpu.CompilerParams(collective_id=0, has_side_effects=True),
-    )(values[None])
+        feed_kernel,
+        grid=(tokens // block,),
+        in_specs=[some(width), whole(width, units), whole(1, units), some(width), whole(units, width)],
+        out_specs=[some(units), some(units), whole(1, units)],
+        out_shape=[
+            jax.ShapeDtypeStruct((tokens, units), jnp.bfloat16),
+            jax.ShapeDtypeStruct((tokens, units), jnp.bfloat16),
+            jax.ShapeDtypeStruct((1, units), jnp.float32),
+        ],
+        compiler_params=pltpu.CompilerParams(vmem_limit_bytes=48 * 2**20),
+        cost_estimate=pl.CostEstimate(
+            flops=4 * tokens * width * units, bytes_accessed=32 * 2**20, transcendentals=tokens * units
+        ),
+    )(hidden, fc1, bias, cot, fc2)
+
+
+W_PEERS = [(k // 4, k // 2 % 2, k % 2) for k in range(1, 8)]
+
+
+def front_kernel(*refs, direct, spread, onward, width):
+    f32, bf16 = jnp.float32, jnp.bfloat16
+    n_in = 3 + direct + spread
+    small, tokens, cot = refs[:3]
+    whole_w, spread_w = refs[3 : 3 + direct], refs[3 + direct : n_in]
+    small_all, hidden_all, cot_all = refs[n_in : n_in + 3]
+    whole_m = refs[n_in + 3 : n_in + 3 + direct]
+    spread_m = refs[n_in + 3 + direct : 2 * n_in]
+    hidden, send_sem, recv_sem, local_sem, small_send, small_recv = refs[2 * n_in :]
+    zh, zl, y, x, c = place = [lax.axis_index(name) for name in FINE]
+    me = (((zh * 2 + zl) * 2 + y) * 2 + x) * 2 + c
+    names = dict(zip(FINE, place))
+    started, used, used_local = [], [0], [0]
+
+    def away(k):
+        return tuple((p + k // 2 ** (4 - i)) % 2 for i, p in enumerate(place))
+
+    def send(src, dst, target):
+        copy = pltpu.make_async_remote_copy(
+            src_ref=src,
+            dst_ref=dst,
+            send_sem=send_sem.at[used[0]],
+            recv_sem=recv_sem.at[used[0]],
+            device_id=target,
+            device_id_type=MESH_ID,
+        )
+        used[0] += 1
+        copy.start()
+        started.append(copy)
+        return copy
+
+    def swap_with(src, dst, axis):
+        return send(src, dst, tuple(1 - p if name == axis else p for name, p in zip(FINE, place)))
+
+    def keep(src, dst):
+        copy = pltpu.make_async_copy(src, dst, local_sem.at[used_local[0]])
+        used_local[0] += 1
+        copy.start()
+        return copy
+
+    barrier = pltpu.get_barrier_semaphore()
+
+    def greet(k, carry):
+        pl.semaphore_signal(barrier, inc=1, device_id=away(k), device_id_type=MESH_ID)
+        return carry
+
+    lax.fori_loop(1, 32, greet, 0)
+    pl.semaphore_wait(barrier, 31)
+
+    def small_copy(k):
+        return pltpu.make_async_remote_copy(
+            src_ref=small,
+            dst_ref=small_all.at[me],
+            send_sem=small_send.at[k],
+            recv_sem=small_recv.at[k],
+            device_id=away(k),
+            device_id_type=MESH_ID,
+        )
+
+    def small_start(k, carry):
+        small_copy(k).start()
+        return carry
+
+    def small_wait(k, carry):
+        small_copy(k).wait()
+        return carry
+
+    lax.fori_loop(1, 32, small_start, 0)
+    small_all[me] = small[...]
+
+    columns, kept = [], []
+    for weight, matrix, goes in zip(spread_w, spread_m, onward):
+        pieces = []
+        for dl, dx, dc in W_PEERS:
+            where = (zh, (zl + dl) % 2, y, (x + dx) % 2, (c + dc) % 2)
+            pieces.append(
+                send(
+                    weight.at[(where[1] * 2 + where[3]) * 2 + where[4]],
+                    matrix.at[zh, zl, y, x * 2 + c] if goes else matrix.at[zl, x * 2 + c],
+                    where,
+                )
+            )
+        own = keep(
+            weight.at[(zl * 2 + x) * 2 + c],
+            matrix.at[zh, zl, y, x * 2 + c] if goes else matrix.at[zl, x * 2 + c],
+        )
+        columns.append((pieces, own))
+    direct_zh = []
+    for weight, matrix in zip(whole_w, whole_m):
+        direct_zh.append(swap_with(weight, matrix.at[zh, y], "zh"))
+        swap_with(weight, matrix.at[zh, y], "y")
+        kept.append(keep(weight, matrix.at[zh, y]))
+    cot_zl = swap_with(cot, cot_all.at[zl, x, c], "zl")
+    cot_x = swap_with(cot, cot_all.at[zl, x, c], "x")
+    cot_c = swap_with(cot, cot_all.at[zl, x, c], "c")
+    kept.append(keep(cot, cot_all.at[zl, x, c]))
+
+    lax.fori_loop(1, 32, small_wait, 0)
+    rows_of = lax.broadcasted_iota(jnp.int32, (32, width), 0)
+    lanes_of = lax.broadcasted_iota(jnp.int32, (32, width), 1)
+    in_place = lanes_of // (width // 32) == rows_of
+
+    def vector(row):
+        part = small_all[:, row, :]
+        spread_out = jnp.concatenate([part] * (width // 128), axis=1)
+        return jnp.sum(jnp.where(in_place, spread_out, 0.0), axis=0, keepdims=True)
+
+    gain, shift = vector(0), vector(1)
+
+    def norm_rows(i, carry):
+        rows = pl.ds(pl.multiple_of(i * 32, 32), 32)
+        values = tokens[rows].astype(f32)
+        centered = values - jnp.mean(values, axis=-1, keepdims=True)
+        variance = jnp.mean(centered * centered, axis=-1, keepdims=True)
+        hidden[rows] = (centered * lax.rsqrt(variance + eps_norm) * gain + shift).astype(bf16)
+        return carry
+
+    lax.fori_loop(0, tokens.shape[0] // 32, norm_rows, 0)
+    hid_zl = swap_with(hidden, hidden_all.at[zl, x, c], "zl")
+    hid_x = swap_with(hidden, hidden_all.at[zl, x, c], "x")
+    hid_c = swap_with(hidden, hidden_all.at[zl, x, c], "c")
+    kept.append(keep(hidden, hidden_all.at[zl, x, c]))
+
+    def forward_columns(i):
+        pieces, own = columns[i]
+        for piece in pieces:
+            piece.wait_recv()
+        own.wait()
+        waits = []
+        if not onward[i]:
+            return waits
+        for half in range(2):
+            block = spread_m[i].at[zh, half, y]
+            waits.append(swap_with(block, block, "zh"))
+            swap_with(block, block, "y")
+        return waits
+
+    def forward_zh(copies, blocks):
+        for copy, block in zip(copies, blocks):
+            copy.wait_recv()
+            swap_with(block, block, "y")
+        return copies
+
+    def halves(i):
+        return [spread_m[i].at[1 - zh, half, y] for half in range(2)]
+
+    received = []
+    columns_zh = [forward_columns(0)]
+    cot_zl.wait_recv()
+    block = cot_all.at[1 - zl, x, c]
+    cot_zx = swap_with(block, block, "x")
+    cot_zc = swap_with(block, block, "c")
+    columns_zh += [forward_columns(i) if onward[i] else [] for i in range(1, spread)]
+    hid_zl.wait_recv()
+    block = hidden_all.at[1 - zl, x, c]
+    hid_zx = swap_with(block, block, "x")
+    hid_zc = swap_with(block, block, "c")
+    forward_zh(direct_zh[:1], [whole_m[0].at[1 - zh, y]])
+    received += direct_zh[:1]
+    for copy, where in ((cot_x, cot_all.at[zl, 1 - x, c]), (cot_zx, cot_all.at[1 - zl, 1 - x, c])):
+        copy.wait_recv()
+        swap_with(where, where, "c")
+        received.append(copy)
+    for copy, where in ((hid_x, hidden_all.at[zl, 1 - x, c]), (hid_zx, hidden_all.at[1 - zl, 1 - x, c])):
+        copy.wait_recv()
+        swap_with(where, where, "c")
+        received.append(copy)
+    received += forward_zh(direct_zh[1:], [m.at[1 - zh, y] for m in whole_m[1:]])
+    for i in range(spread):
+        if onward[i]:
+            received += forward_zh(columns_zh[i], halves(i))
+        else:
+            for piece in columns[i][0]:
+                piece.wait_recv()
+            kept.append(columns[i][1])
+        received += columns[i][0]
+    received += [cot_zl, hid_zl]
+    seen = {id(copy) for copy in received}
+    for copy in started:
+        if id(copy) not in seen:
+            copy.wait_recv()
+    for copy in started:
+        copy.wait_send()
+    for copy in kept:
+        copy.wait()
+
+
+def front(small, tokens, cot, whole_w, spread_w, onward):
+    direct, spread = len(whole_w), len(spread_w)
+    n, width, rows = small.shape[0], tokens.shape[1], tokens.shape[0]
+    bf16 = jnp.bfloat16
+    n_copies = spread * 7 + sum(onward) * 6 + direct * 3 + 14
+    n_local = spread + direct + 2
+    hbm, vmem = pl.BlockSpec(memory_space=pl.ANY), pl.BlockSpec(memory_space=pltpu.VMEM)
+    shapes = [
+        jax.ShapeDtypeStruct((32, n, 128), jnp.float32),
+        jax.ShapeDtypeStruct((2, 2, 2, rows, width), bf16),
+        jax.ShapeDtypeStruct((2, 2, 2, rows, width), bf16),
+    ]
+    shapes += [jax.ShapeDtypeStruct((2, 2) + w.shape, bf16) for w in whole_w]
+    shapes += [
+        jax.ShapeDtypeStruct(((2, 2, 2, 4) if goes else (2, 4)) + w.shape[1:], bf16)
+        for w, goes in zip(spread_w, onward)
+    ]
+    return pl.pallas_call(
+        functools.partial(
+            front_kernel, direct=direct, spread=spread, onward=onward, width=width
+        ),
+        out_shape=shapes,
+        in_specs=[vmem, vmem, hbm] + [hbm] * (direct + spread),
+        out_specs=[vmem] + [hbm] * (2 + direct + spread),
+        scratch_shapes=[
+            pltpu.VMEM((rows, width), bf16),
+            pltpu.SemaphoreType.DMA((n_copies,)),
+            pltpu.SemaphoreType.DMA((n_copies,)),
+            pltpu.SemaphoreType.DMA((n_local,)),
+            pltpu.SemaphoreType.DMA((32,)),
+            pltpu.SemaphoreType.DMA((32,)),
+        ],
+        compiler_params=pltpu.CompilerParams(
+            collective_id=0, has_side_effects=True, vmem_limit_bytes=24 * 2**20
+        ),
+    )(small, tokens, cot, *whole_w, *spread_w)
 
 
 def sum_small(values, collective_id):
@@ -598,6 +841,307 @@
         ],
         compiler_params=pltpu.CompilerParams(collective_id=collective_id, has_side_effects=True),
     )(values)
+
+
+def back_kernel(
+    gqkv, gup, attn, act, qkv_hbm, fc1_hbm, out_hbm, fc2_hbm, fc2_part, fc1_part, out_part, qkv_part,
+    gh_own, br_own, fc2_out, out_out, fc1_out, qkv_out, c_got, w_got, wide_y, wide_z, cols_y, cols_z,
+    qkv_w, fc1_w, out_w, fc2_w, mine, sent, stage, full, wide, cols, wide_s, cols_s, fc1_a, qkv_a,
+    send_sem, recv_sem, local_sem, c_send, c_recv,
+):
+    f32, bf16 = jnp.float32, jnp.bfloat16
+    zh, zl, y, x, c = place = [lax.axis_index(name) for name in FINE]
+    used, used_local = [0], [0]
+    sends = []
+
+    def remote(src, dst, target):
+        copy = pltpu.make_async_remote_copy(
+            src_ref=src,
+            dst_ref=dst,
+            send_sem=send_sem.at[used[0]],
+            recv_sem=recv_sem.at[used[0]],
+            device_id=target,
+            device_id_type=MESH_ID,
+        )
+        used[0] += 1
+        copy.start()
+        sends.append(copy)
+        return copy
+
+    def partner(axis):
+        return tuple(1 - p if name == axis else p for name, p in zip(FINE, place))
+
+    def local(src, dst):
+        copy = pltpu.make_async_copy(src, dst, local_sem.at[used_local[0]])
+        used_local[0] += 1
+        copy.start()
+        return copy
+
+    def load(*pairs):
+        copies = [local(src, dst) for src, dst in pairs]
+        for copy in copies:
+            copy.wait()
+
+    barrier = pltpu.get_barrier_semaphore()
+    peers = [(zh, (zl + dl) % 2, y, (x + dx) % 2, (c + dc) % 2) for dl, dx, dc in W_PEERS]
+    for where in peers + [partner("zh"), partner("y")]:
+        pl.semaphore_signal(barrier, inc=1, device_id=where, device_id_type=MESH_ID)
+    pl.semaphore_wait(barrier, 9)
+
+    gh_weights = [local(qkv_hbm, qkv_w), local(fc1_hbm, fc1_w)]
+    br_weights = [local(out_hbm, out_w), local(fc2_hbm, fc2_w)]
+
+    def row_job(part, rows, first, slot, put):
+        some = pl.ds(0, rows)
+        return dict(
+            part=lambda a, b: part.at[a, b, pl.ds(first, rows)],
+            y=[wide_y.at[slot, j, some] for j in range(2)],
+            z=wide_z.at[slot, some],
+            v=[wide.at[j, some] for j in range(3)],
+            s=wide_s.at[slot, some],
+            put=put,
+            rows=some,
+        )
+
+    def column_job(part, width, away, slot, to):
+        lanes = pl.ds(0, width)
+        return dict(
+            part=lambda a, b: part.at[a, (zl + away) % 2, b],
+            y=[cols_y.at[slot, j, :, lanes] for j in range(2)],
+            z=cols_z.at[slot, :, lanes],
+            v=[cols.at[j, :, lanes] for j in range(3)],
+            s=cols_s.at[slot, :, lanes],
+            away=away,
+            to=to,
+        )
+
+    fc1_width, qkv_width = fc1_w.shape[1], qkv_w.shape[1]
+    out_rows, fc2_rows = out_part.shape[2], fc2_part.shape[2] // 2
+    jobs = [
+        row_job(fc2_part, fc2_rows, i * fc2_rows, i, fc2_out.at[pl.ds(i * fc2_rows, fc2_rows)])
+        for i in range(2)
+    ]
+    jobs += [column_job(fc1_part, fc1_width, away, away, fc1_a) for away in (1, 0)]
+    jobs += [row_job(out_part, out_rows, 0, 2, out_out)]
+    jobs += [column_job(qkv_part, qkv_width, away, 2 + away, qkv_a) for away in (1, 0)]
+    for job in jobs:
+        job["y_far"] = remote(job["part"](1 - zh, 1 - y), job["y"][1], partner("y"))
+        job["y_own"] = remote(job["part"](zh, 1 - y), job["y"][0], partner("y"))
+
+    def pass_on(job):
+        job["y_far"].wait_recv()
+        v = job["v"]
+        load((job["part"](1 - zh, y), v[0]), (job["y"][1], v[1]))
+        job["s"][...] = (v[0][...].astype(f32) + v[1][...].astype(f32)).astype(bf16)
+        job["z_copy"] = remote(job["s"], job["z"], partner("zh"))
+
+    arrivals, kept = [], []
+
+    def finish(job):
+        job["y_own"].wait_recv()
+        job["z_copy"].wait_recv()
+        v = job["v"]
+        load((job["part"](zh, y), v[0]), (job["y"][0], v[1]), (job["z"], v[2]))
+        total = v[0][...].astype(f32) + v[1][...].astype(f32) + v[2][...].astype(f32)
+        if "put" in job:
+            full[job["rows"]] = total
+            load((full.at[job["rows"]], job["put"]))
+            return
+        job["z_copy"].wait_send()
+        sends[:] = [copy for copy in sends if copy is not job["z_copy"]]
+        job["s"][...] = total.astype(bf16)
+        piece = job["s"].shape[0] // 4
+        for dx in range(2):
+            for dc in range(2):
+                where = (zh, (zl + job["away"]) % 2, y, (x + dx) % 2, (c + dc) % 2)
+                row = pl.multiple_of((where[3] * 2 + where[4]) * piece, piece)
+                src = job["s"].at[pl.ds(row, piece)]
+                dst = job["to"].at[(zl * 2 + x) * 2 + c]
+                if job["away"] or dx or dc:
+                    arrivals.append(remote(src, dst, where))
+                else:
+                    kept.append(local(src, dst))
+
+    def core_copy(n, g):
+        return pltpu.make_async_remote_copy(
+            src_ref=sent.at[n, g],
+            dst_ref=c_got.at[n, g],
+            send_sem=c_send.at[n, g],
+            recv_sem=c_recv.at[n, g],
+            device_id=partner("c"),
+            device_id_type=MESH_ID,
+        )
+
+    axes = (("x", "zl"), ("zl", "x"))
+
+    def multiply_groups(n, first, a, v, b, w, multiply):
+        def step(g, carry):
+            one, two = 1 - g // 2, 1 - g % 2
+            dl, dx = (two, one) if n == 0 else (one, two)
+            rest = ((zl + dl) % 2 * 2 + (x + dx) % 2) * 2
+
+            def block(where):
+                rows = pl.ds(pl.multiple_of((rest + where) * 256, 256), 256)
+                return (multiply(a[rows], v[...]) + multiply(b[rows], w[...])).astype(bf16)
+
+            sent[n, g] = block(1 - c)
+            core_copy(n, g).start()
+            mine[n, g] = block(c)
+            return carry
+
+        lax.fori_loop(first, first + 2, step, 0)
+
+    def add(n, g, got):
+        load((got, stage))
+        mine[n, g] = (mine[n, g].astype(f32) + stage[...].astype(f32)).astype(bf16)
+
+    def add_core(n, g):
+        core_copy(n, g).wait_recv()
+        add(n, g, c_got.at[n, g])
+
+    first_copies, second_copies = {}, {}
+
+    def send_first(n):
+        for g in range(2):
+            add_core(n, g)
+            first_copies[n, g] = remote(mine.at[n, g], w_got.at[n, g], partner(axes[n][0]))
+
+    def send_second(n):
+        first_copies[n, 0].wait_recv()
+        add(n, 2, w_got.at[n, 0])
+        second_copies[n] = remote(mine.at[n, 2], w_got.at[n, 2], partner(axes[n][1]))
+
+    def add_first(n):
+        first_copies[n, 1].wait_recv()
+        add(n, 3, w_got.at[n, 1])
+
+    def total(n, out):
+        second_copies[n].wait_recv()
+        load((w_got.at[n, 2], stage))
+        full[...] = mine[n, 3].astype(f32) + stage[...].astype(f32)
+        load((full, out))
+
+    for copy in gh_weights:
+        copy.wait()
+    multiply_groups(0, 0, gqkv, qkv_w, gup, fc1_w, nt)
+    send_first(0)
+    for copy in br_weights:
+        copy.wait()
+    multiply_groups(1, 0, attn, out_w, act, fc2_w, nn)
+    send_first(1)
+    pass_on(jobs[0])
+    multiply_groups(0, 2, gqkv, qkv_w, gup, fc1_w, nt)
+    multiply_groups(1, 2, attn, out_w, act, fc2_w, nn)
+    for n in range(2):
+        add_core(n, 2)
+        add_core(n, 3)
+    send_second(0)
+    pass_on(jobs[1])
+    send_second(1)
+    finish(jobs[0])
+    add_first(0)
+    add_first(1)
+    pass_on(jobs[2])
+    finish(jobs[1])
+    total(0, gh_own)
+    total(1, br_own)
+    pass_on(jobs[3])
+    finish(jobs[2])
+    pass_on(jobs[4])
+    pass_on(jobs[5])
+    finish(jobs[3])
+    pass_on(jobs[6])
+    for job in jobs[4:]:
+        finish(job)
+
+    for copy in arrivals:
+        copy.wait_recv()
+    for copy in kept:
+        copy.wait()
+    unit = fc1_width // 4
+    for w in range(8):
+        for t in range(4):
+            at = ((t // 2 * 2 + w // 4) * 2 + t % 2) * 4 * unit + w % 4 * unit
+            fc1_out[:, at : at + unit] = fc1_a[w, :, t * unit : (t + 1) * unit].astype(f32)
+    low = lax.broadcasted_iota(jnp.int32, (1, 128), 1) < HEAD_DIM
+    for part in range(3):
+        for a in range(2):
+            for dl in range(2):
+                for dx in range(2):
+                    at = part * (qkv_width // 3) + a * 128
+                    even, odd = (
+                        qkv_a[dl * 4 + dx * 2 + k, :, at : at + 128].astype(f32) for k in range(2)
+                    )
+                    to = part * (8 * qkv_width // 3) + a * 1024 + dl * 512 + dx * 128
+                    qkv_out[:, to : to + 128] = jnp.where(low, even, pltpu.roll(odd, 64, 1))
+                    qkv_out[:, to + 256 : to + 384] = jnp.where(low, pltpu.roll(even, 64, 1), odd)
+
+    for copy in sends:
+        copy.wait_send()
+    for n in range(2):
+        for g in range(4):
+            core_copy(n, g).wait_send()
+
+
+def back(gqkv, gup, attn, act, qkv_w, fc1_w, out_w, fc2_w, fc2_part, fc1_part, out_part, qkv_part):
+    bf16, f32 = jnp.bfloat16, jnp.float32
+    width = qkv_w.shape[0]
+    block = gqkv.shape[0] // 8
+    rows, ff_rows = out_w.shape[0] // 4, fc2_w.shape[0] // 4
+    fc1_width, qkv_width = fc1_w.shape[1], qkv_w.shape[1]
+    half = ff_rows // 2
+    any_, vmem = pl.BlockSpec(memory_space=pl.ANY), pl.BlockSpec(memory_space=pltpu.VMEM)
+    shapes = [
+        ((block, width), f32, any_),
+        ((block, width), f32, any_),
+        ((ff_rows, width), f32, any_),
+        ((rows, width), f32, any_),
+        ((rows, 8 * fc1_width), f32, vmem),
+        ((rows, 8 * qkv_width), f32, vmem),
+        ((2, 4, block, width), bf16, any_),
+        ((2, 3, block, width), bf16, any_),
+        ((3, 2, half, width), bf16, any_),
+        ((3, half, width), bf16, any_),
+        ((4, 2, 4 * rows, fc1_width), bf16, any_),
+        ((4, 4 * rows, fc1_width), bf16, any_),
+    ]
+    scratch = [
+        pltpu.VMEM(qkv_w.shape, bf16),
+        pltpu.VMEM(fc1_w.shape, bf16),
+        pltpu.VMEM(out_w.shape, bf16),
+        pltpu.VMEM(fc2_w.shape, bf16),
+        pltpu.VMEM((2, 4, block, width), bf16),
+        pltpu.VMEM((2, 4, block, width), bf16),
+        pltpu.VMEM((block, width), bf16),
+        pltpu.VMEM((block, width), f32),
+        pltpu.VMEM((3, half, width), bf16),
+        pltpu.VMEM((3, 4 * rows, fc1_width), bf16),
+        pltpu.VMEM((3, half, width), bf16),
+        pltpu.VMEM((4, 4 * rows, fc1_width), bf16),
+        pltpu.VMEM((8, rows, fc1_width), bf16),
+        pltpu.VMEM((8, rows, qkv_width), bf16),
+        pltpu.SemaphoreType.DMA((48,)),
+        pltpu.SemaphoreType.DMA((48,)),
+        pltpu.SemaphoreType.DMA((96,)),
+        pltpu.SemaphoreType.DMA((2, 4)),
+        pltpu.SemaphoreType.DMA((2, 4)),
+    ]
+    parts = [
+        fc2_part.reshape(2, 2, ff_rows, width),
+        fc1_part.reshape(2, 2, 2, 4 * rows, fc1_width),
+        out_part.reshape(2, 2, rows, width),
+        qkv_part.reshape(2, 2, 2, 4 * rows, qkv_width),
+    ]
+    return pl.pallas_call(
+        back_kernel,
+        out_shape=[jax.ShapeDtypeStruct(shape, kind) for shape, kind, _ in shapes],
+        in_specs=[vmem] * 4 + [any_] * 8,
+        out_specs=[spec for _, _, spec in shapes],
+        scratch_shapes=scratch,
+        compiler_params=pltpu.CompilerParams(
+            collective_id=2, has_side_effects=True, vmem_limit_bytes=62 * 2**20
+        ),
+    )(gqkv, gup, attn, act, qkv_w, fc1_w, out_w, fc2_w, *parts)[:6]
 
 
 def split_device(
@@ -626,37 +1170,45 @@
     heads = 4
     own_width = heads * HEAD_DIM
 
+    twice = [jnp.concatenate([v, v]).astype(f32) for v in (ln_gain, ln_bias)]
     small = jnp.concatenate(
-        [v.astype(f32) for v in (ln_gain, ln_bias, b_qkv, b_out, b_fc1, b_fc2, lengths)]
+        twice + [v.astype(f32) for v in (b_qkv, b_out, b_fc1, b_fc2, lengths)]
     )
     filled = -(-small.shape[0] // 128) * 128
     small = jnp.pad(small, (0, filled - small.shape[0])).reshape(-1, 128)
-    small_all = gather_small(small).reshape(32, filled)
-    ends = np.cumsum([rows, rows, 3 * rows, rows, ff_rows, rows, 1])
-    gain_all, shift_all, bqkv_all, bout_all, bfc1_all, bfc2_all, lengths_all = (
-        part.reshape(-1) for part in jnp.split(small_all, ends, axis=1)[:-1]
+    places = (x * 2 + c) * local_len + jnp.arange(local_len, dtype=jnp.int32)
+    grad_own = jnp.where((places < lengths[0])[:, None], cotangent[0], jnp.zeros((), bf16))
+    fc1_spread = (
+        w_fc1.reshape((rows, 2, 2, 2, 2, 2, ff_rows))
+        .transpose(2, 4, 5, 0, 1, 3, 6)
+        .reshape(8, rows, -1)
+    )
+    qkv_spread = (
+        w_qkv.reshape((rows, 3, 2, 2, 2, 2, 2, HEAD_DIM))
+        .transpose(3, 5, 6, 0, 1, 2, 4, 7)
+        .reshape(8, rows, -1)
+    )
+    small_all, hidden, grad_out, fc2_mat, fc1_mat, qkv_own = front(
+        small, tokens[0], grad_own, [w_fc2], [fc1_spread, qkv_spread], (True, False)
+    )
+    hidden, grad_out = hidden.reshape(-1, width), grad_out.reshape(-1, width)
+    fc2_mat, fc1_mat = fc2_mat.reshape(-1, width), fc1_mat.reshape(width, -1)
+    qkv_got = gather_blocks(after(qkv_own.reshape(8 * rows, -1), fc2_mat))
+    out_got = gather_blocks(after(w_out, fc2_mat))
+    small_all = small_all.reshape(32, filled)
+    ends = np.cumsum([2 * rows, 2 * rows, 3 * rows, rows, ff_rows, rows, 1])
+    gain_all, shift_all, bqkv_all, bout_all, bfc1_all, bfc2_all, lengths_all = jnp.split(
+        small_all, ends, axis=1
+    )[:-1]
+    gain_all = gain_all[:, :rows].reshape(-1)
+    bqkv_all, bout_all, bfc1_all, bfc2_all = (
+        part.reshape(-1) for part in (bqkv_all, bout_all, bfc1_all, bfc2_all)
     )
     pair_lengths = lax.dynamic_index_in_dim(
         lengths_all.reshape(2, 2, 2, 4)[:, :, :, 0].transpose(0, 2, 1).reshape(4, 2),
         zh * 2 + y,
         keepdims=False,
     ).astype(jnp.int32)
-
-    def own_columns(weight, shape, order):
-        spread = weight.reshape((rows,) + shape).transpose(order)
-        spread = spread.reshape(8, rows, -1)
-        return lax.all_to_all(spread, ROWS_AXES, 0, 0, tiled=True).reshape(8 * rows, -1)
-
-    qkv_own = own_columns(w_qkv, (3, 2, 2, 2, 2, 2, HEAD_DIM), (3, 5, 6, 0, 1, 2, 4, 7))
-    fc1_own = own_columns(w_fc1, (2, 2, 2, 2, 2, ff_rows), (2, 4, 5, 0, 1, 3, 6))
-    out_blocks = by_place(gather_blocks(w_out), zh, y)
-    qkv_blocks = gather_blocks(qkv_own)
-    fc2_blocks = by_place(gather_blocks(w_fc2), zh, y)
-    fc1_blocks = gather_blocks(fc1_own)
-    out_mat = jnp.concatenate(out_blocks, axis=0)
-    fc2_mat = jnp.concatenate(fc2_blocks, axis=0)
-    qkv_mat = natural_rows(by_place(qkv_blocks, zh, y))
-    fc1_mat = natural_rows(by_place(fc1_blocks, zh, y))
 
     inputs = tokens[0].astype(f32)
     average = jnp.mean(inputs, axis=-1, keepdims=True)
@@ -664,12 +1216,6 @@
     variance = jnp.mean(centered * centered, axis=-1, keepdims=True)
     inv_std = lax.rsqrt(variance + eps_norm)
     normed = centered * inv_std
-    hidden_own = (normed * gain_all + shift_all).astype(bf16)
-
-    hidden = lax.all_gather(hidden_own, ROWS_AXES, axis=0, tiled=True)
-    places = (x * 2 + c) * local_len + jnp.arange(local_len, dtype=jnp.int32)
-    grad_own = jnp.where((places < lengths[0])[:, None], cotangent[0], jnp.zeros((), bf16))
-    grad_out = lax.all_gather(grad_own, ROWS_AXES, axis=0, tiled=True)
 
     bqkv = lax.dynamic_index_in_dim(
         bqkv_all.reshape(3, 2, 2, 2, 4, HEAD_DIM).transpose(2, 4, 0, 1, 3, 5).reshape(8, -1),
@@ -682,6 +1228,13 @@
         keepdims=False,
     )
 
+    activated, grad_up, grad_up_sum = feed(hidden, fc1_mat, bfc1[None], grad_out, fc2_mat)
+
+    fc2_part = dot(activated, grad_out, ((0,), (0,))).astype(bf16)
+    fc1_part = dot(hidden, grad_up, ((0,), (0,))).astype(bf16)
+    qkv_got, out_got = after((qkv_got, out_got), (fc2_part, fc1_part))
+    qkv_mat = natural_rows(by_place(qkv_got, zh, y))
+    out_mat = jnp.concatenate(by_place(out_got, zh, y), axis=0)
     grad_mixed = dot(grad_out, out_mat, ((1,), (1,)))
     qkv = dot(hidden, qkv_mat, ((1,), (0,)))
     cosines, sines = tables(total_len, ROT)
@@ -689,23 +1242,23 @@
         pair_lengths, qkv, bqkv[None], grad_mixed, cosines, sines
     )
     attn_mixed, grad_qkv = attn_mixed.astype(bf16), grad_qkv.astype(bf16)
-
-    up_proj = dot(hidden, fc1_mat, ((1,), (0,))) + bfc1
-    activated = gelu_tanh(up_proj).astype(bf16)
-    branch = dot(attn_mixed, out_mat, ((1,), (0,))) + dot(activated, fc2_mat, ((1,), (0,)))
-    branch_own = lax.psum_scatter(
-        branch.astype(bf16), ROWS_AXES, scatter_dimension=0, tiled=True
-    ).astype(f32)
+    qkv_part = dot(hidden, grad_qkv, ((0,), (0,))).astype(bf16)
+    out_part = dot(attn_mixed, grad_out, ((0,), (0,))).astype(bf16)
+    grad_hidden_own, branch_own, grad_fc2, grad_wout, grad_wfc1, grad_wqkv = back(
+        grad_qkv,
+        grad_up,
+        attn_mixed,
+        activated,
+        qkv_mat,
+        fc1_mat,
+        out_mat,
+        fc2_mat,
+        fc2_part,
+        fc1_part,
+        out_part,
+        qkv_part,
+    )
     output = (inputs + branch_own + bout_all + bfc2_all).astype(bf16)[None]
-
-    grad_act = dot(grad_out, fc2_mat, ((1,), (1,)))
-    _, gelu_pull = jax.vjp(gelu_tanh, up_proj)
-    grad_up = gelu_pull(grad_act)[0].astype(bf16)
-
-    grad_hidden = dot(grad_qkv, qkv_mat, ((1,), (1,))) + dot(grad_up, fc1_mat, ((1,), (1,)))
-    grad_hidden_own = lax.psum_scatter(
-        grad_hidden.astype(bf16), ROWS_AXES, scatter_dimension=0, tiled=True
-    ).astype(f32)
     grad_norm = grad_hidden_own * gain_all
     grad_input = grad_own.astype(f32) + inv_std * (
         grad_norm
@@ -713,28 +1266,6 @@
         - normed * jnp.mean(grad_norm * normed, axis=-1, keepdims=True)
     )
     grad_input = grad_input.astype(bf16)[None]
-
-    def place_blocks(values):
-        return by_place(jnp.split(values, 4, axis=0), zh, y)
-
-    fc2_part = dot(activated, grad_out, ((0,), (0,))).astype(bf16)
-    grad_fc2 = reduce_blocks(place_blocks(fc2_part))
-    fc1_part = dot(hidden, grad_up, ((0,), (0,))).astype(bf16)
-    fc1_total = reduce_blocks(by_place(blocks_of_rows(fc1_part), zh, y)).astype(bf16)
-    out_part = dot(attn_mixed, grad_out, ((0,), (0,))).astype(bf16)
-    grad_wout = reduce_blocks(place_blocks(out_part))
-    qkv_part = dot(hidden, grad_qkv, ((0,), (0,))).astype(bf16)
-    qkv_total = reduce_blocks(by_place(blocks_of_rows(qkv_part), zh, y)).astype(bf16)
-
-    def all_columns(total, shape, order, out_width):
-        spread = lax.all_to_all(total.reshape(8, rows, -1), ROWS_AXES, 0, 0, tiled=True)
-        spread = spread.reshape((2, 2, 2, rows) + shape).transpose(order)
-        return spread.reshape(rows, out_width).astype(f32)
-
-    grad_wfc1 = all_columns(fc1_total, (2, 2, ff_rows), (3, 4, 0, 5, 1, 2, 6), w_fc1.shape[1])
-    grad_wqkv = all_columns(
-        qkv_total, (3, 2, 2, HEAD_DIM), (3, 4, 5, 0, 6, 1, 2, 7), w_qkv.shape[1]
-    )
 
     mine = (jnp.arange(8) == place).astype(f32)
     bqkv_term = (
@@ -744,20 +1275,25 @@
         .reshape(-1)
     )
     bfc1_term = (
-        (jnp.sum(grad_up, axis=0, dtype=f32).reshape(1, 2, 2, ff_rows) * mine[:, None, None, None])
+        (grad_up_sum.reshape(1, 2, 2, ff_rows) * mine[:, None, None, None])
         .reshape(2, 4, 2, 2, ff_rows)
         .transpose(2, 0, 3, 1, 4)
         .reshape(-1)
     )
     bias_term = jnp.sum(grad_own, axis=0, dtype=f32)
-    terms = jnp.concatenate([v.reshape(32, -1) for v in (bqkv_term, bfc1_term, bias_term)], axis=1)
-    sums = sum_small(terms.reshape(32, -1, 128), 1).reshape(-1)
-    grad_bqkv, grad_bfc1, grad_bias = jnp.split(sums, np.cumsum([3 * rows, ff_rows]))
     gain_term = jnp.sum(grad_hidden_own * normed, axis=0)
     shift_term = jnp.sum(grad_hidden_own, axis=0)
-    terms = jnp.concatenate([gain_term.reshape(32, -1), shift_term.reshape(32, -1)], axis=1)
-    sums = sum_small(terms.reshape(32, -1, 128), 2).reshape(-1)
-    grad_gain, grad_shift = jnp.split(sums, [rows])
+    terms = jnp.concatenate(
+        [
+            v.reshape(32, -1)
+            for v in (bqkv_term, bfc1_term, bias_term, gain_term, shift_term)
+        ],
+        axis=1,
+    )
+    sums = sum_small(terms.reshape(32, -1, 128), 1).reshape(-1)
+    grad_bqkv, grad_bfc1, grad_bias, grad_gain, grad_shift = jnp.split(
+        sums, np.cumsum([3 * rows, ff_rows, rows, rows])
+    )
     return (
         output,
         grad_input,

time: 649 us -> 601 us (0.926)
  Pallas kernels: 100 us -> 451 us
  waiting for transfers between devices: 223 us -> 13.1 us
  matrix products: 147 us -> 53 us
  starting transfers between devices: 49.5 us -> 7.06 us
  other arithmetic: 52.2 us -> 21.2 us
  between operations: 15.7 us -> 2.01 us
  local copies, waits for them, and re-layouts: 56.2 us -> 45.7 us
    pallas_call x1 -> x3, Pallas kernels: 12.3 us -> 406 us  [the longest x1 213 us: back(): pl.pallas_call(back_kernel, out_shape=[jax.ShapeDtypeStruct(shape, kind)...]
    ppermute x24 -> x6, waiting for transfers between devices: 206 us -> 13.1 us  [swap(): return lax.ppermute(values, axis, [(0, 1), (1, 0)])]
    dot_general x12 -> x6, matrix products: 147 us -> 53 us  [dot(): lax.dot_general(left, right, (dims, ((), ())), preferred_element_type=jnp...]
    pallas_call x2 -> x1, Pallas kernels: 53.4 us -> 10.9 us  [sum_small(): pl.pallas_call(sum_kernel, out_shape=jax.ShapeDtypeStruct((n, 128), jnp.f...]
    convert_element_type x6 -> x0, local copies, waits for them, and re-layouts: 21.6 us -> none  [all_columns(): return spread.reshape(rows, out_width).astype(f32)]
    ppermute x24 -> x6, starting transfers between devices: 28.1 us -> 7.06 us  [swap(): return lax.ppermute(values, axis, [(0, 1), (1, 0)])]
    all_to_all x4 -> x0, starting transfers between devices: 21 us -> none  [the longest x2 12.5 us: all_columns(): lax.all_to_all(total.reshape(8, rows, -1), ROWS_AXES, 0, 0, tiled=True)]
    all_to_all x4 -> x0, waiting for transfers between devices: 17.2 us -> none  [the longest x2 17.2 us: own_columns(): lax.all_to_all(spread, ROWS_AXES, 0, 0, tiled=True).reshape(8 * rows, -1)]
  transfers between devices with their start and end apart: 32 -> 6, of which waited for: 11 -> 1; matrix products, arithmetic and copies ran while one was open for 27% -> 5% of each run, Pallas kernels for 8% -> 4%
where the time goes in v3:
time: 601 us; the launch traced here: 593 us
  Pallas kernels  451 us (75%)
  matrix products  53 us (9%)
  local copies, waits for them, and re-layouts  45.7 us (8%)
  other arithmetic  21.2 us (4%)
  waiting for transfers between devices  13.1 us (2%)
  starting transfers between devices  7.06 us (1%)
    pallas_call x1, Pallas kernels, back(): pl.pallas_call(back_kernel, out_shape=[jax.ShapeDtypeStruct(shape, kind)...  213 us
    pallas_call x1, Pallas kernels, front(): pl.pallas_call(functools.partial(front_kernel, direct=direct, spread=spre...  168 us
    dot_general x6, matrix products, dot(): lax.dot_general(left, right, (dims, ((), ())), preferred_element_type=jnp...  53 us
    pallas_call x1, Pallas kernels, attention(): pl.pallas_call(functools.partial(attention_kernel, total=total, pairs=pai...  34.1 us
    pallas_call x1, Pallas kernels, feed(): pl.pallas_call(feed_kernel, grid=(tokens // block,), in_specs=[some(width...  24.9 us
    unnamed x65, local copies, waits for them, and re-layouts  19 us
    ppermute x6, waiting for transfers between devices, swap(): return lax.ppermute(values, axis, [(0, 1), (1, 0)])  13.1 us
  transfers between devices with their start and end apart: 6, of which 1 were waited for; matrix products, arithmetic and copies ran while one was open for 5% of the time, Pallas kernels for 4%

profile of v3, /device:TPU:0, one launch (start us, length us, event | category | flops | bytes accessed | tf_op | source)
XLA Modules:
  0.0 592.8 jit_solution(745832209111087973)
XLA Ops:
  1.3 0.8 maximum_convert_fusion
  2.1 2.7 concatenate.26
  4.9 1.9 reshape.162
  6.8 0.8 copy.50
  7.6 0.8 reshape.163.refs_4_
  8.4 2.5 reshape.164
  10.9 3.9 copy.49
  14.7 3.6 reshape.165.refs_5_
  18.4 1.6 convert_reduce_fusion.1
  20.0 1.6 copy-done.8
  21.6 168.2 %shard_map.220 = (f32[32,7,128]{2,1,0:T(8,128)S(1)}, bf16[2,2,2,256,2048]{4,3,2,1,0:T(8,128)(2,1)S(1)}, bf16[2,2,2,256,2048]{4,3,2,1,0:T(8,128)(2,1)S(1)}, bf16[...) custom-call(f32[7,128]{1,0:T(8,128)S(1)} %pad_bitcast_fusion.refs_0_,, ...), custom_call_target="tpu_custom_call" | custom-call | tf_op jit(solution)/shard_map/pallas_call | solution.py:809
  189.8 3.2 copy-done.1
  193.1 2.0 copy-done.5
  195.0 2.0 copy-done.6
  197.0 3.2 copy-done.11
  200.2 1.4 collective-permute-start.3
  201.7 2.9 collective-permute-start.1
  206.0 24.9 %shard_map.221 = (bf16[2048,1024]{1,0:T(8,128)(2,1)S(1)}, bf16[2048,1024]{1,0:T(8,128)(2,1)}, f32[1,1024]{1,0:T(1,128)S(1)}) custom-call(bf16[2048,2048]{1,0:T(8,128)(2,1)} %bitcast.64, bf16[2048,1024]{1,0:T(8,128)(2,1)} %bitcast.61, f32[1,1024]{1,0:T(1,128)S(1)} %constant_dynamic-slice_fusion.bias, bf16[2048,2048]{1,0:T(8,128)(2,1)} %bitcast.55, ...), custom_call_target="tpu_custom_call" | custom-call | flops 17179869184 | bytes 33554432 | tf_op jit(solution)/shard_map/pallas_call | solution.py:585
  230.9 11.5 %convolution_convert_fusion = bf16[1024,2048]{1,0:T(8,128)(2,1)} fusion(bf16[2048,1024]{1,0:T(8,128)(2,1)S(1)} %get-tuple-element.48.act, bf16[2048,2048]{1,0:T(8,128)(2,1)S(1)} %bitcast.58), kind=kOutput, calls=%fused_computation | convolution fusion | flops 8592031744 | bytes 16777216 | tf_op jit(solution)/shard_map/dot_general | solution.py:376
  242.4 10.9 %convolution_convert_fusion.1 = bf16[2048,1024]{1,0:T(8,128)(2,1)} fusion(bf16[2048,2048]{1,0:T(8,128)(2,1)S(1)} %bitcast.65, bf16[2048,1024]{1,0:T(8,128)(2,1)S(1)} %copy-done.15), kind=kOutput, calls=%fused_computation.1 | convolution fusion | flops 8592031744 | bytes 16777216 | tf_op jit(solution)/shard_map/dot_general | solution.py:376
  254.0 1.5 collective-permute-start.2
  255.5 1.9 multiply_sine_fusion
  259.1 0.7 reduce.10
  259.8 1.7 concatenate.27.cos_ref
  261.8 1.9 concatenate.28.sin_ref
  263.8 13.1 %collective-permute-done.5 = bf16[64,2048]{1,0:T(8,128)(2,1)} collective-permute-done((bf16[64,2048]{1,0:T(8,128)(2,1)}, bf16[64,2048]{1,0:T(8,128)(2,1)}, u32[]{:S(2)}, u32[]{:S(2)}) %collective-permute-start.5) | collective-permute-done | bytes 262176 | tf_op jit(solution)/shard_map/ppermute | solution.py:342
  276.9 1.2 broadcast_select_fusion.15
  278.1 1.1 pad_maximum_fusion.out_hbm
  279.2 6.3 %fusion.17.go_in = f32[2048,256]{1,0:T(8,128)S(1)} fusion(bf16[2048,2048]{1,0:T(8,128)(2,1)} %bitcast.56, bf16[64,2048]{1,0:T(8,128)(2,1)S(1)} %get-tuple-element.83, bf16[64,2048]{1,0:T(8,128)(2,1)S(1)} %get-tuple-element.82, bf16[64,2048]{1,0:T(8,128)(2,1)S(1)} %get-tuple-element.81, bf16[64,2048]{1,0:T(8,128)(2,1)S(1)} %get-tuple-element.80), kind=kOutput, calls=%fused_computation.76 | convolution fusion | flops 2151677952 | bytes 11534336 | tf_op jit(solution)/shard_map/dot_general | solution.py:376
  285.6 2.1 broadcast_select_fusion.4
  288.0 1.6 copy-done.16
  289.6 8.6 %fusion.20.q_in.k_in.v_in = f32[2048,768]{1,0:T(8,128)} fusion(bf16[2048,2048]{1,0:T(8,128)(2,1)S(1)} %bitcast.68, bf16[2048,768]{1,0:T(8,128)(2,1)S(1)} %slice_dynamic-update-slice_fusion.qkv_hbm), kind=kOutput, calls=%fused_computation.79 | convolution fusion | flops 6442450944 | bytes 17825792 | tf_op jit(solution)/shard_map/dot_general | solution.py:376
  298.2 34.1 %shard_map.222 = (f32[2048,256]{1,0:T(8,128)S(1)}, f32[2048,768]{1,0:T(8,128)}, f32[2,1,768]{2,1,0:T(1,128)S(1)}) custom-call(s32[2]{0:T(128)S(1)} %convert_reduce_fusion.2.len_ref, f32[1,768]{1,0:T(1,128)S(1)} %constant_dynamic-slice_fusion.1.bias_ref, f32[1024,128]{1,0:T(8,128)S(1)} %copy-done.9, f32[1024,128]{1,0:T(8,128)S(1)} %copy-done.10, ...), custom_call_target="tpu_custom_call" | custom-call | flops 6442450944 | bytes 20971520 | tf_op jit(solution)/shard_map/pallas_call | solution.py:469
  332.3 3.1 convert_element_type.104.gqkv
  335.4 8.6 %convolution_convert_fusion.2 = bf16[2048,768]{1,0:T(8,128)(2,1)} fusion(bf16[2048,2048]{1,0:T(8,128)(2,1)S(1)} %bitcast.69, bf16[2048,768]{1,0:T(8,128)(2,1)S(1)} %convert_element_type.104.gqkv), kind=kOutput, calls=%fused_computation.2 | convolution fusion | flops 6444023808 | bytes 14680064 | tf_op jit(solution)/shard_map/dot_general | solution.py:376
  344.4 7.1 %convolution_convert_fusion.3 = bf16[256,2048]{1,0:T(8,128)(2,1)} fusion(bf16[2048,256]{1,0:T(8,128)(2,1)S(1)} %convert_element_type.105.attn, bf16[2048,2048]{1,0:T(8,128)(2,1)} %bitcast.57), kind=kOutput, calls=%fused_computation.8 | convolution fusion | flops 2148007936 | bytes 10485760 | tf_op jit(solution)/shard_map/dot_general | solution.py:376
  351.5 212.5 %shard_map.223 = (f32[256,2048]{1,0:T(8,128)}, f32[256,2048]{1,0:T(8,128)}, f32[256,2048]{1,0:T(8,128)}, f32[64,2048]{1,0:T(8,128)}, f32[64,8192]{1,0:T(8,128)},...) custom-call(bf16[2048,768]{1,0:T(8,128)(2,1)} %copy-done.14, ...), custom_call_target="tpu_custom_call" | custom-call | tf_op jit(solution)/shard_map/pallas_call | solution.py:1135
  564.0 2.7 fusion.8
  566.9 0.7 reshape.183.src
  567.6 10.9 %shard_map.224 = f32[5,128]{1,0:T(8,128)} custom-call(f32[32,5,128]{2,1,0:T(8,128)} %reshape.183.src), custom_call_target="tpu_custom_call" | custom-call | tf_op jit(solution)/shard_map/pallas_call | solution.py:832
  578.6 1.2 split.70
  579.8 1.3 split.72
  581.1 1.4 fusion.19
  582.5 5.0 fusion.15
  588.0 1.1 copy.66
  589.1 0.8 copy.67
  589.9 1.3 copy.68
  591.3 1.3 copy.69
  (114 shorter events, 5.5 us)
Async XLA Ops:
  4.9 3.5 copy-start.20
  10.9 9.1 %copy-start = (bf16[1,256,2048]{2,1,0:T(8,128)(2,1)S(1)}, bf16[1,256,2048]{2,1,0:T(8,128)(2,1)}, u32[]{:S(2)}) copy-start(bf16[1,256,2048]{2,1,0:T(8,128)(2,1)} %param.13) | copy-start | bytes 3145732
  18.4 181.8 %copy-start.22 = (bf16[64,2048]{1,0:T(8,128)(2,1)S(1)}, bf16[64,2048]{1,0:T(8,128)(2,1)}, u32[]{:S(2)}) copy-start(bf16[64,2048]{1,0:T(8,128)(2,1)} %param.19) | copy-start | bytes 786436
  20.0 169.8 %copy-start.3 = (bf16[256,2048]{1,0:T(8,128)(2,1)}, bf16[256,2048]{1,0:T(8,128)(2,1)S(1)}, u32[]{:S(2)}) copy-start(bf16[256,2048]{1,0:T(8,128)(2,1)S(1)} %get-tuple-element.73.refs_2_) | copy-start | bytes 3145732
  20.0 1.6 copy-start.8
  189.8 3.2 copy-start.1
  193.0 2.0 copy-start.5
  195.0 2.0 copy-start.6
  197.0 3.2 copy-start.11
  200.2 57.2 %collective-permute-start.4 = (bf16[64,2048]{1,0:T(8,128)(2,1)S(1)}, bf16[64,2048]{1,0:T(8,128)(2,1)}, u32[]{:S(2)}, u32[]{:S(2)}) collective-permute-start(bf16[64,2048]{1,0:T(8,128)(2,1)S(1)} %copy-done.22), channel_id=1, source_target_pairs={{0,16},{16,0},{1,17},{17,1},{2,18},{18,2},{3,19},{19,3},{4,20},{20... | collective-permute-start | bytes 786440 | tf_op jit(solution)/shard_map/ppermute | solution.py:342
  200.2 63.6 %collective-permute-start.3 = (bf16[64,2048]{1,0:T(8,128)(2,1)S(1)}, bf16[64,2048]{1,0:T(8,128)(2,1)}, u32[]{:S(2)}, u32[]{:S(2)}) collective-permute-start(bf16[64,2048]{1,0:T(8,128)(2,1)S(1)} %copy-done.22), channel_id=1, source_target_pairs={{0,4},{4,0},{1,5},{5,1},{2,6},{6,2},{3,7},{7,3},{8,12},{12,8},{9,1... | collective-permute-start | bytes 786440 | tf_op jit(solution)/shard_map/ppermute | solution.py:342
  201.7 52.4 %collective-permute-start.1 = (bf16[512,768]{1,0:T(8,128)(2,1)}, bf16[512,768]{1,0:T(8,128)(2,1)}, u32[]{:S(2)}, u32[]{:S(2)}) collective-permute-start(bf16[512,768]{1,0:T(8,128)(2,1)} %bitcast.9), channel_id=1, source_target_pairs={{0,16},{16,0},{1,17},{17,1},{2,18},{18,2},{3,19},{19,3},{4,20},{20... | collective-permute-start | bytes 2359304 | tf_op jit(solution)/shard_map/ppermute | solution.py:342
  204.6 72.3 %collective-permute-start = (bf16[512,768]{1,0:T(8,128)(2,1)}, bf16[512,768]{1,0:T(8,128)(2,1)}, u32[]{:S(2)}, u32[]{:S(2)}) collective-permute-start(bf16[512,768]{1,0:T(8,128)(2,1)} %bitcast.9), channel_id=1, source_target_pairs={{0,4},{4,0},{1,5},{5,1},{2,6},{6,2},{3,7},{7,3},{8,12},{12,8},{9,1... | collective-permute-start | bytes 2359304 | tf_op jit(solution)/shard_map/ppermute | solution.py:342
  205.9 24.9 %copy-start.2 = (bf16[2,2,2,256,2048]{4,3,2,1,0:T(8,128)(2,1)S(1)}, bf16[2,2,2,256,2048]{4,3,2,1,0:T(8,128)(2,1)}, u32[]{:S(2)}) copy-start(bf16[2,2,2,256,2048]{4,3,2,1,0:T(8,128)(2,1)} %copy-done.1) | copy-start | bytes 25165828
  230.9 11.5 %copy-start.7 = (bf16[2048,1024]{1,0:T(8,128)(2,1)}, bf16[2048,1024]{1,0:T(8,128)(2,1)S(1)}, u32[]{:S(2)}) copy-start(bf16[2048,1024]{1,0:T(8,128)(2,1)S(1)} %get-tuple-element.48.act) | copy-start | bytes 12582916
  230.9 11.5 %copy-start.12 = (bf16[2,2,2,256,2048]{4,3,2,1,0:T(8,128)(2,1)S(1)}, bf16[2,2,2,256,2048]{4,3,2,1,0:T(8,128)(2,1)}, u32[]{:S(2)}) copy-start(bf16[2,2,2,256,2048]{4,3,2,1,0:T(8,128)(2,1)} %copy-done.11) | copy-start | bytes 25165828
  230.9 11.5 %copy-start.15 = (bf16[2048,1024]{1,0:T(8,128)(2,1)S(1)}, bf16[2048,1024]{1,0:T(8,128)(2,1)}, u32[]{:S(2)}) copy-start(bf16[2048,1024]{1,0:T(8,128)(2,1)} %get-tuple-element.49.gup) | copy-start | bytes 12582916
  254.0 22.9 %collective-permute-start.2 = (bf16[512,768]{1,0:T(8,128)(2,1)}, bf16[512,768]{1,0:T(8,128)(2,1)}, u32[]{:S(2)}, u32[]{:S(2)}) collective-permute-start(bf16[512,768]{1,0:T(8,128)(2,1)} %collective-permute-done.1), channel_id=1, source_target_pairs={{0,4},{4,0},{1,5},{5,1},{2,6},{6,2},{3,7},{7,3},{8,12},{12,8},{9,1... | collective-permute-start | bytes 2359304 | tf_op jit(solution)/shard_map/ppermute | solution.py:342
  257.4 19.5 %collective-permute-start.5 = (bf16[64,2048]{1,0:T(8,128)(2,1)}, bf16[64,2048]{1,0:T(8,128)(2,1)}, u32[]{:S(2)}, u32[]{:S(2)}) collective-permute-start(bf16[64,2048]{1,0:T(8,128)(2,1)} %collective-permute-done.4), channel_id=1, source_target_pairs={{0,4},{4,0},{1,5},{5,1},{2,6},{6,2},{3,7},{7,3},{8,12},{12,8},{9,1... | collective-permute-start | bytes 786440 | tf_op jit(solution)/shard_map/ppermute | solution.py:342
  278.1 11.5 %slice-start = ((s8[8388608]{0:T(1024)(128)(4,1)}), s8[4194304]{0:T(1024)(128)(4,1)S(1)}, s32[]{:S(2)}) async-start(s8[8388608]{0:T(1024)(128)(4,1)} %bitcast.66), calls=%async_computation | async-start | bytes 8388608
  279.2 10.4 %slice-start.1 = ((s8[8388608]{0:T(1024)(128)(4,1)}), s8[4194304]{0:T(1024)(128)(4,1)S(1)}, s32[]{:S(2)}) async-start(s8[8388608]{0:T(1024)(128)(4,1)} %bitcast.66), calls=%async_computation.1 | async-start | bytes 8388608
  287.9 1.6 copy-start.16
  289.6 8.6 %copy-start.9 = (f32[1024,128]{1,0:T(8,128)S(1)}, f32[1024,128]{1,0:T(8,128)}, u32[]{:S(2)}) copy-start(f32[1024,128]{1,0:T(8,128)} %concatenate.27.cos_ref) | copy-start | bytes 1572868
  289.6 8.6 %copy-start.10 = (f32[1024,128]{1,0:T(8,128)S(1)}, f32[1024,128]{1,0:T(8,128)}, u32[]{:S(2)}) copy-start(f32[1024,128]{1,0:T(8,128)} %concatenate.28.sin_ref) | copy-start | bytes 1572868
  335.4 8.6 %copy-start.14 = (bf16[2048,768]{1,0:T(8,128)(2,1)}, bf16[2048,768]{1,0:T(8,128)(2,1)S(1)}, u32[]{:S(2)}) copy-start(bf16[2048,768]{1,0:T(8,128)(2,1)S(1)} %convert_element_type.104.gqkv) | copy-start | bytes 9437188
  344.4 7.1 %copy-start.13 = (bf16[2048,256]{1,0:T(8,128)(2,1)}, bf16[2048,256]{1,0:T(8,128)(2,1)S(1)}, u32[]{:S(2)}) copy-start(bf16[2048,256]{1,0:T(8,128)(2,1)S(1)} %convert_element_type.105.attn) | copy-start | bytes 3145732
  564.0 18.4 %copy-start.4 = (bf16[256,2048]{1,0:T(8,128)(2,1)S(1)}, bf16[256,2048]{1,0:T(8,128)(2,1)}, u32[]{:S(2)}) copy-start(bf16[256,2048]{1,0:T(8,128)(2,1)} %copy-done.3) | copy-start | bytes 3145732
  582.5 5.0 copy-start.23
  582.5 5.5 copy-start.19
  587.5 1.7 copy-start.21
  587.5 2.5 copy-start.18
  589.1 2.1 copy-start.17

commit v4 on v0

--- a/solution.py
+++ b/solution.py
@@ -1,8 +1,12 @@
+import functools
 import math
 
 import jax
 import jax.numpy as jnp
+import numpy as np
 from jax import lax
+from jax.experimental import pallas as pl
+from jax.experimental.pallas import tpu as pltpu
 from jax.sharding import PartitionSpec as P
 
 HEAD_DIM = 64
@@ -292,7 +296,7 @@
     )
 
 
-def solution(mesh):
+def general_solution(mesh):
     placed = (
         P("dp", "ctx", None),
         P("dp"),
@@ -328,3 +332,1057 @@
         ),
         check_vma=False,
     )
+
+
+FINE = ("zh", "zl", "y", "x", "c")
+ROWS_AXES = ("zl", "x", "c")
+
+
+def dot(left, right, dims):
+    return lax.dot_general(left, right, (dims, ((), ())), preferred_element_type=jnp.float32)
+
+
+QB = 256
+
+
+def nt(a, b):
+    return dot(a, b, ((1,), (1,)))
+
+
+def nn(a, b):
+    return dot(a, b, ((1,), (0,)))
+
+
+def tn(a, b):
+    return dot(a, b, ((0,), (0,)))
+
+
+def attend_pair(pair, length, bias, cosines_ref, sines_ref, qkv, mixed, q_s, k_s, v_s, g_s, gk_s, gv_s):
+    f32, bf16 = jnp.float32, jnp.bfloat16
+    total, width = mixed.shape
+    lane = lax.broadcasted_iota(jnp.int32, (1, 128), 1)
+    first = lane % HEAD_DIM < ROT // 2
+    heads = [lane < HEAD_DIM, lane >= HEAD_DIM]
+
+    def other(v):
+        return jnp.where(first, pltpu.roll(v, 128 - ROT // 2, 1), pltpu.roll(v, ROT // 2, 1))
+
+    def col(part):
+        return pl.ds(pl.multiple_of(part * width + pair * 128, 128), 128)
+
+    for b in range(total // QB):
+        rows = pl.ds(b * QB, QB)
+        cosines, sines = cosines_ref[rows], sines_ref[rows]
+
+        def turn(v):
+            return v * cosines + other(v) * sines
+
+        q = turn(qkv[rows, col(0)] + bias[:, col(0)]) * 0.125
+        k = turn(qkv[rows, col(1)] + bias[:, col(1)])
+        v = qkv[rows, col(2)] + bias[:, col(2)]
+        g = mixed[rows, col(0)]
+        for h in range(2):
+            q_s[h, rows] = jnp.where(heads[h], q, 0.0).astype(bf16)
+            k_s[h, rows] = jnp.where(heads[h], k, 0.0).astype(bf16)
+            v_s[h, rows] = jnp.where(heads[h], v, 0.0).astype(bf16)
+            g_s[h, rows] = jnp.where(heads[h], g, 0.0).astype(bf16)
+    gk_s[...] = jnp.zeros_like(gk_s)
+    gv_s[...] = jnp.zeros_like(gv_s)
+
+    for b in range(total // QB):
+        rows = pl.ds(b * QB, QB)
+        upto = (b + 1) * QB
+        keys = pl.ds(0, upto)
+        limit = jnp.minimum(lax.broadcasted_iota(jnp.int32, (1, QB), 1) + (b * QB + 1), length)
+        allowed = lax.broadcasted_iota(jnp.int32, (upto, QB), 0) < limit
+        out = grad = jnp.zeros((QB, 128), f32)
+        for h in range(2):
+            qh, gh = q_s[h, rows], g_s[h, rows]
+            scores = jnp.where(allowed, nt(k_s[h, keys], qh), -1e30)
+            exponent = jnp.exp(scores - jnp.max(scores, axis=0, keepdims=True))
+            share = exponent * (1.0 / jnp.sum(exponent, axis=0, keepdims=True))
+            rounded = share.astype(bf16)
+            back = nt(v_s[h, keys], gh)
+            back = (share * (back - jnp.sum(share * back, axis=0, keepdims=True))).astype(bf16)
+            gv_s[keys] += nn(rounded, gh)
+            gk_s[keys] += nn(back, qh)
+            out += tn(rounded, v_s[h, keys])
+            grad += tn(back, k_s[h, keys])
+        mixed[rows, col(0)] = out
+        grad *= 0.125
+        qkv[rows, col(0)] = grad * cosines_ref[rows] - other(grad) * sines_ref[rows]
+    for b in range(total // QB):
+        rows = pl.ds(b * QB, QB)
+        grad = gk_s[rows]
+        qkv[rows, col(1)] = grad * cosines_ref[rows] - other(grad) * sines_ref[rows]
+        qkv[rows, col(2)] = gv_s[rows]
+
+
+def tables(total, rot):
+    half = rot // 2
+    inv = jnp.exp(-math.log(10000.0) * 2.0 * jnp.arange(half, dtype=jnp.float32) / rot)
+    ang = jnp.arange(total, dtype=jnp.int32).astype(jnp.float32)[:, None] * inv[None, :]
+    c, s = jnp.cos(ang), jnp.sin(ang)
+    one, nil = jnp.ones((total, 64 - rot), jnp.float32), jnp.zeros((total, 64 - rot), jnp.float32)
+    cosines = jnp.concatenate([c, c, one] * 2, axis=1)
+    sines = jnp.concatenate([-s, s, nil] * 2, axis=1)
+    return cosines, sines
+
+
+MESH_ID = pl.DeviceIdType.MESH
+
+
+def exchange_kernel(src, dst, send_sem, recv_sem):
+    place = [lax.axis_index(name) for name in FINE]
+    me = 0
+    for p in place:
+        me = me * 2 + p
+
+    def away(k):
+        return tuple((p + k // 2 ** (4 - i)) % 2 for i, p in enumerate(place))
+
+    def index_of(where):
+        number = 0
+        for p in where:
+            number = number * 2 + p
+        return number
+
+    barrier = pltpu.get_barrier_semaphore()
+
+    def greet(k, carry):
+        pl.semaphore_signal(barrier, inc=1, device_id=away(k), device_id_type=MESH_ID)
+        return carry
+
+    lax.fori_loop(1, 32, greet, 0)
+    pl.semaphore_wait(barrier, 31)
+
+    def copy(k):
+        where = away(k)
+        return pltpu.make_async_remote_copy(
+            src_ref=src.at[index_of(where)],
+            dst_ref=dst.at[me],
+            send_sem=send_sem.at[k],
+            recv_sem=recv_sem.at[k],
+            device_id=where,
+            device_id_type=MESH_ID,
+        )
+
+    def send(k, carry):
+        copy(k).start()
+        return carry
+
+    lax.fori_loop(1, 32, send, 0)
+    dst[me] = src[me]
+
+    def finish(k, carry):
+        copy(k).wait()
+        return carry
+
+    lax.fori_loop(1, 32, finish, 0)
+
+
+def sum_kernel(src, out, dst, send_sem, recv_sem):
+    exchange_kernel(src, dst, send_sem, recv_sem)
+    out[...] = jnp.sum(dst[...], axis=0)
+
+
+W_PEERS = [(k // 4, k // 2 % 2, k % 2) for k in range(1, 8)]
+
+
+def sum_small(values, collective_id):
+    n = values.shape[1]
+    return pl.pallas_call(
+        sum_kernel,
+        out_shape=jax.ShapeDtypeStruct((n, 128), jnp.float32),
+        in_specs=[pl.BlockSpec(memory_space=pltpu.VMEM)],
+        out_specs=pl.BlockSpec(memory_space=pltpu.VMEM),
+        scratch_shapes=[
+            pltpu.VMEM((32, n, 128), jnp.float32),
+            pltpu.SemaphoreType.DMA((32,)),
+            pltpu.SemaphoreType.DMA((32,)),
+        ],
+        compiler_params=pltpu.CompilerParams(collective_id=collective_id, has_side_effects=True),
+    )(values)
+
+
+def main_kernel(
+    small, tokens, cot_own, cosines, sines, fc2_own, out_own, fc1_spread, qkv_spread,
+    gh_own, br_own, fc2_out, out_out, fc1_a, qkv_a, up_sum, qkv_sum, small_all, qkv_all, out_all, fc1_all, fc2_all,
+    fc2_part, fc1_part, out_part, qkv_part, c_got, w_got, wide_y, wide_z, cols_y, cols_z,
+    hidden, cot, act, gup, attn, gqkv, qkv_w, out_w, stage, full, wide, cols, wide_s, cols_s, fc1_bias, qkv_bias,
+    send_sem, recv_sem, local_sem, block_sem, c_send, c_recv, small_send, small_recv,
+):
+    f32, bf16 = jnp.float32, jnp.bfloat16
+    zh, zl, y, x, c = place = [lax.axis_index(name) for name in FINE]
+    seat = (zl * 2 + x) * 2 + c
+    used, used_local = [0], [0]
+    sends = []
+
+    class Copy:
+        def __init__(self, describe):
+            self.describe = describe
+
+        def start(self):
+            self.describe().start()
+
+        def wait(self):
+            self.describe().wait()
+
+        def wait_send(self):
+            self.describe().wait_send()
+
+        def wait_recv(self):
+            self.describe().wait_recv()
+
+    def remote(ends, target):
+        n = used[0]
+        used[0] += 1
+
+        def describe():
+            src, dst = ends()
+            return pltpu.make_async_remote_copy(
+                src_ref=src,
+                dst_ref=dst,
+                send_sem=send_sem.at[n],
+                recv_sem=recv_sem.at[n],
+                device_id=target(),
+                device_id_type=MESH_ID,
+            )
+
+        copy = Copy(describe)
+        copy.start()
+        sends.append(copy)
+        return copy
+
+    def partner(axis):
+        return tuple(1 - p if name == axis else p for name, p in zip(FINE, place))
+
+    def beside():
+        return partner("y")
+
+    def across():
+        return partner("zh")
+
+    def local(ends):
+        n = used_local[0]
+        used_local[0] += 1
+
+        def describe():
+            src, dst = ends()
+            return pltpu.make_async_copy(src, dst, local_sem.at[n])
+
+        copy = Copy(describe)
+        copy.start()
+        return copy
+
+    def load(*pairs):
+        copies = [local(lambda pair=pair: pair) for pair in pairs]
+        for copy in copies:
+            copy.wait()
+
+    def index_of(where):
+        number = 0
+        for p in where:
+            number = number * 2 + p
+        return number
+
+    def away(k):
+        return tuple((p + k // 2 ** (4 - i)) % 2 for i, p in enumerate(place))
+
+    barrier = pltpu.get_barrier_semaphore()
+
+    def greet(k, carry):
+        pl.semaphore_signal(barrier, inc=1, device_id=away(k), device_id_type=MESH_ID)
+        return carry
+
+    lax.fori_loop(1, 32, greet, 0)
+    pl.semaphore_wait(barrier, 31)
+
+    blocks, block_rows, width = hidden.shape
+    token_count, units = gup.shape
+    total_len = token_count // 2
+    mine, sent = hidden, cot
+
+    def small_copy(k):
+        return pltpu.make_async_remote_copy(
+            src_ref=small,
+            dst_ref=small_all.at[index_of(place)],
+            send_sem=small_send.at[k],
+            recv_sem=small_recv.at[k],
+            device_id=away(k),
+            device_id_type=MESH_ID,
+        )
+
+    def small_start(k, carry):
+        small_copy(k).start()
+        return carry
+
+    def small_wait(k, carry):
+        small_copy(k).wait()
+        return carry
+
+    lax.fori_loop(1, 32, small_start, 0)
+    small_all[index_of(place)] = small[...]
+    tokens_in = local(lambda: (tokens, stage))
+
+    def spread(weight, matrix):
+        pieces = []
+        for dl, dx, dc in W_PEERS:
+
+            def where(dl=dl, dx=dx, dc=dc):
+                return zh, (zl + dl) % 2, y, (x + dx) % 2, (c + dc) % 2
+
+            def ends(where=where):
+                _, to_zl, _, to_x, to_c = where()
+                return weight.at[(to_zl * 2 + to_x) * 2 + to_c], matrix.at[zh, zl, y, x * 2 + c]
+
+            pieces.append(remote(ends, where))
+        return pieces, local(lambda: (weight.at[seat], matrix.at[zh, zl, y, x * 2 + c]))
+
+    def parts_of(ends_list):
+        return [remote(ends, across) for ends in ends_list], [remote(ends, beside) for ends in ends_list]
+
+    def forward(copy, block):
+        copy.wait_recv()
+        return remote(lambda: (block(), block()), beside)
+
+    def half_of(matrix, half):
+        return lambda: matrix.at[1 - zh, half, y]
+
+    def own_half(matrix, half):
+        return lambda: (matrix.at[zh, half, y], matrix.at[zh, half, y])
+
+    fc1_pieces = spread(fc1_spread, fc1_all)
+    half_rows = fc2_own.shape[0] // 2
+
+    def fc2_rows_of(a, half):
+        return lambda: fc2_all.at[a, y, pl.ds(half * half_rows, half_rows)]
+
+    def fc2_ends(half):
+        return lambda: (fc2_own.at[pl.ds(half * half_rows, half_rows)], fc2_rows_of(zh, half)())
+
+    def over(own, gathered, axis):
+        return remote(lambda: (own(), gathered()), lambda: partner(axis))
+
+    def own_cot():
+        return cot_own
+
+    def seat_of(array, dl=0, dx=0):
+        return lambda: array.at[((zl + dl) % 2 * 2 + (x + dx) % 2) * 2 + c]
+
+    cot_zl = over(own_cot, seat_of(cot), "zl")
+    fc2_zh, fc2_y = parts_of([fc2_ends(half) for half in range(2)])
+    cot_x = over(own_cot, seat_of(cot), "x")
+    core = [over(own_cot, seat_of(cot), "c")]
+    qkv_pieces = spread(qkv_spread, qkv_all)
+    own_copies = [
+        local(lambda: (cot_own, cot.at[seat])),
+        local(lambda: (fc2_own, fc2_all.at[zh, y])),
+        local(lambda: (out_own, out_all.at[zh, y])),
+    ]
+
+    lax.fori_loop(1, 32, small_wait, 0)
+    tokens_in.wait()
+    in_place = lax.broadcasted_iota(jnp.int32, (32, width), 1) // (width // 32) == (
+        lax.broadcasted_iota(jnp.int32, (32, width), 0)
+    )
+
+    def vector(row):
+        spread_out = jnp.concatenate([small_all[:, row, :]] * (width // 128), axis=1)
+        return jnp.sum(jnp.where(in_place, spread_out, 0.0), axis=0, keepdims=True)
+
+    gain, shift = vector(0), vector(1)
+
+    def norm_rows(i, carry):
+        rows = pl.ds(pl.multiple_of(i * 32, 32), 32)
+        values = stage[rows].astype(f32)
+        centered = values - jnp.mean(values, axis=-1, keepdims=True)
+        variance = jnp.mean(centered * centered, axis=-1, keepdims=True)
+        hidden[seat, rows] = (centered * lax.rsqrt(variance + eps_norm) * gain + shift).astype(bf16)
+        return carry
+
+    lax.fori_loop(0, block_rows // 32, norm_rows, 0)
+    hid_zl = over(seat_of(hidden), seat_of(hidden), "zl")
+    hid_x = over(seat_of(hidden), seat_of(hidden), "x")
+    core.append(over(seat_of(hidden), seat_of(hidden), "c"))
+
+    for t in range(4):
+        owner = index_of((t // 2, zl, t % 2, x, c))
+        for half in range(2):
+            at = t * 2 * 128 + half * 128
+            fc1_bias[:, at : at + 128] = small_all[owner, pl.ds(4 + half, 1), :]
+    low = lax.broadcasted_iota(jnp.int32, (1, 128), 1) < HEAD_DIM
+    for part in range(3):
+        for a in range(2):
+            chunks = []
+            for b in range(2):
+                chunk = part * 32 + index_of((a, zl, b, x, c))
+                row = small_all[chunk // 3, pl.ds(2 + chunk % 3 // 2, 1), :]
+                chunks.append(jnp.where(chunk % 3 % 2 == b, row, pltpu.roll(row, HEAD_DIM, 1)))
+            at = (part * 2 + a) * 128
+            qkv_bias[:, at : at + 128] = jnp.where(low, chunks[0], chunks[1])
+
+    def length_of(seq):
+        row = small_all[index_of((zh, seq, y, 0, 0)), pl.ds(7, 1), :]
+        return jnp.concatenate([row] * (QB // 128), axis=1).astype(jnp.int32)
+
+    def all_there(pieces):
+        for piece in pieces[0]:
+            piece.wait_recv()
+        pieces[1].wait()
+
+    all_there(fc1_pieces)
+    fc1_zh, fc1_y = parts_of([own_half(fc1_all, half) for half in range(2)])
+    cot_zl.wait_recv()
+    cot_zx = over(seat_of(cot, 1), seat_of(cot, 1), "x")
+    core.append(over(seat_of(cot, 1), seat_of(cot, 1), "c"))
+    hid_zl.wait_recv()
+    hid_zx = over(seat_of(hidden, 1), seat_of(hidden, 1), "x")
+    core.append(over(seat_of(hidden, 1), seat_of(hidden, 1), "c"))
+    fc2_fwd = [forward(copy, fc2_rows_of(1 - zh, half)) for half, copy in enumerate(fc2_zh)]
+    all_there(qkv_pieces)
+    out_zh, out_y = parts_of([lambda: (out_own, out_all.at[zh, y])])
+    qkv_zh, qkv_y = parts_of([own_half(qkv_all, half) for half in range(2)])
+    for array, copies in ((cot, ((cot_x, 0), (cot_zx, 1))), (hidden, ((hid_x, 0),))):
+        for copy, dl in copies:
+            copy.wait_recv()
+            core.append(over(seat_of(array, dl, 1), seat_of(array, dl, 1), "c"))
+    fc1_fwd = [forward(copy, half_of(fc1_all, half)) for half, copy in enumerate(fc1_zh)]
+    hid_zx.wait_recv()
+    core.append(over(seat_of(hidden, 1, 1), seat_of(hidden, 1, 1), "c"))
+    for copy in own_copies + core + fc2_y + fc2_fwd + fc1_y + fc1_fwd:
+        if copy in own_copies:
+            copy.wait()
+        else:
+            copy.wait_recv()
+    late_in = out_y + qkv_y
+    early_sends = len(sends)
+
+    def row_job(part, rows, first, slot, put):
+        some = pl.ds(0, rows)
+        return dict(
+            part=lambda a, b: part.at[a, b, pl.ds(first, rows)],
+            y=[wide_y.at[slot, j, some] for j in range(2)],
+            z=wide_z.at[slot, some],
+            v=[wide.at[j, some] for j in range(3)],
+            s=wide_s.at[slot, some],
+            put=put,
+            rows=some,
+        )
+
+    def column_job(part, width, away, slot, to):
+        lanes = pl.ds(0, width)
+        return dict(
+            part=lambda a, b: part.at[a, (zl + away) % 2, b],
+            y=[cols_y.at[slot, j, :, lanes] for j in range(2)],
+            z=cols_z.at[slot, :, lanes],
+            v=[cols.at[j, :, lanes] for j in range(3)],
+            s=cols_s.at[slot, :, lanes],
+            away=away,
+            to=to,
+        )
+
+    fc1_width, qkv_width = units, gqkv.shape[1]
+    out_rows, fc2_rows = out_part.shape[2], fc2_part.shape[2] // 2
+    jobs = [
+        row_job(fc2_part, fc2_rows, i * fc2_rows, i, fc2_out.at[pl.ds(i * fc2_rows, fc2_rows)])
+        for i in range(2)
+    ]
+    jobs += [column_job(fc1_part, fc1_width, away, away, fc1_a) for away in (1, 0)]
+    jobs += [row_job(out_part, out_rows, 0, 2, out_out)]
+    jobs += [column_job(qkv_part, qkv_width, away, 2 + away, qkv_a) for away in (1, 0)]
+
+    def send_beside(job):
+        job["y_far"] = remote(lambda: (job["part"](1 - zh, 1 - y), job["y"][1]), beside)
+        job["y_own"] = remote(lambda: (job["part"](zh, 1 - y), job["y"][0]), beside)
+
+    def pass_on(job):
+        job["y_far"].wait_recv()
+        v = job["v"]
+        load((job["part"](1 - zh, y), v[0]), (job["y"][1], v[1]))
+        job["s"][...] = (v[0][...].astype(f32) + v[1][...].astype(f32)).astype(bf16)
+        job["z_copy"] = remote(lambda: (job["s"], job["z"]), across)
+
+    arrivals, kept = [], []
+
+    def finish(job):
+        job["y_own"].wait_recv()
+        job["z_copy"].wait_recv()
+        v = job["v"]
+        load((job["part"](zh, y), v[0]), (job["y"][0], v[1]), (job["z"], v[2]))
+        total = v[0][...].astype(f32) + v[1][...].astype(f32) + v[2][...].astype(f32)
+        if "put" in job:
+            full[job["rows"]] = total
+            load((full.at[job["rows"]], job["put"]))
+            return
+        job["z_copy"].wait_send()
+        sends[:] = [copy for copy in sends if copy is not job["z_copy"]]
+        job["s"][...] = total.astype(bf16)
+        piece = job["s"].shape[0] // 4
+        for dx in range(2):
+            for dc in range(2):
+
+                def where(dx=dx, dc=dc):
+                    return zh, (zl + job["away"]) % 2, y, (x + dx) % 2, (c + dc) % 2
+
+                def ends(where=where):
+                    _, _, _, to_x, to_c = where()
+                    row = pl.multiple_of((to_x * 2 + to_c) * piece, piece)
+                    return job["s"].at[pl.ds(row, piece)], job["to"].at[(zl * 2 + x) * 2 + c]
+
+                if job["away"] or dx or dc:
+                    arrivals.append(remote(ends, where))
+                else:
+                    kept.append(local(ends))
+
+    def core_copy(n, g):
+        return pltpu.make_async_remote_copy(
+            src_ref=sent.at[4 * n + g],
+            dst_ref=c_got.at[n, g],
+            send_sem=c_send.at[n, g],
+            recv_sem=c_recv.at[n, g],
+            device_id=partner("c"),
+            device_id_type=MESH_ID,
+        )
+
+    axes = ("x", "zl")
+
+    def multiply_groups(n, first, a, v, b, w, multiply):
+        def step(g, carry):
+            one, two = 1 - g // 2, 1 - g % 2
+            rest = ((zl + two) % 2 * 2 + (x + one) % 2) * 2
+
+            def block(where):
+                rows = pl.ds(pl.multiple_of((rest + where) * 256, 256), 256)
+                near, far = v[...].reshape(-1, v.shape[-1]), w[...].reshape(-1, w.shape[-1])
+                return (multiply(a[rows], near) + multiply(b[rows], far)).astype(bf16)
+
+            sent[4 * n + g] = block(1 - c)
+            core_copy(n, g).start()
+            mine[4 * n + g] = block(c)
+            return carry
+
+        lax.fori_loop(first, first + 2, step, 0)
+
+    def add(n, g, got):
+        load((got, stage))
+        mine[4 * n + g] = (mine[4 * n + g].astype(f32) + stage[...].astype(f32)).astype(bf16)
+
+    def add_core(n, g):
+        core_copy(n, g).wait_recv()
+        add(n, g, c_got.at[n, g])
+
+    first_copies, second_copies = {}, {}
+
+    def send_first(n):
+        for g in range(2):
+            add_core(n, g)
+            first_copies[n, g] = remote(
+                lambda g=g: (mine.at[4 * n + g], w_got.at[n, g]), lambda: partner(axes[0])
+            )
+
+    def send_second(n):
+        first_copies[n, 0].wait_recv()
+        add(n, 2, w_got.at[n, 0])
+        second_copies[n] = remote(
+            lambda: (mine.at[4 * n + 2], w_got.at[n, 2]), lambda: partner(axes[1])
+        )
+
+    def add_first(n):
+        first_copies[n, 1].wait_recv()
+        add(n, 3, w_got.at[n, 1])
+
+    def total(n, out):
+        second_copies[n].wait_recv()
+        load((w_got.at[n, 2], stage))
+        full[...] = mine[4 * n + 3].astype(f32) + stage[...].astype(f32)
+        load((full, out))
+
+    def part_tiles(left, right, at, put, tile):
+        def step(i, carry):
+            lanes = pl.ds(pl.multiple_of(at(i) * 256, 256), 256)
+            product = tn(left(lanes), right())
+            slot = i % 2
+
+            @pl.when(i >= 2)
+            def _():
+                pltpu.make_async_copy(tile.at[slot], put(i - 2), block_sem.at[slot]).wait()
+
+            tile[slot] = product.astype(bf16)
+            pltpu.make_async_copy(tile.at[slot], put(i), block_sem.at[slot]).start()
+            return carry
+
+        def between(first, last):
+            lax.fori_loop(first, last, step, 0)
+
+        def drain(last):
+            for i in (last - 2, last - 1):
+                pltpu.make_async_copy(tile.at[i % 2], put(i), block_sem.at[i % 2]).wait()
+
+        return between, drain
+
+    def far_first(i):
+        far, beside = 1 - i % 2, 1 - i // 2
+        return (zh + far) % 2, (y + beside) % 2
+
+    def fc_weights(fc1_w, fc2_w):
+        return [local(lambda: (fc1_all, fc1_w)), local(lambda: (fc2_all, fc2_w))]
+
+    def feed(fc1_w, fc2_w, tile_wide, tile_cols):
+        for copy in fc_weights(fc1_w, fc2_w):
+            copy.wait()
+        up_sum[...] = jnp.zeros_like(up_sum)
+
+        def step(b, carry):
+            rows = pl.ds(pl.multiple_of(b * 256, 256), 256)
+            up = nn(hidden[b], fc1_w[...].reshape(width, units)) + fc1_bias[...]
+            bent = jnp.tanh(gelu_coef * (up + 0.044715 * up * up * up))
+            act[rows] = (0.5 * up * (1.0 + bent)).astype(bf16)
+            slope = 0.5 * (1.0 + bent) + 0.5 * up * (1.0 - bent * bent) * gelu_coef * (
+                1.0 + 3.0 * 0.044715 * up * up
+            )
+            back = (nt(cot[b], fc2_w[...].reshape(units, width)) * slope).astype(bf16)
+            gup[rows] = back
+            up_sum[...] += jnp.sum(back.astype(f32), axis=0, keepdims=True)
+            return carry
+
+        lax.fori_loop(0, blocks // 2, step, 0)
+        late_in.append(forward(out_zh[0], lambda: out_all.at[1 - zh, y]))
+        late_in.append(forward(qkv_zh[0], half_of(qkv_all, 0)))
+        lax.fori_loop(blocks // 2, blocks, step, 0)
+
+        def unit_place(i):
+            a, b = far_first(i)
+            return a * 2 + b
+
+        def unit_put(i):
+            a, b = far_first(i)
+            return fc2_part.at[a, b]
+
+        between, drain = part_tiles(
+            lambda lanes: act[:, lanes], lambda: cot[...].reshape(token_count, width), unit_place, unit_put, tile_wide
+        )
+        between(0, 2)
+        drain(2)
+        late_in.append(forward(qkv_zh[1], half_of(qkv_all, 1)))
+        for job in jobs[:2]:
+            send_beside(job)
+        between, drain = part_tiles(
+            lambda lanes: act[:, lanes],
+            lambda: cot[...].reshape(token_count, width),
+            lambda i: unit_place(i + 2),
+            lambda i: unit_put(i + 2),
+            tile_wide,
+        )
+        between(0, 2)
+        drain(2)
+        feature_tiles(gup, fc1_part, tile_cols, jobs[2:4])
+
+    def feature_tiles(right, part, tile, of):
+        for late in range(2):
+
+            def where(i, late=late):
+                a, b = far_first(i // 2 + 2 * late)
+                return a, i % 2, b
+
+            def feature_place(i, where=where):
+                a, half, b = where(i)
+                return a * 4 + half * 2 + b
+
+            between, drain = part_tiles(
+                lambda lanes: hidden[:, :, lanes].reshape(token_count, 256),
+                lambda: right[...],
+                feature_place,
+                lambda i, where=where: part.at[where(i)],
+                tile,
+            )
+            between(0, 4)
+            drain(4)
+            if late == 0:
+                for job in of:
+                    send_beside(job)
+
+    fc_scratch = (pltpu.VMEM(fc1_all.shape, bf16), pltpu.VMEM(fc2_all.shape, bf16))
+    pl.run_scoped(
+        feed,
+        *fc_scratch,
+        pltpu.VMEM((2, 256, width), bf16),
+        pltpu.VMEM((2, 256, units), bf16),
+    )
+
+    for copy in late_in:
+        copy.wait_recv()
+    load((qkv_all, qkv_w), (out_all, out_w))
+
+    def attend(projected, mixed, q_s, k_s, v_s, g_s, gk_s, gv_s):
+        for seq in range(2):
+
+            def project(b, carry, seq=seq):
+                rows = pl.ds(pl.multiple_of(b * 256, 256), 256)
+                block = b + seq * (blocks // 2)
+                projected[rows] = nn(hidden[block], qkv_w[...].reshape(width, qkv_width))
+                mixed[rows] = nt(cot[block], out_w[...].reshape(-1, width))
+                return carry
+
+            lax.fori_loop(0, blocks // 2, project, 0)
+
+            def pair_step(pair, carry, seq=seq):
+                attend_pair(
+                    pair, length_of(seq), qkv_bias, cosines, sines, projected, mixed, q_s, k_s, v_s, g_s, gk_s, gv_s
+                )
+                return carry
+
+            lax.fori_loop(0, mixed.shape[1] // 128, pair_step, 0)
+            qkv_sum[seq] = jnp.zeros((1, qkv_width), f32)
+
+            def store(b, carry, seq=seq):
+                rows = pl.ds(pl.multiple_of(b * 256, 256), 256)
+                to = pl.ds(pl.multiple_of(b * 256 + seq * total_len, 256), 256)
+                grads = projected[rows].astype(bf16)
+                gqkv[to] = grads
+                attn[to] = mixed[rows].astype(bf16)
+                qkv_sum[seq] += jnp.sum(grads.astype(f32), axis=0, keepdims=True)
+                return carry
+
+            lax.fori_loop(0, blocks // 2, store, 0)
+            pass_on(jobs[seq])
+
+    heads = pltpu.VMEM((2, total_len, 128), bf16)
+    pl.run_scoped(
+        attend,
+        pltpu.VMEM((total_len, qkv_width), f32),
+        pltpu.VMEM((total_len, attn.shape[1]), f32),
+        heads,
+        heads,
+        heads,
+        heads,
+        pltpu.VMEM((total_len, 128), f32),
+        pltpu.VMEM((total_len, 128), f32),
+    )
+
+    def attend_parts(tile_cols, tile_out):
+        feature_tiles(gqkv, qkv_part, tile_cols, jobs[5:7])
+        tile_out[...] = tn(attn[...], cot[...].reshape(token_count, width)).astype(bf16)
+        rows = tile_out.shape[0] // 4
+        load(*((tile_out.at[pl.ds(rows * i, rows)], out_part.at[i // 2, i % 2]) for i in range(4)))
+        send_beside(jobs[4])
+
+    pl.run_scoped(
+        attend_parts, pltpu.VMEM((2, 256, qkv_width), bf16), pltpu.VMEM((attn.shape[1], width), bf16)
+    )
+
+    def sums(fc1_w, fc2_w):
+        weights = fc_weights(fc1_w, fc2_w)
+        for copy in sends[:early_sends]:
+            copy.wait_send()
+        pass_on(jobs[2])
+        weights[0].wait()
+        multiply_groups(0, 0, gqkv, qkv_w, gup, fc1_w, nt)
+        send_first(0)
+        weights[1].wait()
+        multiply_groups(1, 0, attn, out_w, act, fc2_w, nn)
+        send_first(1)
+        finish(jobs[0])
+        multiply_groups(0, 2, gqkv, qkv_w, gup, fc1_w, nt)
+        multiply_groups(1, 2, attn, out_w, act, fc2_w, nn)
+
+    pl.run_scoped(sums, *fc_scratch)
+    for n in range(2):
+        add_core(n, 2)
+        add_core(n, 3)
+    send_second(0)
+    pass_on(jobs[3])
+    send_second(1)
+    finish(jobs[1])
+    add_first(0)
+    add_first(1)
+    finish(jobs[2])
+    pass_on(jobs[5])
+    total(0, gh_own)
+    total(1, br_own)
+    pass_on(jobs[6])
+    pass_on(jobs[4])
+    for job in (jobs[3], jobs[5], jobs[6], jobs[4]):
+        finish(job)
+    for copy in arrivals:
+        copy.wait_recv()
+    for copy in kept:
+        copy.wait()
+    for copy in sends[early_sends:]:
+        copy.wait_send()
+    for n in range(2):
+        for g in range(4):
+            core_copy(n, g).wait_send()
+
+
+def main(small, tokens, cot, cosines, sines, fc2_own, out_own, fc1_spread, qkv_spread):
+    bf16, f32 = jnp.bfloat16, jnp.float32
+    block, width = tokens.shape
+    tokens_all = 8 * block
+    rows, ff_rows = out_own.shape[0], fc2_own.shape[0]
+    fc1_width, qkv_width = fc1_spread.shape[2], qkv_spread.shape[2]
+    half = ff_rows // 2
+    any_, vmem = pl.BlockSpec(memory_space=pl.ANY), pl.BlockSpec(memory_space=pltpu.VMEM)
+    shapes = [
+        ((block, width), f32, any_),
+        ((block, width), f32, any_),
+        ((ff_rows, width), f32, any_),
+        ((rows, width), f32, any_),
+        ((8, rows, fc1_width), bf16, any_),
+        ((8, rows, qkv_width), bf16, any_),
+        ((1, fc1_width), f32, vmem),
+        ((2, 1, qkv_width), f32, vmem),
+        ((32,) + small.shape, f32, vmem),
+        ((2, 2, 2, 4, rows, qkv_width), bf16, any_),
+        ((2, 2, rows, width), bf16, any_),
+        ((2, 2, 2, 4, rows, fc1_width), bf16, any_),
+        ((2, 2, ff_rows, width), bf16, any_),
+        ((2, 2, ff_rows, width), bf16, any_),
+        ((2, 2, 2, 4 * rows, fc1_width), bf16, any_),
+        ((2, 2, rows, width), bf16, any_),
+        ((2, 2, 2, 4 * rows, qkv_width), bf16, any_),
+        ((2, 4, block, width), bf16, any_),
+        ((2, 3, block, width), bf16, any_),
+        ((3, 2, half, width), bf16, any_),
+        ((3, half, width), bf16, any_),
+        ((4, 2, 4 * rows, fc1_width), bf16, any_),
+        ((4, 4 * rows, fc1_width), bf16, any_),
+    ]
+    scratch = [
+        pltpu.VMEM((8, block, width), bf16),
+        pltpu.VMEM((8, block, width), bf16),
+        pltpu.VMEM((tokens_all, fc1_width), bf16),
+        pltpu.VMEM((tokens_all, fc1_width), bf16),
+        pltpu.VMEM((tokens_all, 4 * rows), bf16),
+        pltpu.VMEM((tokens_all, qkv_width), bf16),
+        pltpu.VMEM((2, 2, 2, 4, rows, qkv_width), bf16),
+        pltpu.VMEM((2, 2, rows, width), bf16),
+        pltpu.VMEM((block, width), bf16),
+        pltpu.VMEM((block, width), f32),
+        pltpu.VMEM((3, half, width), bf16),
+        pltpu.VMEM((3, 4 * rows, fc1_width), bf16),
+        pltpu.VMEM((3, half, width), bf16),
+        pltpu.VMEM((4, 4 * rows, fc1_width), bf16),
+        pltpu.VMEM((1, fc1_width), f32),
+        pltpu.VMEM((1, qkv_width), f32),
+        pltpu.SemaphoreType.DMA((96,)),
+        pltpu.SemaphoreType.DMA((96,)),
+        pltpu.SemaphoreType.DMA((96,)),
+        pltpu.SemaphoreType.DMA((2,)),
+        pltpu.SemaphoreType.DMA((2, 4)),
+        pltpu.SemaphoreType.DMA((2, 4)),
+        pltpu.SemaphoreType.DMA((32,)),
+        pltpu.SemaphoreType.DMA((32,)),
+    ]
+    return pl.pallas_call(
+        main_kernel,
+        out_shape=[jax.ShapeDtypeStruct(shape, kind) for shape, kind, _ in shapes],
+        in_specs=[vmem, any_, any_, vmem, vmem] + [any_] * 4,
+        out_specs=[spec for _, _, spec in shapes],
+        scratch_shapes=scratch,
+        compiler_params=pltpu.CompilerParams(
+            collective_id=0, has_side_effects=True, vmem_limit_bytes=63 * 2**20
+        ),
+    )(small, tokens, cot, cosines, sines, fc2_own, out_own, fc1_spread, qkv_spread)[:9]
+
+
+def columns_kernel(fc1_in, qkv_in, fc1_out, qkv_out):
+    f32 = jnp.float32
+    unit, part_width = fc1_in.shape[2] // 4, qkv_in.shape[2] // 3
+    for w in range(8):
+        for t in range(4):
+            at = ((t // 2 * 2 + w // 4) * 2 + t % 2) * 4 * unit + w % 4 * unit
+            fc1_out[:, at : at + unit] = fc1_in[w, :, t * unit : (t + 1) * unit].astype(f32)
+    low = lax.broadcasted_iota(jnp.int32, (1, 128), 1) < HEAD_DIM
+    for part in range(3):
+        for a in range(2):
+            for dl in range(2):
+                for dx in range(2):
+                    at = part * part_width + a * 128
+                    even, odd = (
+                        qkv_in[dl * 4 + dx * 2 + k, :, at : at + 128].astype(f32) for k in range(2)
+                    )
+                    to = part * 8 * part_width + a * 1024 + dl * 512 + dx * 128
+                    qkv_out[:, to : to + 128] = jnp.where(low, even, pltpu.roll(odd, 64, 1))
+                    qkv_out[:, to + 256 : to + 384] = jnp.where(low, pltpu.roll(even, 64, 1), odd)
+
+
+def plain_columns(fc1_in, qkv_in):
+    _, rows, fc1_width = fc1_in.shape
+    vmem = pl.BlockSpec(memory_space=pltpu.VMEM)
+    return pl.pallas_call(
+        columns_kernel,
+        out_shape=[
+            jax.ShapeDtypeStruct((rows, 8 * fc1_width), jnp.float32),
+            jax.ShapeDtypeStruct((rows, 8 * qkv_in.shape[2]), jnp.float32),
+        ],
+        in_specs=[vmem, vmem],
+        out_specs=[vmem, vmem],
+        compiler_params=pltpu.CompilerParams(vmem_limit_bytes=24 * 2**20),
+    )(fc1_in, qkv_in)
+
+
+def split_device(
+    tokens,
+    lengths,
+    ln_gain,
+    ln_bias,
+    w_qkv,
+    b_qkv,
+    w_out,
+    b_out,
+    w_fc1,
+    b_fc1,
+    w_fc2,
+    b_fc2,
+    cotangent,
+):
+    bf16, f32 = jnp.bfloat16, jnp.float32
+    zh, zl, y, x, c = (lax.axis_index(name) for name in FINE)
+    place = (zl * 2 + x) * 2 + c
+    _, local_len, width = tokens.shape
+    rows = w_qkv.shape[0]
+    ff_rows = w_fc2.shape[0]
+    pieces = 4
+    total_len = local_len * pieces
+    heads = 4
+    own_width = heads * HEAD_DIM
+
+    row = 2 * rows
+    small = jnp.concatenate(
+        [v.astype(f32) for v in (ln_gain, ln_gain, ln_bias, ln_bias, b_qkv, b_out, b_fc1, b_fc2)]
+        + [jnp.zeros(row - rows, f32), jnp.broadcast_to(lengths.astype(f32), (row,))]
+    ).reshape(-1, row)
+    places = (x * 2 + c) * local_len + jnp.arange(local_len, dtype=jnp.int32)
+    grad_own = jnp.where((places < lengths[0])[:, None], cotangent[0], jnp.zeros((), bf16))
+    fc1_spread = (
+        w_fc1.reshape((rows, 2, 2, 2, 2, 2, ff_rows))
+        .transpose(2, 4, 5, 0, 1, 3, 6)
+        .reshape(8, rows, -1)
+    )
+    qkv_spread = (
+        w_qkv.reshape((rows, 3, 2, 2, 2, 2, 2, HEAD_DIM))
+        .transpose(3, 5, 6, 0, 1, 2, 4, 7)
+        .reshape(8, rows, -1)
+    )
+    cosines, sines = tables(total_len, ROT)
+    (
+        grad_hidden_own,
+        branch_own,
+        grad_fc2,
+        grad_wout,
+        fc1_columns,
+        qkv_columns,
+        grad_up_sum,
+        grad_qkv_sum,
+        small_all,
+    ) = main(
+        small, tokens[0], grad_own, cosines, sines, w_fc2, w_out, fc1_spread, qkv_spread
+    )
+    grad_wfc1, grad_wqkv = plain_columns(fc1_columns, qkv_columns)
+    gain_all = small_all[:, 0, :rows].reshape(-1)
+    bout_all, bfc2_all = small_all[:, 3, rows:].reshape(-1), small_all[:, 6, :rows].reshape(-1)
+
+    inputs = tokens[0].astype(f32)
+    average = jnp.mean(inputs, axis=-1, keepdims=True)
+    centered = inputs - average
+    variance = jnp.mean(centered * centered, axis=-1, keepdims=True)
+    inv_std = lax.rsqrt(variance + eps_norm)
+    normed = centered * inv_std
+
+    output = (inputs + branch_own + bout_all + bfc2_all).astype(bf16)[None]
+    grad_norm = grad_hidden_own * gain_all
+    grad_input = grad_own.astype(f32) + inv_std * (
+        grad_norm
+        - jnp.mean(grad_norm, axis=-1, keepdims=True)
+        - normed * jnp.mean(grad_norm * normed, axis=-1, keepdims=True)
+    )
+    grad_input = grad_input.astype(bf16)[None]
+
+    mine = (jnp.arange(8) == place).astype(f32)
+    bqkv_term = (
+        (jnp.sum(grad_qkv_sum, axis=0).reshape(1, 3, 2, 2, HEAD_DIM) * mine[:, None, None, None, None])
+        .reshape(2, 4, 3, 2, 2, HEAD_DIM)
+        .transpose(2, 3, 0, 4, 1, 5)
+        .reshape(-1)
+    )
+    bfc1_term = (
+        (grad_up_sum.reshape(1, 2, 2, ff_rows) * mine[:, None, None, None])
+        .reshape(2, 4, 2, 2, ff_rows)
+        .transpose(2, 0, 3, 1, 4)
+        .reshape(-1)
+    )
+    bias_term = jnp.sum(grad_own, axis=0, dtype=f32)
+    gain_term = jnp.sum(grad_hidden_own * normed, axis=0)
+    shift_term = jnp.sum(grad_hidden_own, axis=0)
+    terms = jnp.concatenate(
+        [
+            v.reshape(32, -1)
+            for v in (bqkv_term, bfc1_term, bias_term, gain_term, shift_term)
+        ],
+        axis=1,
+    )
+    sums = sum_small(terms.reshape(32, -1, 128), 1).reshape(-1)
+    grad_bqkv, grad_bfc1, grad_bias, grad_gain, grad_shift = jnp.split(
+        sums, np.cumsum([3 * rows, ff_rows, rows, rows])
+    )
+    return (
+        output,
+        grad_input,
+        grad_gain,
+        grad_shift,
+        grad_wqkv,
+        grad_bqkv,
+        grad_wout,
+        grad_bias,
+        grad_wfc1,
+        grad_bfc1,
+        grad_fc2,
+        grad_bias,
+    )
+
+
+def fine_mesh(mesh):
+    return jax.sharding.Mesh(mesh.devices.reshape(2, 2, 2, 2, 2), FINE)
+
+
+def fine_solution(mesh):
+    everyone, seqs, parts = FINE, ("zh", "zl", "y"), ("x", "c")
+    placed = (
+        P(seqs, parts, None),
+        P(seqs),
+        P(everyone),
+        P(everyone),
+        P(everyone, None),
+        P(everyone),
+        P(everyone, None),
+        P(everyone),
+        P(everyone, None),
+        P(everyone),
+        P(everyone, None),
+        P(everyone),
+        P(seqs, parts, None),
+    )
+    given = (
+        P(seqs, parts, None),
+        P(seqs, parts, None),
+        P(everyone),
+        P(everyone),
+        P(everyone, None),
+        P(everyone),
+        P(everyone, None),
+        P(everyone),
+        P(everyone, None),
+        P(everyone),
+        P(everyone, None),
+        P(everyone),
+    )
+    return jax.shard_map(
+        split_device, mesh=fine_mesh(mesh), in_specs=placed, out_specs=given, check_vma=False
+    )
+
+
+def solution(mesh):
+    if mesh.shape["dp"] == 8 and mesh.shape["ctx"] == 4:
+        return fine_solution(mesh)
+    return general_solution(mesh)

time: 3690 us -> 516 us (0.14)
  waiting for transfers between devices: 2870 us -> 0 us
  Pallas kernels: 0 us -> 472 us
  matrix products: 305 us -> 0 us
  blocking collectives: 167 us -> 0 us
  local copies, waits for them, and re-layouts: 184 us -> 22.9 us
  other arithmetic: 136 us -> 16 us
    unnamed x14 -> x0, waiting for transfers between devices: 1570 us -> none
    reduce_scatter x6 -> x0, waiting for transfers between devices: 957 us -> none  [the longest x1 698 us: on_device(): lax.psum_scatter(wfc2_term, ('dp', 'ctx'), scatter_dimension=0, tiled=True)]
    pallas_call x0 -> x3, Pallas kernels: none -> 472 us  [the longest x1 458 us: main(): pl.pallas_call(main_kernel, out_shape=[jax.ShapeDtypeStruct(shape, kind)...]
    all_gather x6 -> x0, waiting for transfers between devices: 343 us -> none  [the longest x1 140 us: on_device(): lax.all_gather(w_fc1, ('dp', 'ctx'), axis=0, tiled=True)]
    dot_general x18 -> x0, matrix products: 305 us -> none  [the longest x1 27.4 us: on_device(): jnp.einsum('tk,td->kd', activated, grad_out, preferred_element_type=jnp.f...]
    reshape x8 -> x10, local copies, waits for them, and re-layouts: 148 us -> 9.42 us  [the longest x2 3.72 us: split_device(): w_qkv.reshape((rows, 3, 2, 2, 2, 2, 2, HEAD_DIM))]
    unnamed x2 -> x0, blocking collectives: 84.7 us -> none
    all_gather x2 -> x0, blocking collectives: 82.8 us -> none  [the longest x1 41.5 us: on_device(): lax.all_gather(fc1_bias_rows, ('dp', 'ctx'), axis=0, tiled=True)]
  transfers between devices with their start and end apart: 13 -> 0, of which waited for: 10 -> 0; matrix products, arithmetic and copies ran while one was open for 17% -> 0% of each run, Pallas kernels for 0% -> 0%
where the time goes in v4:
time: 516 us; the launch traced here: 512 us
  Pallas kernels  472 us (91%)
  local copies, waits for them, and re-layouts  22.9 us (4%)
  other arithmetic  16 us (3%)
    pallas_call x1, Pallas kernels, main(): pl.pallas_call(main_kernel, out_shape=[jax.ShapeDtypeStruct(shape, kind)...  458 us
    pallas_call x1, Pallas kernels, sum_small(): pl.pallas_call(sum_kernel, out_shape=jax.ShapeDtypeStruct((n, 128), jnp.f...  11.6 us

profile of v4, /device:TPU:0, one launch (start us, length us, event | category | flops | bytes accessed | tf_op | source)
XLA Modules:
  0.0 512.3 jit_solution(1677459374106030462)
XLA Ops:
  1.3 2.5 convert_reduce_fusion.1
  3.8 1.9 multiply_sine_fusion
  5.8 1.9 concatenate.14.sines
  7.7 0.0 copy-start.13
  7.7 0.0 copy-start.14
  7.8 1.7 concatenate.13.cosines
  9.5 0.0 copy-done.9
  9.6 0.7 concatenate.12
  10.3 2.5 reshape.121
  12.8 1.2 copy.34
  14.0 0.0 copy-start.5
  14.0 1.7 reshape.122.qkv_spread
  15.7 0.8 reshape.119
  16.5 0.8 copy.35
  17.3 1.5 reshape.120.fc1_spread
  18.9 457.7 %shard_map.220 = (f32[256,2048]{1,0:T(8,128)}, f32[256,2048]{1,0:T(8,128)}, f32[256,2048]{1,0:T(8,128)}, f32[64,2048]{1,0:T(8,128)}, bf16[8,64,1024]{2,1,0:T(8,1...) custom-call(f32[8,128]{1,0:T(8,128)} %bitcast.28, ...), custom_call_target="tpu_custom_call" | custom-call | tf_op jit(solution)/shard_map/pallas_call | solution.py:1177
  476.6 0.0 copy-start.2
  476.6 1.3 slice_reduce_fusion
  477.9 0.1 mul.162
  478.0 1.4 convert_reduce_fusion
  479.4 0.0 copy-start.8
  479.4 0.0 copy-start.7
  479.4 1.6 fusion.9
  481.1 0.0 copy-start.3
  481.1 2.6 fusion.8
  483.8 0.1 reshape.124
  483.8 0.1 reshape.125
  483.9 0.5 broadcast.91
  484.4 0.7 reduce.16
  485.2 0.1 mul.181
  485.3 0.1 broadcast_multiply_fusion.1
  485.4 0.1 mul.170
  485.4 0.1 broadcast_multiply_fusion
  485.5 0.1 mul.176
  485.6 0.1 reshape.123
  485.7 0.1 concatenate.15
  485.8 0.7 reshape.126.src
  486.5 11.6 %shard_map.221 = f32[5,128]{1,0:T(8,128)} custom-call(f32[32,5,128]{2,1,0:T(8,128)} %reshape.126.src), custom_call_target="tpu_custom_call" | custom-call | tf_op jit(solution)/shard_map/pallas_call | solution.py:494
  498.1 1.4 fusion.17
  499.5 1.2 split.17
  500.7 1.3 split.19
  502.0 0.1 add.62
  502.1 0.1 add.65
  502.2 5.0 fusion.15
  507.2 2.2 shard_map.222
  509.4 0.5 copy.40
  509.9 0.8 copy.41
  510.7 1.3 copy.42
  (40 shorter events, 0.2 us)
Async XLA Ops:
  7.7 1.8 copy-start.9
  7.7 1.8 copy-start.10
  7.7 1.8 copy-start.11
  7.7 1.8 copy-start.12
  7.7 1.9 copy-start.13
  7.7 1.9 copy-start.14
  14.0 1.7 copy-start.5
  476.6 4.5 copy-start.2
  479.4 5.0 copy-start.8
  479.4 5.9 %copy-start.7 = (f32[2,1,768]{2,1,0:T(1,128)S(1)}, f32[2,1,768]{2,1,0:T(1,128)}, u32[]{:S(2)}) copy-start(f32[2,1,768]{2,1,0:T(1,128)} %get-tuple-element.26) | copy-start | bytes 18436
  481.1 21.0 %copy-start.3 = (bf16[256,2048]{1,0:T(8,128)(2,1)S(1)}, bf16[256,2048]{1,0:T(8,128)(2,1)}, u32[]{:S(2)}) copy-start(bf16[256,2048]{1,0:T(8,128)(2,1)} %get-tuple-element.42.cot_own) | copy-start | bytes 3145732
  499.4 9.9 %copy-start.15 = (f32[64]{0:T(128)}, f32[64]{0:T(128)S(1)}, u32[]{:S(2)}) copy-start(f32[64]{0:T(128)S(1)} %get-tuple-element.96) | copy-start | bytes 772
  502.1 5.0 copy-start
  502.1 5.0 copy-start.1
  502.1 7.7 %copy-start.6 = (f32[64,2048]{1,0:T(8,128)S(1)}, f32[64,2048]{1,0:T(8,128)}, u32[]{:S(2)}) copy-start(f32[64,2048]{1,0:T(8,128)} %get-tuple-element.95) | copy-start | bytes 1572868
  507.1 3.5 copy-start.4

commit v5 on v4

--- a/solution.py
+++ b/solution.py
@@ -673,8 +673,7 @@
     cot_zl = over(own_cot, seat_of(cot), "zl")
     fc2_zh, fc2_y = parts_of([fc2_ends(half) for half in range(2)])
     cot_x = over(own_cot, seat_of(cot), "x")
-    core = [over(own_cot, seat_of(cot), "c")]
-    qkv_pieces = spread(qkv_spread, qkv_all)
+    core = {("cot", 0, 0): over(own_cot, seat_of(cot), "c")}
     own_copies = [
         local(lambda: (cot_own, cot.at[seat])),
         local(lambda: (fc2_own, fc2_all.at[zh, y])),
@@ -704,7 +703,7 @@
     lax.fori_loop(0, block_rows // 32, norm_rows, 0)
     hid_zl = over(seat_of(hidden), seat_of(hidden), "zl")
     hid_x = over(seat_of(hidden), seat_of(hidden), "x")
-    core.append(over(seat_of(hidden), seat_of(hidden), "c"))
+    core["hidden", 0, 0] = over(seat_of(hidden), seat_of(hidden), "c")
 
     for t in range(4):
         owner = index_of((t // 2, zl, t % 2, x, c))
@@ -731,32 +730,38 @@
             piece.wait_recv()
         pieces[1].wait()
 
+    def to_core(name, copy, dl, dx):
+        array = {"cot": cot, "hidden": hidden}[name]
+        copy.wait_recv()
+        core[name, dl, dx] = over(seat_of(array, dl, dx), seat_of(array, dl, dx), "c")
+
     all_there(fc1_pieces)
     fc1_zh, fc1_y = parts_of([own_half(fc1_all, half) for half in range(2)])
-    cot_zl.wait_recv()
+    to_core("cot", cot_zl, 1, 0)
     cot_zx = over(seat_of(cot, 1), seat_of(cot, 1), "x")
-    core.append(over(seat_of(cot, 1), seat_of(cot, 1), "c"))
-    hid_zl.wait_recv()
+    fc2_fwd = [forward(fc2_zh[0], fc2_rows_of(1 - zh, 0))]
+    to_core("cot", cot_x, 0, 1)
+    fc2_fwd.append(forward(fc2_zh[1], fc2_rows_of(1 - zh, 1)))
+    to_core("hidden", hid_zl, 1, 0)
     hid_zx = over(seat_of(hidden, 1), seat_of(hidden, 1), "x")
-    core.append(over(seat_of(hidden, 1), seat_of(hidden, 1), "c"))
-    fc2_fwd = [forward(copy, fc2_rows_of(1 - zh, half)) for half, copy in enumerate(fc2_zh)]
+    qkv_pieces = spread(qkv_spread, qkv_all)
+    to_core("hidden", hid_x, 0, 1)
+    fc1_fwd = [forward(fc1_zh[0], half_of(fc1_all, 0))]
+    to_core("cot", cot_zx, 1, 1)
+    fc1_fwd.append(forward(fc1_zh[1], half_of(fc1_all, 1)))
     all_there(qkv_pieces)
     out_zh, out_y = parts_of([lambda: (out_own, out_all.at[zh, y])])
     qkv_zh, qkv_y = parts_of([own_half(qkv_all, half) for half in range(2)])
-    for array, copies in ((cot, ((cot_x, 0), (cot_zx, 1))), (hidden, ((hid_x, 0),))):
-        for copy, dl in copies:
-            copy.wait_recv()
-            core.append(over(seat_of(array, dl, 1), seat_of(array, dl, 1), "c"))
-    fc1_fwd = [forward(copy, half_of(fc1_all, half)) for half, copy in enumerate(fc1_zh)]
-    hid_zx.wait_recv()
-    core.append(over(seat_of(hidden, 1, 1), seat_of(hidden, 1, 1), "c"))
-    for copy in own_copies + core + fc2_y + fc2_fwd + fc1_y + fc1_fwd:
-        if copy in own_copies:
-            copy.wait()
-        else:
-            copy.wait_recv()
+    for copy in own_copies:
+        copy.wait()
+    for copy in fc2_y + fc2_fwd + fc1_y + fc1_fwd:
+        copy.wait_recv()
+
+    def tokens_here(dl, dx):
+        for name in ("cot", "hidden"):
+            core[name, dl, dx].wait_recv()
+
     late_in = out_y + qkv_y
-    early_sends = len(sends)
 
     def row_job(part, rows, first, slot, put):
         some = pl.ds(0, rows)
@@ -845,12 +850,13 @@
             device_id_type=MESH_ID,
         )
 
-    axes = ("x", "zl")
+    axes = (("x", "zl"), ("x", "zl"))
 
     def multiply_groups(n, first, a, v, b, w, multiply):
         def step(g, carry):
             one, two = 1 - g // 2, 1 - g % 2
-            rest = ((zl + two) % 2 * 2 + (x + one) % 2) * 2
+            dl, dx = two, one
+            rest = ((zl + dl) % 2 * 2 + (x + dx) % 2) * 2
 
             def block(where):
                 rows = pl.ds(pl.multiple_of((rest + where) * 256, 256), 256)
@@ -878,14 +884,14 @@
         for g in range(2):
             add_core(n, g)
             first_copies[n, g] = remote(
-                lambda g=g: (mine.at[4 * n + g], w_got.at[n, g]), lambda: partner(axes[0])
+                lambda g=g: (mine.at[4 * n + g], w_got.at[n, g]), lambda: partner(axes[n][0])
             )
 
     def send_second(n):
         first_copies[n, 0].wait_recv()
         add(n, 2, w_got.at[n, 0])
         second_copies[n] = remote(
-            lambda: (mine.at[4 * n + 2], w_got.at[n, 2]), lambda: partner(axes[1])
+            lambda: (mine.at[4 * n + 2], w_got.at[n, 2]), lambda: partner(axes[n][1])
         )
 
     def add_first(n):
@@ -933,7 +939,8 @@
             copy.wait()
         up_sum[...] = jnp.zeros_like(up_sum)
 
-        def step(b, carry):
+        def step(i, carry):
+            b = ((zl + i // 2) % 2 * 2 + (x + i // 4) % 2) * 2 + (c + i) % 2
             rows = pl.ds(pl.multiple_of(b * 256, 256), 256)
             up = nn(hidden[b], fc1_w[...].reshape(width, units)) + fc1_bias[...]
             bent = jnp.tanh(gelu_coef * (up + 0.044715 * up * up * up))
@@ -946,10 +953,16 @@
             up_sum[...] += jnp.sum(back.astype(f32), axis=0, keepdims=True)
             return carry
 
-        lax.fori_loop(0, blocks // 2, step, 0)
+        tokens_here(0, 0)
+        tokens_here(1, 0)
+        lax.fori_loop(0, 4, step, 0)
+        to_core("hidden", hid_zx, 1, 1)
+        tokens_here(0, 1)
+        lax.fori_loop(4, 6, step, 0)
         late_in.append(forward(out_zh[0], lambda: out_all.at[1 - zh, y]))
         late_in.append(forward(qkv_zh[0], half_of(qkv_all, 0)))
-        lax.fori_loop(blocks // 2, blocks, step, 0)
+        tokens_here(1, 1)
+        lax.fori_loop(6, 8, step, 0)
 
         def unit_place(i):
             a, b = far_first(i)
@@ -1071,17 +1084,19 @@
         attend_parts, pltpu.VMEM((2, 256, qkv_width), bf16), pltpu.VMEM((attn.shape[1], width), bf16)
     )
 
+    early_sends = list(core.values()) + [cot_zl, cot_x, cot_zx, hid_zl, hid_x, hid_zx]
+
     def sums(fc1_w, fc2_w):
         weights = fc_weights(fc1_w, fc2_w)
-        for copy in sends[:early_sends]:
+        for copy in early_sends:
             copy.wait_send()
-        pass_on(jobs[2])
         weights[0].wait()
         multiply_groups(0, 0, gqkv, qkv_w, gup, fc1_w, nt)
         send_first(0)
         weights[1].wait()
         multiply_groups(1, 0, attn, out_w, act, fc2_w, nn)
         send_first(1)
+        pass_on(jobs[2])
         finish(jobs[0])
         multiply_groups(0, 2, gqkv, qkv_w, gup, fc1_w, nt)
         multiply_groups(1, 2, attn, out_w, act, fc2_w, nn)
@@ -1090,26 +1105,29 @@
     for n in range(2):
         add_core(n, 2)
         add_core(n, 3)
+    pass_on(jobs[3])
+    finish(jobs[1])
     send_second(0)
-    pass_on(jobs[3])
-    send_second(1)
-    finish(jobs[1])
-    add_first(0)
-    add_first(1)
     finish(jobs[2])
     pass_on(jobs[5])
-    total(0, gh_own)
-    total(1, br_own)
+    add_first(0)
     pass_on(jobs[6])
     pass_on(jobs[4])
-    for job in (jobs[3], jobs[5], jobs[6], jobs[4]):
-        finish(job)
+    finish(jobs[3])
+    send_second(1)
+    add_first(1)
+    total(0, gh_own)
+    finish(jobs[5])
+    finish(jobs[6])
+    finish(jobs[4])
+    total(1, br_own)
     for copy in arrivals:
         copy.wait_recv()
     for copy in kept:
         copy.wait()
-    for copy in sends[early_sends:]:
-        copy.wait_send()
+    for copy in sends:
+        if not any(copy is early for early in early_sends):
+            copy.wait_send()
     for n in range(2):
         for g in range(4):
             core_copy(n, g).wait_send()

time: 516 us -> 466 us (0.903)
  Pallas kernels: 472 us -> 422 us
    pallas_call x1, Pallas kernels: 458 us -> 409 us  [main(): pl.pallas_call(main_kernel, out_shape=[jax.ShapeDtypeStruct(shape, kind)...]
where the time goes in v5:
time: 466 us; the launch traced here: 462 us
  Pallas kernels  422 us (91%)
  local copies, waits for them, and re-layouts  22.9 us (5%)
  other arithmetic  16 us (3%)
    pallas_call x1, Pallas kernels, main(): pl.pallas_call(main_kernel, out_shape=[jax.ShapeDtypeStruct(shape, kind)...  409 us
    pallas_call x1, Pallas kernels, sum_small(): pl.pallas_call(sum_kernel, out_shape=jax.ShapeDtypeStruct((n, 128), jnp.f...  10.5 us

profile of v5, /device:TPU:0, one launch (start us, length us, event | category | flops | bytes accessed | tf_op | source)
XLA Modules:
  0.0 462.4 jit_solution(8074157827018282644)
XLA Ops:
  1.3 2.5 convert_reduce_fusion.1
  3.8 1.9 multiply_sine_fusion
  5.8 1.9 concatenate.14.sines
  7.7 0.0 copy-start.13
  7.7 0.0 copy-start.14
  7.8 1.7 concatenate.13.cosines
  9.5 0.0 copy-done.9
  9.5 0.0 copy-done.10
  9.6 0.7 concatenate.12
  10.3 2.5 reshape.121
  12.8 1.2 copy.34
  14.0 0.0 copy-start.5
  14.0 1.7 reshape.122.qkv_spread
  15.7 0.8 reshape.119
  16.5 0.8 copy.35
  17.3 1.5 reshape.120.fc1_spread
  18.9 409.0 %shard_map.220 = (f32[256,2048]{1,0:T(8,128)}, f32[256,2048]{1,0:T(8,128)}, f32[256,2048]{1,0:T(8,128)}, f32[64,2048]{1,0:T(8,128)}, bf16[8,64,1024]{2,1,0:T(8,1...) custom-call(f32[8,128]{1,0:T(8,128)} %bitcast.28, ...), custom_call_target="tpu_custom_call" | custom-call | tf_op jit(solution)/shard_map/pallas_call | solution.py:1195
  427.9 0.0 copy-start.2
  427.9 1.3 slice_reduce_fusion
  429.2 0.1 mul.162
  429.2 1.4 convert_reduce_fusion
  430.7 1.6 fusion.9
  432.4 0.0 copy-start.3
  432.4 2.6 fusion.8
  435.0 0.1 reshape.124
  435.1 0.1 reshape.125
  435.2 0.5 broadcast.91
  435.7 0.7 reduce.16
  436.4 0.1 mul.181
  436.5 0.1 broadcast_multiply_fusion.1
  436.6 0.1 mul.170
  436.7 0.1 broadcast_multiply_fusion
  436.8 0.1 mul.176
  436.9 0.1 reshape.123
  437.0 0.1 concatenate.15
  437.1 0.7 reshape.126.src
  437.7 10.5 %shard_map.221 = f32[5,128]{1,0:T(8,128)} custom-call(f32[32,5,128]{2,1,0:T(8,128)} %reshape.126.src), custom_call_target="tpu_custom_call" | custom-call | tf_op jit(solution)/shard_map/pallas_call | solution.py:494
  448.2 1.4 fusion.17
  449.6 1.2 split.17
  450.8 1.3 split.19
  452.1 0.1 add.62
  452.2 0.1 add.65
  452.3 5.0 %fusion.15 = (bf16[1,256,2048]{2,1,0:T(8,128)(2,1)}, bf16[1,256,2048]{2,1,0:T(8,128)(2,1)}) fusion(f32[256,2048]{1,0:T(8,128)} %get-tuple-element.25, bf16[256,2048]{1,0:T(8,128)(2,1)S(1)} %copy-done.3, f32[256]{0:T(256)S(1)} %get-tuple-element.51, f32[256]{0:T(256)S(1)} %get-tuple-element.52, f32[2048]{0:T(1024)S(1)} %mul.162, f32[256]{0:T(256)S(1)} %add_rsqrt_fusion, ...), kind=kLoop, calls=%fused_computation.22 | loop fusion | flops 7864320 | bytes 8417280 | tf_op jit(solution)/shard_map/broadcast_in_dim | solution.py:1318
  457.3 0.0 copy-done
  457.3 2.2 shard_map.222
  459.5 0.5 copy.40
  460.0 0.8 copy.41
  460.8 1.3 copy.42
  (40 shorter events, 0.2 us)
Async XLA Ops:
  7.7 1.8 copy-start.9
  7.7 1.8 copy-start.10
  7.7 1.8 copy-start.11
  7.7 1.8 copy-start.12
  7.7 1.9 copy-start.13
  7.7 1.9 copy-start.14
  14.0 1.7 copy-start.5
  427.9 4.5 copy-start.2
  430.7 5.0 %copy-start.8 = (f32[1,1024]{1,0:T(1,128)S(1)}, f32[1,1024]{1,0:T(1,128)}, u32[]{:S(2)}) copy-start(f32[1,1024]{1,0:T(1,128)} %get-tuple-element.27) | copy-start | bytes 12292
  430.7 5.9 %copy-start.7 = (f32[2,1,768]{2,1,0:T(1,128)S(1)}, f32[2,1,768]{2,1,0:T(1,128)}, u32[]{:S(2)}) copy-start(f32[2,1,768]{2,1,0:T(1,128)} %get-tuple-element.26) | copy-start | bytes 18436
  432.4 19.9 %copy-start.3 = (bf16[256,2048]{1,0:T(8,128)(2,1)S(1)}, bf16[256,2048]{1,0:T(8,128)(2,1)}, u32[]{:S(2)}) copy-start(bf16[256,2048]{1,0:T(8,128)(2,1)} %get-tuple-element.42.cot_own) | copy-start | bytes 3145732
  449.6 9.9 %copy-start.15 = (f32[64]{0:T(128)}, f32[64]{0:T(128)S(1)}, u32[]{:S(2)}) copy-start(f32[64]{0:T(128)S(1)} %get-tuple-element.96) | copy-start | bytes 772
  452.3 5.0 %copy-start = (bf16[8,64,1024]{2,1,0:T(8,128)(2,1)S(1)}, bf16[8,64,1024]{2,1,0:T(8,128)(2,1)}, u32[]{:S(2)}) copy-start(bf16[8,64,1024]{2,1,0:T(8,128)(2,1)} %get-tuple-element.28.fc1_in) | copy-start | bytes 3145732
  452.3 5.0 %copy-start.1 = (bf16[8,64,768]{2,1,0:T(8,128)(2,1)S(1)}, bf16[8,64,768]{2,1,0:T(8,128)(2,1)}, u32[]{:S(2)}) copy-start(bf16[8,64,768]{2,1,0:T(8,128)(2,1)} %get-tuple-element.29.qkv_in) | copy-start | bytes 2359300
  452.3 7.7 %copy-start.6 = (f32[64,2048]{1,0:T(8,128)S(1)}, f32[64,2048]{1,0:T(8,128)}, u32[]{:S(2)}) copy-start(f32[64,2048]{1,0:T(8,128)} %get-tuple-element.95) | copy-start | bytes 1572868
  457.3 3.5 copy-start.4
